TPU v7x, 32 devices: a whole 2x2x4 slice. The times are simulated.
32 devices in a mesh: tm: 16 (over z, x, core), tile: 2 (over y).
Axes of the slice: x: 2, y: 2, z: 4, core: 2. Of those that a mesh axis runs over, the one named last changes fastest.
Arguments:
- latent: bfloat16 [16, 4, 160, 384], P('tm', 'tile'), may hold values from -6 to 6
- gain: float32 [384], replicated, may hold values from 0.1 to 1.9
- conv_weight: bfloat16 [3, 3, 3, 384, 384], replicated, may hold values from -0.0625 to 0.0625
- conv_bias: float32 [384], replicated, may hold values from -3 to 3
- time_weight: bfloat16 [3, 384, 768], replicated, may hold values from -0.1875 to 0.1875
- time_bias: float32 [768], replicated, may hold values from -3 to 3
- up_weight: bfloat16 [3, 3, 384, 192], replicated, may hold values from -0.109375 to 0.109375
- up_bias: float32 [192], replicated, may hold values from -3 to 3
Outputs:
- decoded: bfloat16 [32, 8, 320, 192], P('tm', 'tile')
All inputs are finite; a program needn't handle non-finite values.
Results may differ from a plain program's by a relative error of at most 0.0057.
Values may be sent and summed in bfloat16 or wider, within the bound.
No kernel may reach another device: no remote copies, remote signals or barrier semaphores. Data moves between devices by JAX's collectives and lax.ppermute only.
A program may use at most 64 MiB of HBM per device.

v0:
```python
import jax
import jax.numpy as jnp
from jax import lax
from jax.sharding import PartitionSpec as P


def shifted(block, axis, distance):
    devices = range(lax.axis_size(axis))
    route = [(i - distance, i) for i in devices if i - distance in devices]
    return lax.ppermute(block, axis, route)


def padded_2(array, sides, width):
    for axis, dim in sides:
        count, length = (lax.axis_size(axis), array.shape[dim])
        up = [(i, (i + 1) % count) for i in range(count - 1)]
        down = [(j, i) for i, j in up]
        last = lax.slice_in_dim(array, length - width, length, axis=dim)
        leading = lax.slice_in_dim(array, 0, width, axis=dim)
        before = lax.ppermute(last, axis, up)
        after = lax.ppermute(leading, axis, down)
        array = jnp.concatenate([before, array, after], axis=dim)
    return array


def activate(field, gain):
    values = field.astype(jnp.float32)
    meansq = jnp.mean(values * values, axis=-1, keepdims=True)
    scaled = values * lax.rsqrt(meansq + 1e-06) * gain
    return (scaled * jax.nn.sigmoid(scaled)).astype(jnp.bfloat16)


def history(field):
    nearer = shifted(field, "tm", 1)
    farther = shifted(field, "tm", 2)
    return jnp.concatenate([farther, nearer, field], axis=0)


def causal_conv(stacked, conv_weight):
    rows_out = stacked.shape[1] - 2
    cols = stacked.shape[2]
    chans = stacked.shape[3]
    outs_n = conv_weight.shape[4]
    padded = jnp.pad(stacked, ((0, 0), (0, 0), (1, 1), (0, 0)))
    total = jnp.zeros((rows_out * cols, outs_n), jnp.float32)
    for step_t in range(3):
        for step_h in range(3):
            slab = padded[step_t, step_h : step_h + rows_out]
            wide = jnp.concatenate(
                [slab[:, shift_w : shift_w + cols] for shift_w in range(3)], axis=-1
            )
            total = total + jnp.dot(
                wide.reshape(-1, 3 * chans),
                conv_weight[step_t, step_h].reshape(3 * chans, outs_n),
                preferred_element_type=jnp.float32,
            )
    return total.reshape(rows_out, cols, outs_n)


def time_mix(stacked, time_weight, time_bias):
    rows_n, cols, chans = (stacked.shape[1], stacked.shape[2], stacked.shape[3])
    flat = stacked.reshape(3, rows_n * cols, chans)
    halves = []
    for half in range(2):
        total = time_bias[half * chans : (half + 1) * chans] + jnp.zeros(
            (rows_n * cols, chans), jnp.float32
        )
        for step_t in range(3):
            total = total + jnp.dot(
                flat[step_t],
                time_weight[step_t, :, half * chans : (half + 1) * chans],
                preferred_element_type=jnp.float32,
            )
        halves.append(total.reshape(rows_n, cols, chans))
    return jnp.stack(halves, axis=0)


def upsample_conv(edged, up_weight, up_bias):
    rows_n = edged.shape[1] - 2
    cols2 = 2 * edged.shape[2]
    chans = edged.shape[3]
    outs_n = up_weight.shape[3]
    upsampled = jnp.repeat(jnp.repeat(edged, 2, axis=1), 2, axis=2)[:, 1 : 2 * rows_n + 3]
    padded = jnp.pad(upsampled, ((0, 0), (0, 0), (1, 1), (0, 0)))
    total = jnp.zeros((2 * 2 * rows_n * cols2, outs_n), jnp.float32)
    for step_h in range(3):
        slab = padded[:, step_h : step_h + 2 * rows_n]
        wide = jnp.concatenate(
            [slab[:, :, shift_w : shift_w + cols2] for shift_w in range(3)], axis=-1
        )
        total = total + jnp.dot(
            wide.reshape(-1, 3 * chans),
            up_weight[step_h].reshape(3 * chans, outs_n),
            preferred_element_type=jnp.float32,
        )
    return (total + up_bias).astype(jnp.bfloat16).reshape(2, 2 * rows_n, cols2, outs_n)


def local(latent, gain, conv_weight, conv_bias, time_weight, time_bias, up_weight, up_bias):
    stacked = history(activate(latent, gain))
    stacked = padded_2(stacked, (("tile", 1),), 1)
    inner = causal_conv(stacked, conv_weight)
    block = (inner + conv_bias + latent[0].astype(jnp.float32)).astype(jnp.bfloat16)
    frames = time_mix(history(block[None]), time_weight, time_bias).astype(jnp.bfloat16)
    edged = padded_2(frames, (("tile", 1),), 1)
    return upsample_conv(edged, up_weight, up_bias)


def solution(mesh):
    placed = (P("tm", "tile", None, None), P(), P(), P(), P(), P(), P(), P())
    return jax.shard_map(
        local, mesh=mesh, in_specs=placed, out_specs=P("tm", "tile", None, None), check_vma=False
    )
```

profile of v0, /device:TPU:0, one launch (start us, length us, event | category | flops | bytes accessed | tf_op | source)
XLA Modules:
  0.0 95.7 jit_solution(15373893655598522016)
XLA Ops:
  0.0 1.1 %multiply_reduce_fusion = f32[2,160]{1,0:T(2,128)S(1)} fusion(bf16[1,2,160,384]{3,2,1,0:T(8,128)(2,1)} %param.8), kind=kLoop, calls=%fused_computation.56 | loop fusion | flops 368320 | bytes 247040 | tf_op jit(solution)/shard_map/reduce_sum | solution.py:28
  1.1 1.2 %multiply_convert_fusion = bf16[1,2,160,384]{3,2,1,0:T(8,128)(2,1)S(1)} fusion(bf16[1,2,160,384]{3,2,1,0:T(8,128)(2,1)} %param.8, f32[384]{0:T(512)} %param.9, f32[2,160]{1,0:T(2,128)S(1)} %add_rsqrt_fusion), kind=kLoop, calls=%fused_computation.55 | loop fusion | flops 983040 | bytes 494336 | tf_op jit(solution)/shard_map/convert_element_type | solution.py:30
  2.3 4.9 %collective-permute-start = (bf16[1,2,160,384]{3,2,1,0:T(8,128)(2,1)S(1)}, bf16[1,2,160,384]{3,2,1,0:T(8,128)(2,1)S(1)}, u32[]{:S(2)}, u32[]{:S(2)}) collective-permute-start(bf16[1,2,160,384]{3,2,1,0:T(8,128)(2,1)S(1)} %multiply_convert_fusion), channel_id=1, source_target_pairs={{0,4},{2,6},{4,8},{6,10},{8,12},{10,14},{12,16},{14,18},{16,20},{1... | collective-permute-start | bytes 737288 | tf_op jit(solution)/shard_map/ppermute | solution.py:10
  7.2 1.5 %collective-permute-start.1 = (bf16[1,2,160,384]{3,2,1,0:T(8,128)(2,1)S(1)}, bf16[1,2,160,384]{3,2,1,0:T(8,128)(2,1)S(1)}, u32[]{:S(2)}, u32[]{:S(2)}) collective-permute-start(bf16[1,2,160,384]{3,2,1,0:T(8,128)(2,1)S(1)} %multiply_convert_fusion), channel_id=1, source_target_pairs={{0,2},{2,4},{4,6},{6,8},{8,10},{10,12},{12,14},{14,16},{16,18},{18... | collective-permute-start | bytes 737288 | tf_op jit(solution)/shard_map/ppermute | solution.py:10
  8.6 0.8 fusion.45
  9.4 4.1 %collective-permute-done = bf16[1,2,160,384]{3,2,1,0:T(8,128)(2,1)S(1)} collective-permute-done((bf16[1,2,160,384]{3,2,1,0:T(8,128)(2,1)S(1)}, bf16[1,2,160,384]{3,2,1,0:T(8,128)(2,1)S(1)}, u32[]{:S(2)}, u32[]{:S(2)}) %collective-permute-start) | collective-permute-done | bytes 245792 | tf_op jit(solution)/shard_map/ppermute | solution.py:10
  13.5 0.1 pad_maximum_fusion.4
  13.6 0.1 fusion.35
  13.7 3.4 %collective-permute-start.2 = (bf16[3,1,160,384]{3,2,1,0:T(8,128)(2,1)S(1)}, bf16[3,1,160,384]{3,2,1,0:T(8,128)(2,1)S(1)}, u32[]{:S(2)}, u32[]{:S(2)}) collective-permute-start(bf16[3,1,160,384]{3,2,1,0:T(8,128)(2,1)S(1)} %get-tuple-element.35), channel_id=1, source_target_pairs={{0,1},{2,3},{4,5},{6,7},{8,9},{10,11},{12,13},{14,15},{16,17},{18,... | collective-permute-start | bytes 1105928 | tf_op jit(solution)/shard_map/ppermute | solution.py:20
  17.1 1.3 %collective-permute-start.3 = (bf16[3,1,160,384]{3,2,1,0:T(8,128)(2,1)S(1)}, bf16[3,1,160,384]{3,2,1,0:T(8,128)(2,1)S(1)}, u32[]{:S(2)}, u32[]{:S(2)}) collective-permute-start(bf16[3,1,160,384]{3,2,1,0:T(8,128)(2,1)S(1)} %get-tuple-element.36), channel_id=1, source_target_pairs={{1,0},{3,2},{5,4},{7,6},{9,8},{11,10},{13,12},{15,14},{17,16},{19,... | collective-permute-start | bytes 1105928 | tf_op jit(solution)/shard_map/ppermute | solution.py:21
  18.4 3.9 %fusion.32 = (bf16[1,1,3,384,384]{4,3,2,1,0:T(8,128)(2,1)S(1)}, bf16[1,1,3,384,384]{4,3,2,1,0:T(8,128)(2,1)S(1)}, bf16[1,1,3,384,384]{4,3,2,1,0:T(8,128)(2,1)S(1...) fusion(bf16[3,3,3,384,384]{4,3,2,1,0:T(8,128)(2,1)} %param.10), kind=kLoop, calls=%fused_computation.85 | loop fusion | bytes 15925248 | tf_op jit(solution)/shard_map/slice | solution.py:54
  22.4 3.1 %collective-permute-done.2 = bf16[3,1,160,384]{3,2,1,0:T(8,128)(2,1)S(1)} collective-permute-done((bf16[3,1,160,384]{3,2,1,0:T(8,128)(2,1)S(1)}, bf16[3,1,160,384]{3,2,1,0:T(8,128)(2,1)S(1)}, u32[]{:S(2)}, u32[]{:S(2)}) %collective-permute-start.2) | collective-permute-done | bytes 368672 | tf_op jit(solution)/shard_map/ppermute | solution.py:20
  25.5 4.7 %collective-permute-done.3 = bf16[3,1,160,384]{3,2,1,0:T(8,128)(2,1)S(1)} collective-permute-done((bf16[3,1,160,384]{3,2,1,0:T(8,128)(2,1)S(1)}, bf16[3,1,160,384]{3,2,1,0:T(8,128)(2,1)S(1)}, u32[]{:S(2)}, u32[]{:S(2)}) %collective-permute-start.3) | collective-permute-done | bytes 368672 | tf_op jit(solution)/shard_map/ppermute | solution.py:21
  30.2 0.4 select_maximum_fusion
  30.7 0.2 slice_bitcast_fusion
  30.9 0.1 fusion.44
  31.0 0.3 fusion.36
  31.3 0.3 fusion.38
  31.6 0.3 fusion.40
  31.9 0.3 fusion.42
  32.1 0.1 pad_maximum_fusion.5
  32.2 0.6 fusion.46
  32.9 0.1 pad_maximum_fusion.11
  33.4 0.6 convolution_add_fusion.9
  34.0 0.6 convolution_add_fusion.8
  34.6 0.6 convolution_add_fusion.7
  35.2 0.6 convolution_add_fusion.6
  35.8 0.6 convolution_add_fusion.5
  36.4 0.6 convolution_add_fusion.4
  37.0 0.6 convolution_add_fusion.3
  37.6 0.6 fusion.14
  38.3 2.0 %collective-permute-start.5 = (bf16[1,2,160,384]{3,2,1,0:T(8,128)(2,1)S(1)}, bf16[1,2,160,384]{3,2,1,0:T(8,128)(2,1)S(1)}, u32[]{:S(2)}, u32[]{:S(2)}) collective-permute-start(bf16[1,2,160,384]{3,2,1,0:T(8,128)(2,1)S(1)} %add_convert_fusion), channel_id=1, source_target_pairs={{0,2},{2,4},{4,6},{6,8},{8,10},{10,12},{12,14},{14,16},{16,18},{18... | collective-permute-start | bytes 737288 | tf_op jit(solution)/shard_map/ppermute | solution.py:10
  40.3 4.0 %collective-permute-start.4 = (bf16[1,2,160,384]{3,2,1,0:T(8,128)(2,1)S(1)}, bf16[1,2,160,384]{3,2,1,0:T(8,128)(2,1)S(1)}, u32[]{:S(2)}, u32[]{:S(2)}) collective-permute-start(bf16[1,2,160,384]{3,2,1,0:T(8,128)(2,1)S(1)} %add_convert_fusion), channel_id=1, source_target_pairs={{0,4},{2,6},{4,8},{6,10},{8,12},{10,14},{12,16},{14,18},{16,20},{1... | collective-permute-start | bytes 737288 | tf_op jit(solution)/shard_map/ppermute | solution.py:10
  44.3 0.3 fusion.15
  44.6 0.3 fusion.20
  45.0 0.3 fusion.17
  45.3 0.3 fusion.22
  45.7 4.6 %collective-permute-done.4 = bf16[1,2,160,384]{3,2,1,0:T(8,128)(2,1)S(1)} collective-permute-done((bf16[1,2,160,384]{3,2,1,0:T(8,128)(2,1)S(1)}, bf16[1,2,160,384]{3,2,1,0:T(8,128)(2,1)S(1)}, u32[]{:S(2)}, u32[]{:S(2)}) %collective-permute-start.4) | collective-permute-done | bytes 245792 | tf_op jit(solution)/shard_map/ppermute | solution.py:10
  50.3 0.3 fusion.13
  50.6 0.3 fusion.12
  51.1 1.5 %collective-permute-start.6 = (bf16[2,1,160,384]{3,2,1,0:T(8,128)(2,1)S(1)}, bf16[2,1,160,384]{3,2,1,0:T(8,128)(2,1)S(1)}, u32[]{:S(2)}, u32[]{:S(2)}) collective-permute-start(bf16[2,1,160,384]{3,2,1,0:T(8,128)(2,1)S(1)} %get-tuple-element.37), channel_id=1, source_target_pairs={{0,1},{2,3},{4,5},{6,7},{8,9},{10,11},{12,13},{14,15},{16,17},{18,... | collective-permute-start | bytes 737288 | tf_op jit(solution)/shard_map/ppermute | solution.py:20
  52.5 1.5 %collective-permute-start.7 = (bf16[2,1,160,384]{3,2,1,0:T(8,128)(2,1)S(1)}, bf16[2,1,160,384]{3,2,1,0:T(8,128)(2,1)S(1)}, u32[]{:S(2)}, u32[]{:S(2)}) collective-permute-start(bf16[2,1,160,384]{3,2,1,0:T(8,128)(2,1)S(1)} %get-tuple-element.38), channel_id=1, source_target_pairs={{1,0},{3,2},{5,4},{7,6},{9,8},{11,10},{13,12},{15,14},{17,16},{19,... | collective-permute-start | bytes 737288 | tf_op jit(solution)/shard_map/ppermute | solution.py:21
  54.0 0.1 fusion.34
  54.2 0.4 copy.10
  54.6 0.4 copy.11
  55.1 0.4 copy.12
  55.5 3.0 %collective-permute-done.6 = bf16[2,1,160,384]{3,2,1,0:T(8,128)(2,1)S(1)} collective-permute-done((bf16[2,1,160,384]{3,2,1,0:T(8,128)(2,1)S(1)}, bf16[2,1,160,384]{3,2,1,0:T(8,128)(2,1)S(1)}, u32[]{:S(2)}, u32[]{:S(2)}) %collective-permute-start.6) | collective-permute-done | bytes 245792 | tf_op jit(solution)/shard_map/ppermute | solution.py:20
  58.6 4.2 %collective-permute-done.7 = bf16[2,1,160,384]{3,2,1,0:T(8,128)(2,1)S(1)} collective-permute-done((bf16[2,1,160,384]{3,2,1,0:T(8,128)(2,1)S(1)}, bf16[2,1,160,384]{3,2,1,0:T(8,128)(2,1)S(1)}, u32[]{:S(2)}, u32[]{:S(2)}) %collective-permute-start.7) | collective-permute-done | bytes 245792 | tf_op jit(solution)/shard_map/ppermute | solution.py:21
  62.7 0.2 pad_maximum_fusion.3
  62.9 0.2 broadcast_in_dim.4
  63.1 3.5 %broadcast_in_dim.5 = bf16[2,8,160,2,384]{4,3,2,1,0:T(2,128)(2,1)} broadcast(bf16[2,8,160,384]{3,2,1,0:T(8,128)(2,1)S(1)} %bitcast.116), dimensions={0,1,2,4} | broadcast | bytes 5898240 | tf_op jit(solution)/shard_map/broadcast_in_dim | solution.py:83
  66.6 9.1 %reshape.100 = bf16[2,8,320,384]{3,2,1,0:T(8,128)(2,1)} reshape(bf16[2,8,160,2,384]{4,3,2,1,0:T(2,128)(2,1)} %broadcast_in_dim.5) | data formatting | bytes 7864320 | tf_op jit(solution)/shard_map/reshape | solution.py:83
  75.6 2.1 %copy-done = bf16[2,8,320,384]{3,2,1,0:T(8,128)(2,1)S(1)} copy-done((bf16[2,8,320,384]{3,2,1,0:T(8,128)(2,1)S(1)}, bf16[2,8,320,384]{3,2,1,0:T(8,128)(2,1)}, u32[]{:S(2)}) %copy-start) | copy-done | bytes 3932184
  77.7 0.9 fusion.33
  78.6 0.9 slice-done
  79.6 4.3 %pad_slice_fusion.1 = (bf16[2,4,320,384]{3,2,1,0:T(8,128)(2,1)S(1)}, bf16[2,4,320,384]{3,2,1,0:T(8,128)(2,1)S(1)}, bf16[2,4,320,384]{3,2,1,0:T(8,128)(2,1)S(1)},...) fusion(bf16[2,6,320,384]{3,2,1,0:T(8,128)(2,1)S(1)} %slice-done), kind=kLoop, calls=%fused_computation.18 | loop fusion | bytes 14745600 | tf_op jit(solution)/shard_map/slice | solution.py:89
  83.8 1.0 %pad_maximum_fusion = bf16[2,4,320,1152]{3,2,1,0:T(8,128)(2,1)S(1)} fusion(bf16[2,4,320,384]{3,2,1,0:T(8,128)(2,1)S(1)} %get-tuple-element.18, bf16[2,4,320,384]{3,2,1,0:T(8,128)(2,1)S(1)} %get-tuple-element.16, bf16[2,4,320,384]{3,2,1,0:T(8,128)(2,1)S(1)} %get-tuple-element.22), kind=kLoop, calls=%fused_computation | loop fusion | flops 17694720 | bytes 11796480 | tf_op jit(solution)/shard_map/concatenate | solution.py:88
  84.9 2.1 %fusion.47 = f32[2560,192]{0,1:T(8,128)S(1)} fusion(bf16[2560,1152]{1,0:T(8,128)(2,1)S(1)} %bitcast.115, bf16[1152,192]{0,1:T(8,128)(2,1)S(1)} %bitcast.145), kind=kOutput, calls=%fused_computation.100 | convolution fusion | flops 1132462080 | bytes 8306688 | tf_op jit(solution)/shard_map/dot_general | solution.py:91
  87.0 1.0 %pad_maximum_fusion.2 = bf16[2,4,320,1152]{3,2,1,0:T(8,128)(2,1)S(1)} fusion(bf16[2,4,320,384]{3,2,1,0:T(8,128)(2,1)S(1)} %get-tuple-element.21, bf16[2,4,320,384]{3,2,1,0:T(8,128)(2,1)S(1)} %get-tuple-element.14, bf16[2,4,320,384]{3,2,1,0:T(8,128)(2,1)S(1)} %get-tuple-element.17), kind=kLoop, calls=%fused_computation.2 | loop fusion | flops 17694720 | bytes 11796480 | tf_op jit(solution)/shard_map/concatenate | solution.py:88
  88.0 1.0 %pad_maximum_fusion.1 = bf16[2,4,320,1152]{3,2,1,0:T(8,128)(2,1)S(1)} fusion(bf16[2,4,320,384]{3,2,1,0:T(8,128)(2,1)S(1)} %get-tuple-element.20, bf16[2,4,320,384]{3,2,1,0:T(8,128)(2,1)S(1)} %get-tuple-element.15, bf16[2,4,320,384]{3,2,1,0:T(8,128)(2,1)S(1)} %get-tuple-element.19), kind=kLoop, calls=%fused_computation.1 | loop fusion | flops 17694720 | bytes 11796480 | tf_op jit(solution)/shard_map/concatenate | solution.py:88
  89.1 2.1 %convolution_add_fusion.1 = f32[2560,192]{0,1:T(8,128)S(1)} fusion(f32[2560,192]{0,1:T(8,128)S(1)} %fusion.47, bf16[2560,1152]{1,0:T(8,128)(2,1)S(1)} %bitcast.114, bf16[1152,192]{0,1:T(8,128)(2,1)S(1)} %bitcast.144), kind=kOutput, calls=%fused_computation.7 | convolution fusion | flops 1132953600 | bytes 10272768 | tf_op jit(solution)/shard_map/dot_general | solution.py:91
  91.2 2.1 %fusion.1 = bf16[2560,192]{0,1:T(8,128)(2,1)S(1)} fusion(f32[2560,192]{0,1:T(8,128)S(1)} %convolution_add_fusion.1, bf16[2560,1152]{1,0:T(8,128)(2,1)S(1)} %bitcast.117, bf16[1152,192]{0,1:T(8,128)(2,1)S(1)} %bitcast.150, f32[192]{0:T(256)S(1)} %copy-done.5), kind=kOutput, calls=%fused_computation.8 | convolution fusion | flops 1133936640 | bytes 9290496 | tf_op jit(solution)/shard_map/dot_general | solution.py:91
  93.3 1.2 %reshape.104 = bf16[2,4,320,192]{2,1,0,3:T(4,128)(2,1)S(1)} reshape(bf16[2560,192]{0,1:T(8,128)(2,1)S(1)} %fusion.1) | data formatting | bytes 1966080 | tf_op jit(solution)/shard_map/reshape | solution.py:96
  94.6 1.2 %copy.13 = bf16[2,4,320,192]{2,3,1,0:T(8,128)(2,1)} copy(bf16[2,4,320,192]{2,1,0,3:T(4,128)(2,1)S(1)} %reshape.104) | data formatting | bytes 1966080 | tf_op jit(solution)/shard_map/reshape | solution.py:96
  (27 shorter events, 0.8 us)
Async XLA Ops:
  2.3 11.2 %collective-permute-start = (bf16[1,2,160,384]{3,2,1,0:T(8,128)(2,1)S(1)}, bf16[1,2,160,384]{3,2,1,0:T(8,128)(2,1)S(1)}, u32[]{:S(2)}, u32[]{:S(2)}) collective-permute-start(bf16[1,2,160,384]{3,2,1,0:T(8,128)(2,1)S(1)} %multiply_convert_fusion), channel_id=1, source_target_pairs={{0,4},{2,6},{4,8},{6,10},{8,12},{10,14},{12,16},{14,18},{16,20},{1... | collective-permute-start | bytes 737288 | tf_op jit(solution)/shard_map/ppermute | solution.py:10
  7.2 6.3 %collective-permute-start.1 = (bf16[1,2,160,384]{3,2,1,0:T(8,128)(2,1)S(1)}, bf16[1,2,160,384]{3,2,1,0:T(8,128)(2,1)S(1)}, u32[]{:S(2)}, u32[]{:S(2)}) collective-permute-start(bf16[1,2,160,384]{3,2,1,0:T(8,128)(2,1)S(1)} %multiply_convert_fusion), channel_id=1, source_target_pairs={{0,2},{2,4},{4,6},{6,8},{8,10},{10,12},{12,14},{14,16},{16,18},{18... | collective-permute-start | bytes 737288 | tf_op jit(solution)/shard_map/ppermute | solution.py:10
  13.7 11.8 %collective-permute-start.2 = (bf16[3,1,160,384]{3,2,1,0:T(8,128)(2,1)S(1)}, bf16[3,1,160,384]{3,2,1,0:T(8,128)(2,1)S(1)}, u32[]{:S(2)}, u32[]{:S(2)}) collective-permute-start(bf16[3,1,160,384]{3,2,1,0:T(8,128)(2,1)S(1)} %get-tuple-element.35), channel_id=1, source_target_pairs={{0,1},{2,3},{4,5},{6,7},{8,9},{10,11},{12,13},{14,15},{16,17},{18,... | collective-permute-start | bytes 1105928 | tf_op jit(solution)/shard_map/ppermute | solution.py:20
  17.1 13.1 %collective-permute-start.3 = (bf16[3,1,160,384]{3,2,1,0:T(8,128)(2,1)S(1)}, bf16[3,1,160,384]{3,2,1,0:T(8,128)(2,1)S(1)}, u32[]{:S(2)}, u32[]{:S(2)}) collective-permute-start(bf16[3,1,160,384]{3,2,1,0:T(8,128)(2,1)S(1)} %get-tuple-element.36), channel_id=1, source_target_pairs={{1,0},{3,2},{5,4},{7,6},{9,8},{11,10},{13,12},{15,14},{17,16},{19,... | collective-permute-start | bytes 1105928 | tf_op jit(solution)/shard_map/ppermute | solution.py:21
  36.4 1.2 %copy-start.1 = (bf16[1,2,160,384]{3,2,1,0:T(8,128)(2,1)S(1)}, bf16[1,2,160,384]{3,2,1,0:T(8,128)(2,1)}, u32[]{:S(2)}) copy-start(bf16[1,2,160,384]{3,2,1,0:T(8,128)(2,1)} %param.8) | copy-start | bytes 737284
  36.4 1.2 %copy-start.4 = (f32[384]{0:T(512)S(1)}, f32[384]{0:T(512)}, u32[]{:S(2)}) copy-start(f32[384]{0:T(512)} %param.11) | copy-start | bytes 4612
  37.6 6.7 %copy-start.2 = (bf16[3,384,768]{2,1,0:T(8,128)(2,1)S(1)}, bf16[3,384,768]{2,1,0:T(8,128)(2,1)}, u32[]{:S(2)}) copy-start(bf16[3,384,768]{2,1,0:T(8,128)(2,1)} %param.12) | copy-start | bytes 5308420
  38.3 6.7 %collective-permute-start.5 = (bf16[1,2,160,384]{3,2,1,0:T(8,128)(2,1)S(1)}, bf16[1,2,160,384]{3,2,1,0:T(8,128)(2,1)S(1)}, u32[]{:S(2)}, u32[]{:S(2)}) collective-permute-start(bf16[1,2,160,384]{3,2,1,0:T(8,128)(2,1)S(1)} %add_convert_fusion), channel_id=1, source_target_pairs={{0,2},{2,4},{4,6},{6,8},{8,10},{10,12},{12,14},{14,16},{16,18},{18... | collective-permute-start | bytes 737288 | tf_op jit(solution)/shard_map/ppermute | solution.py:10
  40.3 10.0 %collective-permute-start.4 = (bf16[1,2,160,384]{3,2,1,0:T(8,128)(2,1)S(1)}, bf16[1,2,160,384]{3,2,1,0:T(8,128)(2,1)S(1)}, u32[]{:S(2)}, u32[]{:S(2)}) collective-permute-start(bf16[1,2,160,384]{3,2,1,0:T(8,128)(2,1)S(1)} %add_convert_fusion), channel_id=1, source_target_pairs={{0,4},{2,6},{4,8},{6,10},{8,12},{10,14},{12,16},{14,18},{16,20},{1... | collective-permute-start | bytes 737288 | tf_op jit(solution)/shard_map/ppermute | solution.py:10
  50.3 3.7 %copy-start.3 = (bf16[3,3,384,192]{2,3,1,0:T(8,128)(2,1)S(1)}, bf16[3,3,384,192]{2,3,1,0:T(8,128)(2,1)}, u32[]{:S(2)}) copy-start(bf16[3,3,384,192]{2,3,1,0:T(8,128)(2,1)} %param.14) | copy-start | bytes 3981316
  51.1 7.5 %collective-permute-start.6 = (bf16[2,1,160,384]{3,2,1,0:T(8,128)(2,1)S(1)}, bf16[2,1,160,384]{3,2,1,0:T(8,128)(2,1)S(1)}, u32[]{:S(2)}, u32[]{:S(2)}) collective-permute-start(bf16[2,1,160,384]{3,2,1,0:T(8,128)(2,1)S(1)} %get-tuple-element.37), channel_id=1, source_target_pairs={{0,1},{2,3},{4,5},{6,7},{8,9},{10,11},{12,13},{14,15},{16,17},{18,... | collective-permute-start | bytes 737288 | tf_op jit(solution)/shard_map/ppermute | solution.py:20
  52.5 10.2 %collective-permute-start.7 = (bf16[2,1,160,384]{3,2,1,0:T(8,128)(2,1)S(1)}, bf16[2,1,160,384]{3,2,1,0:T(8,128)(2,1)S(1)}, u32[]{:S(2)}, u32[]{:S(2)}) collective-permute-start(bf16[2,1,160,384]{3,2,1,0:T(8,128)(2,1)S(1)} %get-tuple-element.38), channel_id=1, source_target_pairs={{1,0},{3,2},{5,4},{7,6},{9,8},{11,10},{13,12},{15,14},{17,16},{19,... | collective-permute-start | bytes 737288 | tf_op jit(solution)/shard_map/ppermute | solution.py:21
  75.6 2.1 %copy-start = (bf16[2,8,320,384]{3,2,1,0:T(8,128)(2,1)S(1)}, bf16[2,8,320,384]{3,2,1,0:T(8,128)(2,1)}, u32[]{:S(2)}) copy-start(bf16[2,8,320,384]{3,2,1,0:T(8,128)(2,1)} %reshape.100) | copy-start | bytes 11796484
  77.7 1.8 %slice-start = ((bf16[2,8,320,384]{3,2,1,0:T(8,128)(2,1)}), bf16[2,6,320,384]{3,2,1,0:T(8,128)(2,1)S(1)}, s32[]{:S(2)}) async-start(bf16[2,8,320,384]{3,2,1,0:T(8,128)(2,1)} %reshape.100), calls=%async_computation | async-start | bytes 5898240 | tf_op jit(solution)/shard_map/slice | solution.py:83
  89.1 2.1 %copy-start.5 = (f32[192]{0:T(256)S(1)}, f32[192]{0:T(256)}, u32[]{:S(2)}) copy-start(f32[192]{0:T(256)} %param.15) | copy-start | bytes 2308
where the time goes:
time: 96.6 us; the launch traced here: 95.7 us
  local copies, waits for them, and re-layouts  31.1 us (32%)
  waiting for transfers between devices  23.7 us (25%)
  starting transfers between devices  20 us (21%)
  matrix products  13.6 us (14%)
  other arithmetic  6.79 us (7%)
    ppermute x4, starting transfers between devices, shifted(): return lax.ppermute(block, axis, route)  12.3 us
    reshape x1, local copies, waits for them, and re-layouts, upsample_conv(): jnp.repeat(jnp.repeat(edged, 2, axis=1), 2, axis=2)[:, 1:2 * rows_n + 3]  9.07 us
    ppermute x2, waiting for transfers between devices, padded_2(): after = lax.ppermute(leading, axis, down)  8.89 us
    ppermute x4, waiting for transfers between devices, shifted(): return lax.ppermute(block, axis, route)  8.72 us
    dot_general x3, matrix products, upsample_conv(): jnp.dot(wide.reshape(-1, 3 * chans), up_weight[step_h].reshape(3 * chans,...  6.32 us
    ppermute x2, waiting for transfers between devices, padded_2(): before = lax.ppermute(last, axis, up)  6.13 us
    dot_general x9, matrix products, causal_conv(): jnp.dot(wide.reshape(-1, 3 * chans), conv_weight[step_t, step_h].reshape(...  5.3 us
    slice x2, local copies, waits for them, and re-layouts, upsample_conv(): slab[:, :, shift_w:shift_w + cols2]  5.14 us
  transfers between devices with their start and end apart: 8, of which 6 were waited for; matrix products, arithmetic and copies ran while one was open for 8% of the time, Pallas kernels for 0%

commit v1 on v0

v1 whole, which is shorter than its diff:
```python
import functools

import jax
import jax.numpy as jnp
from jax import lax
from jax.experimental import pallas as pl
from jax.experimental.pallas import tpu as pltpu
from jax.sharding import PartitionSpec as P

F32 = jnp.float32
BF16 = jnp.bfloat16
VMEM = pl.BlockSpec(memory_space=pltpu.VMEM)
SMEM = pl.BlockSpec(memory_space=pltpu.SMEM)
ANY = pl.BlockSpec(memory_space=pl.ANY)


def activate(rows, gain):
    values = rows.astype(F32)
    meansq = jnp.mean(values * values, axis=-1, keepdims=True)
    scaled = values * lax.rsqrt(meansq + 1e-06) * gain
    return (scaled * jax.nn.sigmoid(scaled)).astype(BF16)


def moved(rows, step):
    cols = rows.shape[0]
    index = lax.broadcasted_iota(jnp.int32, rows.shape, 0)
    edge = 0 if step == 1 else cols - 1
    return jnp.where(index == edge, 0.0, pltpu.roll(rows, step % cols, 0))


def conv_kernel(halos, place, own, edges, main2, edges2, packed1, gain, bias, w_hbm, block, near, wbuf, act, sems):
    flip = place[0]
    rows, cols, chans = own.shape
    lead = halos - 1

    def copies(dt):
        return [
            pltpu.make_async_copy(
                w_hbm.at[dt, jnp.where(flip == 1, 2 - dh, dh), dw],
                wbuf.at[dt, pl.ds(dh * chans, chans), pl.ds(dw * chans, chans)],
                sems.at[dt, dh, dw],
            )
            for dh in range(3)
            for dw in range(3)
        ]

    order = (2, 0, 1)
    for dt in order:
        for copy in copies(dt):
            copy.start()

    scale = gain[...]
    mains = {2: own, 0: main2, 1: packed1}
    for dt in order:
        for q in range(rows):
            act[dt, lead + q] = activate(mains[dt][jnp.where(flip == 1, rows - 1 - q, q)], scale)
        for h in range(halos):
            source = {2: edges, 0: edges2}[dt][h] if dt != 1 else packed1[rows + h]
            act[dt, 0 if h < lead else lead + rows] = activate(source, scale)

    totals = [None] * rows
    for dt in order:
        for copy in copies(dt):
            copy.wait()
        for q in range(rows):
            first = max(lead + q - 1, 0)
            last = lead + q + 1
            left = jnp.concatenate([act[dt, s] for s in range(first, last + 1)], axis=-1)
            dh0 = first - (lead + q - 1)
            part = jnp.dot(left, wbuf[dt, dh0 * chans :, :], preferred_element_type=F32)
            totals[q] = part if totals[q] is None else totals[q] + part

    for q in range(rows):
        total = totals[q]
        mixed = (
            total[:, chans : 2 * chans]
            + moved(total[:, :chans], 1)
            + moved(total[:, 2 * chans :], -1)
        )
        where = jnp.where(flip == 1, rows - 1 - q, q)
        value = (mixed + bias[...] + own[where].astype(F32)).astype(BF16)
        block[where] = value
        if halos == 1:
            if q == rows - 1:
                near[0] = value
        else:
            if q == 0:
                near[0] = value
            if q == rows - 1:
                near[1] = value


def up_kernel(halos, place, own, edges, main2, edges2, packed1, tbias, ubias, tw_hbm, uw_hbm, out_hbm,
              tw, uw, doubled, wide, outs, sems, osems):
    flip = place[0]
    rows, cols, chans = own.shape
    lead = halos - 1
    count = rows + halos
    outs_n = ubias.shape[-1]
    lanes = 128
    rest = outs_n - lanes
    load_t = pltpu.make_async_copy(tw_hbm, tw, sems.at[0])
    load_u = pltpu.make_async_copy(uw_hbm, uw, sems.at[1])
    load_t.start()
    load_u.start()

    def row_of(dt, s):
        if lead <= s < lead + rows:
            q = s - lead
            main = {2: own, 0: main2, 1: packed1}[dt]
            return main[jnp.where(flip == 1, rows - 1 - q, q)]
        h = 0 if s < lead else halos - 1
        return packed1[rows + h] if dt == 1 else {2: edges, 0: edges2}[dt][h]

    left = jnp.concatenate(
        [jnp.concatenate([row_of(dt, s) for dt in range(3)], axis=-1) for s in range(count)], axis=0
    )
    load_t.wait()
    mixed = jnp.dot(left, tw[...], preferred_element_type=F32) + tbias[...]
    for s in range(count):
        value = mixed[s * cols : (s + 1) * cols]
        if halos == 2 and s == 0:
            value = jnp.where(place[1] == 1, value, 0.0)
        if halos == 2 and s == count - 1:
            value = jnp.where(place[2] == 1, value, 0.0)
        for f in range(2):
            doubled[f, s] = value[:, f * chans : (f + 1) * chans].astype(BF16)

    load_u.wait()
    lane = lax.broadcasted_iota(jnp.int32, (cols, lanes), 1)
    stores = []
    for q in range(rows):
        for phase in range(2):
            s = lead + q
            taken = [r for r in (s - 1 + phase, s + phase) if r >= 0]
            left = jnp.concatenate(
                [jnp.concatenate([doubled[f, r] for r in taken], axis=-1) for f in range(2)], axis=0
            )
            right = uw[phase, (2 - len(taken)) * chans :, :]
            both = jnp.dot(left, right, preferred_element_type=F32)
            for f in range(2):
                part = both[f * cols : (f + 1) * cols]
                g = [part[:, k * lanes : (k + 1) * lanes] for k in range(6)]
                even = g[0] + moved(g[2], 1) + ubias[:, :lanes]
                odd = g[1] + moved(g[3], -1) + ubias[:, :lanes]
                tail = g[4] + jnp.where(lane < rest, moved(g[5], 1), moved(g[5], -1))
                wide[0, pl.ds(0, cols, stride=2), :] = even
                wide[0, pl.ds(1, cols, stride=2), :] = odd
                wide[1, pl.ds(0, cols, stride=2), :] = tail
                wide[1, pl.ds(1, cols, stride=2), :] = pltpu.roll(tail, lanes - rest, 1)
                o = 2 * q + phase
                outs[f, o, :, :lanes] = wide[0].astype(BF16)
                outs[f, o, :, lanes:] = (wide[1, :, :rest] + ubias[:, lanes:]).astype(BF16)
                copy = pltpu.make_async_copy(
                    outs.at[f, o],
                    out_hbm.at[f, jnp.where(flip == 1, 2 * rows - 1 - o, o)],
                    osems.at[f, o],
                )
                copy.start()
                stores.append(copy)
    for copy in stores:
        copy.wait()


def merged_taps(up_weight, flip):
    taps = up_weight.astype(F32)
    taps = jnp.where(flip == 1, taps[::-1], taps)
    near = jnp.stack([jnp.stack([taps[0], taps[1] + taps[2]]), jnp.stack([taps[0] + taps[1], taps[2]])])
    e0, e12 = near[:, :, 0], near[:, :, 1] + near[:, :, 2]
    o01, o2 = near[:, :, 0] + near[:, :, 1], near[:, :, 2]
    lanes = 128
    wide = jnp.concatenate(
        [a[..., :lanes] for a in (e12, o01, e0, o2)] + [a[..., lanes:] for a in (e12, o01, e0, o2)], axis=-1
    )
    return wide.astype(BF16).reshape(2, -1, wide.shape[-1])


def exchange(main, near, halos, core):
    frames = lax.axis_size("tm")
    tiles = lax.axis_size("tile")
    later = [(i, i + 2) for i in range(frames - 2)]
    main2 = lax.ppermute(main, "tm", later)
    if halos == 1:
        sides = [(near[0], [(0, 1), (1, 0)])]
    else:
        sides = [
            (near[1], [(j, j + 1) for j in range(tiles - 1)]),
            (near[0], [(j + 1, j) for j in range(tiles - 1)]),
        ]
    edges = jnp.stack([lax.ppermute(row, "tile", route) for row, route in sides])
    edges2 = jnp.stack(
        [
            lax.ppermute(
                row,
                ("tm", "tile"),
                [(a * tiles + i, b * tiles + j) for a, b in later for i, j in route],
            )
            for row, route in sides
        ]
    )
    packed = jnp.where(core == 0, jnp.concatenate([main, edges]), jnp.concatenate([main2, edges2]))
    packed1 = lax.ppermute(packed, "tm", [(i, i ^ 1) for i in range(frames)])
    return main, edges, main2, edges2, packed1


def local(latent, gain, conv_weight, conv_bias, time_weight, time_bias, up_weight, up_bias):
    tiles = lax.axis_size("tile")
    tile = lax.axis_index("tile")
    core = lax.axis_index("tm") % 2
    halos = 1 if tiles == 2 else 2
    main = latent[0]
    rows, cols, chans = main.shape
    outs_n = up_weight.shape[3]
    flip = tile if halos == 1 else 0 * tile
    place = jnp.stack([flip, tile > 0, tile < tiles - 1]).astype(jnp.int32)
    up_w = merged_taps(up_weight, flip)

    if halos == 1:
        near = [lax.dynamic_index_in_dim(main, (rows - 1) * (1 - tile), 0, keepdims=False)]
    else:
        near = [main[0], main[rows - 1]]

    args = exchange(main, near, halos, core)
    block, near = pl.pallas_call(
        functools.partial(conv_kernel, halos),
        out_shape=(
            jax.ShapeDtypeStruct((rows, cols, chans), BF16),
            jax.ShapeDtypeStruct((halos, cols, chans), BF16),
        ),
        in_specs=[SMEM] + [VMEM] * 7 + [ANY],
        out_specs=(VMEM, VMEM),
        scratch_shapes=[
            pltpu.VMEM((3, 3 * chans, 3 * chans), BF16),
            pltpu.VMEM((3, rows + halos, cols, chans), BF16),
            pltpu.SemaphoreType.DMA((3, 3, 3)),
        ],
        compiler_params=pltpu.CompilerParams(vmem_limit_bytes=48 << 20),
        cost_estimate=pl.CostEstimate(flops=2500000000, bytes_accessed=9000000, transcendentals=600000),
    )(place, *args, gain[None], conv_bias[None], conv_weight)

    args = exchange(block, [near[h] for h in range(halos)], halos, core)
    return pl.pallas_call(
        functools.partial(up_kernel, halos),
        out_shape=jax.ShapeDtypeStruct((2, 2 * rows, 2 * cols, outs_n), BF16),
        in_specs=[SMEM] + [VMEM] * 7 + [ANY] * 2,
        out_specs=ANY,
        scratch_shapes=[
            pltpu.VMEM((3 * chans, 2 * chans), BF16),
            pltpu.VMEM((2, 2 * chans, 4 * outs_n), BF16),
            pltpu.VMEM((2, rows + halos, cols, chans), BF16),
            pltpu.VMEM((2, 2 * cols, 128), F32),
            pltpu.VMEM((2, 2 * rows, 2 * cols, outs_n), BF16),
            pltpu.SemaphoreType.DMA((2,)),
            pltpu.SemaphoreType.DMA((2, 2 * rows)),
        ],
        compiler_params=pltpu.CompilerParams(vmem_limit_bytes=48 << 20),
        cost_estimate=pl.CostEstimate(flops=2500000000, bytes_accessed=6000000, transcendentals=0),
    )(place, *args, time_bias[None], up_bias[None], time_weight.reshape(3 * chans, 2 * chans), up_w)


def solution(mesh):
    placed = (P("tm", "tile", None, None), P(), P(), P(), P(), P(), P(), P())
    return jax.shard_map(
        local, mesh=mesh, in_specs=placed, out_specs=P("tm", "tile", None, None), check_vma=False
    )
```

time: 96.6 us -> 67.1 us (0.69)
  waiting for transfers between devices: 23.7 us -> 8.02 us
  Pallas kernels: 0 us -> 14.2 us
  matrix products: 13.6 us -> 0 us
  local copies, waits for them, and re-layouts: 31.1 us -> 19 us
  other arithmetic: 6.79 us -> 3.32 us
  starting transfers between devices: 20 us -> 21.1 us
    ppermute x8, waiting for transfers between devices: 23.7 us -> 8.02 us  [the longest x2 4.94 us: exchange(): main2 = lax.ppermute(main, 'tm', later)]
    pallas_call x0 -> x2, Pallas kernels: none -> 14.2 us  [the longest x1 7.66 us: local(): pl.pallas_call(functools.partial(up_kernel, halos), out_shape=jax.ShapeDt...]
    dot_general x18 -> x0, matrix products: 13.6 us -> none  [the longest x3 6.32 us: upsample_conv(): jnp.dot(wide.reshape(-1, 3 * chans), up_weight[step_h].reshape(3 * chans,...]
    reshape x3 -> x0, local copies, waits for them, and re-layouts: 11.5 us -> none  [the longest x1 9.07 us: upsample_conv(): jnp.repeat(jnp.repeat(edged, 2, axis=1), 2, axis=2)[:, 1:2 * rows_n + 3]]
    concatenate x0 -> x1, local copies, waits for them, and re-layouts: none -> 5.02 us  [merged_taps(): jnp.concatenate([a[..., :lanes] for a in (e12, o01, e0, o2)] + [a[..., la...]
    concatenate x15 -> x0, other arithmetic: 4.39 us -> none  [the longest x3 3.11 us: upsample_conv(): jnp.concatenate([slab[:, :, shift_w:shift_w + cols2] for shift_w in range...]
    slice x16, local copies, waits for them, and re-layouts: 13.4 us -> 9.5 us  [the longest x8 7.02 us: merged_taps(): a[..., lanes:]]
    broadcast_in_dim x2 -> x3, local copies, waits for them, and re-layouts: 3.68 us -> 0.01 us  [the longest x1 0.01 us: local(): time_bias[None]]
  transfers between devices with their start and end apart: 8 -> 8, of which waited for: 6 -> 3; matrix products, arithmetic and copies ran while one was open for 8% -> 26% of each run, Pallas kernels for 0% -> 0%
where the time goes in v1:
time: 67.1 us; the launch traced here: 65.9 us
  starting transfers between devices  21.1 us (31%)
  local copies, waits for them, and re-layouts  19 us (28%)
  Pallas kernels  14.2 us (21%)
  waiting for transfers between devices  8.02 us (12%)
  other arithmetic  3.32 us (5%)
    ppermute x2, starting transfers between devices, exchange(): main2 = lax.ppermute(main, 'tm', later)  9.28 us
    ppermute x2, starting transfers between devices, exchange(): lax.ppermute(row, ('tm', 'tile'), [(a * tiles + i, b * tiles + j) for a,...  8.58 us
    pallas_call x1, Pallas kernels, local(): pl.pallas_call(functools.partial(up_kernel, halos), out_shape=jax.ShapeDt...  7.66 us
    slice x8, local copies, waits for them, and re-layouts, merged_taps(): a[..., lanes:]  7.02 us
    pallas_call x1, Pallas kernels, local(): pl.pallas_call(functools.partial(conv_kernel, halos), out_shape=(jax.Shap...  6.51 us
    concatenate x1, local copies, waits for them, and re-layouts, merged_taps(): jnp.concatenate([a[..., :lanes] for a in (e12, o01, e0, o2)] + [a[..., la...  5.02 us
    ppermute x2, waiting for transfers between devices, exchange(): main2 = lax.ppermute(main, 'tm', later)  4.94 us
    ppermute x2, starting transfers between devices, exchange(): lax.ppermute(row, 'tile', route)  3.17 us
  transfers between devices with their start and end apart: 8, of which 3 were waited for; matrix products, arithmetic and copies ran while one was open for 26% of the time, Pallas kernels for 0%

profile of v1, /device:TPU:0, one launch (start us, length us, event | category | flops | bytes accessed | tf_op | source)
XLA Modules:
  0.0 65.9 jit_solution(36550605874107214)
XLA Ops:
  0.0 0.0 copy-start.4
  0.0 5.0 %collective-permute-start.1 = (bf16[2,160,384]{2,1,0:T(8,128)(2,1)}, bf16[2,160,384]{2,1,0:T(8,128)(2,1)S(1)}, u32[]{:S(2)}, u32[]{:S(2)}) collective-permute-start(bf16[2,160,384]{2,1,0:T(8,128)(2,1)} %bitcast.33), channel_id=1, source_target_pairs={{0,4},{2,6},{4,8},{6,10},{8,12},{10,14},{12,16},{14,18},{16,20},{1... | collective-permute-start | bytes 737288 | tf_op jit(solution)/shard_map/ppermute | solution.py:182
  5.0 0.9 %dynamic-slice_bitcast_fusion = bf16[160,384]{1,0:T(8,128)(2,1)S(1)} fusion(bf16[1,2,160,384]{3,2,1,0:T(8,128)(2,1)} %param.8, s32[]{:T(128)S(6)} %select_n.31), kind=kLoop, calls=%fused_computation.20 | loop fusion | bytes 245764 | tf_op jit(solution)/shard_map/jit(dynamic_index_in_dim)/squeeze | solution.py:219
  5.9 1.6 %collective-permute-start = (bf16[160,384]{1,0:T(8,128)(2,1)S(1)}, bf16[160,384]{1,0:T(8,128)(2,1)S(1)}, u32[]{:S(2)}, u32[]{:S(2)}) collective-permute-start(bf16[160,384]{1,0:T(8,128)(2,1)S(1)} %dynamic-slice_bitcast_fusion), channel_id=1, source_target_pairs={{0,1},{1,0},{2,3},{3,2},{4,5},{5,4},{6,7},{7,6},{8,9},{9,8},{10,11... | collective-permute-start | bytes 368648 | tf_op jit(solution)/shard_map/ppermute | solution.py:190
  7.5 3.4 %collective-permute-start.2 = (bf16[160,384]{1,0:T(8,128)(2,1)S(1)}, bf16[160,384]{1,0:T(8,128)(2,1)S(1)}, u32[]{:S(2)}, u32[]{:S(2)}) collective-permute-start(bf16[160,384]{1,0:T(8,128)(2,1)S(1)} %dynamic-slice_bitcast_fusion), channel_id=1, source_target_pairs={{0,5},{1,4},{2,7},{3,6},{4,9},{5,8},{6,11},{7,10},{8,13},{9,12},{1... | collective-permute-start | bytes 368648 | tf_op jit(solution)/shard_map/ppermute | solution.py:193
  10.9 0.0 collective-permute-done
  10.9 2.4 %collective-permute-done.2 = bf16[160,384]{1,0:T(8,128)(2,1)S(1)} collective-permute-done((bf16[160,384]{1,0:T(8,128)(2,1)S(1)}, bf16[160,384]{1,0:T(8,128)(2,1)S(1)}, u32[]{:S(2)}, u32[]{:S(2)}) %collective-permute-start.2) | collective-permute-done | bytes 122912 | tf_op jit(solution)/shard_map/ppermute | solution.py:193
  13.3 0.0 collective-permute-done.1.main2
  13.3 1.0 %maximum_select_fusion = bf16[3,160,384]{2,1,0:T(8,128)(2,1)S(1)} fusion(bf16[1,160,384]{2,1,0:T(8,128)(2,1)S(1)} %bitcast.40, bf16[2,160,384]{2,1,0:T(8,128)(2,1)} %bitcast.34, bf16[1,160,384]{2,1,0:T(8,128)(2,1)S(1)} %bitcast.42, bf16[2,160,384]{2,1,0:T(8,128)(2,1)S(1)} %collective-permute-done.1.main2, pred[]{:T(512)S(6)} %eq.9), kind=kLoop, calls=%fused_computation.18 | loop fusion | flops 552960 | bytes 1105921 | tf_op jit(solution)/shard_map/jit(_where)/select_n | solution.py:201
  14.3 0.1 collective-permute-start.3
  14.4 0.1 pad_add_fusion.place
  14.5 0.0 copy-done.4
  14.5 0.0 copy-start.7
  14.5 0.0 copy-start.8
  14.5 0.2 convert_element_type.3
  14.7 0.5 copy-done.7
  15.2 0.0 copy-done.8
  15.2 0.0 copy-start
  15.2 0.2 reverse_select_fusion
  15.4 0.7 %collective-permute-done.3.packed1 = bf16[3,160,384]{2,1,0:T(8,128)(2,1)S(1)} collective-permute-done((bf16[3,160,384]{2,1,0:T(8,128)(2,1)S(1)}, bf16[3,160,384]{2,1,0:T(8,128)(2,1)S(1)}, u32[]{:S(2)}, u32[]{:S(2)}) %collective-permute-start.3) | collective-permute-done | bytes 368672 | tf_op jit(solution)/shard_map/ppermute | solution.py:202
  16.1 0.1 copy-done
  16.1 6.5 %shard_map.82 = (bf16[2,160,384]{2,1,0:T(8,128)(2,1)S(1)}, bf16[1,160,384]{2,1,0:T(8,128)(2,1)S(1)}) custom-call(s32[3]{0:T(128)S(1)} %pad_add_fusion.place, bf16[2,160,384]{2,1,0:T(8,128)(2,1)S(1)} %bitcast.35, bf16[1,160,384]{2,1,0:T(8,128)(2,1)S(1)} %bitcast.41, bf16[2,160,384]{2,1,0:T(8,128)(2,1)S(1)} %collective-permute-done.1.main2, ...), custom_call_target="tpu_custom_call" | custom-call | flops 2500000000 | bytes 9000000 | tf_op jit(solution)/shard_map/pallas_call | solution.py:224
  22.7 1.6 %collective-permute-start.4 = (bf16[160,384]{1,0:T(8,128)(2,1)S(1)}, bf16[160,384]{1,0:T(8,128)(2,1)S(1)}, u32[]{:S(2)}, u32[]{:S(2)}) collective-permute-start(bf16[160,384]{1,0:T(8,128)(2,1)S(1)} %bitcast.45), channel_id=1, source_target_pairs={{0,1},{1,0},{2,3},{3,2},{4,5},{5,4},{6,7},{7,6},{8,9},{9,8},{10,11... | collective-permute-start | bytes 368648 | tf_op jit(solution)/shard_map/ppermute | solution.py:190
  24.2 5.2 %collective-permute-start.6 = (bf16[160,384]{1,0:T(8,128)(2,1)S(1)}, bf16[160,384]{1,0:T(8,128)(2,1)S(1)}, u32[]{:S(2)}, u32[]{:S(2)}) collective-permute-start(bf16[160,384]{1,0:T(8,128)(2,1)S(1)} %bitcast.46), channel_id=1, source_target_pairs={{0,5},{1,4},{2,7},{3,6},{4,9},{5,8},{6,11},{7,10},{8,13},{9,12},{1... | collective-permute-start | bytes 368648 | tf_op jit(solution)/shard_map/ppermute | solution.py:193
  29.5 4.3 %collective-permute-start.5 = (bf16[2,160,384]{2,1,0:T(8,128)(2,1)S(1)}, bf16[2,160,384]{2,1,0:T(8,128)(2,1)S(1)}, u32[]{:S(2)}, u32[]{:S(2)}) collective-permute-start(bf16[2,160,384]{2,1,0:T(8,128)(2,1)S(1)} %get-tuple-element.7.own), channel_id=1, source_target_pairs={{0,4},{2,6},{4,8},{6,10},{8,12},{10,14},{12,16},{14,18},{16,20},{1... | collective-permute-start | bytes 737288 | tf_op jit(solution)/shard_map/ppermute | solution.py:182
  33.8 0.3 fusion.4
  34.1 0.0 collective-permute-done.4
  34.1 0.0 collective-permute-done.6
  34.1 4.9 %collective-permute-done.5.main2 = bf16[2,160,384]{2,1,0:T(8,128)(2,1)S(1)} collective-permute-done((bf16[2,160,384]{2,1,0:T(8,128)(2,1)S(1)}, bf16[2,160,384]{2,1,0:T(8,128)(2,1)S(1)}, u32[]{:S(2)}, u32[]{:S(2)}) %collective-permute-start.5) | collective-permute-done | bytes 245792 | tf_op jit(solution)/shard_map/ppermute | solution.py:182
  39.1 0.8 %maximum_select_fusion.1 = bf16[3,160,384]{2,1,0:T(8,128)(2,1)} fusion(bf16[1,160,384]{2,1,0:T(8,128)(2,1)S(1)} %bitcast.36, bf16[2,160,384]{2,1,0:T(8,128)(2,1)S(1)} %get-tuple-element.7.own, bf16[1,160,384]{2,1,0:T(8,128)(2,1)S(1)} %bitcast.38, bf16[2,160,384]{2,1,0:T(8,128)(2,1)S(1)} %collective-permute-done.5.main2, pred[]{:T(512)S(6)} %eq.9), kind=kLoop, calls=%fused_computation.19 | loop fusion | flops 552960 | bytes 1105921 | tf_op jit(solution)/shard_map/jit(_where)/select_n | solution.py:201
  39.9 0.0 collective-permute-start.7
  39.9 0.2 maximum_bitcast_fusion
  40.1 0.2 convert_bitcast_fusion
  40.5 0.7 %slice.84 = bf16[2,2,384,64]{2,3,1,0:T(8,128)(2,1)} slice(bf16[2,2,384,192]{2,3,1,0:T(8,128)(2,1)S(1)} %get-tuple-element.9), slice={[0:2], [0:2], [0:384], [128:192]} | slice | bytes 393216 | tf_op jit(solution)/shard_map/slice | solution.py:173
  41.2 0.3 fusion.3
  41.5 0.7 %slice.81 = bf16[2,2,384,64]{2,3,1,0:T(8,128)(2,1)} slice(bf16[2,2,384,192]{2,3,1,0:T(8,128)(2,1)S(1)} %get-tuple-element.12), slice={[0:2], [0:2], [0:384], [128:192]} | slice | bytes 393216 | tf_op jit(solution)/shard_map/slice | solution.py:173
  42.2 0.7 %slice.82 = bf16[2,2,384,64]{2,3,1,0:T(8,128)(2,1)} slice(bf16[2,2,384,192]{2,3,1,0:T(8,128)(2,1)S(1)} %get-tuple-element.11), slice={[0:2], [0:2], [0:384], [128:192]} | slice | bytes 393216 | tf_op jit(solution)/shard_map/slice | solution.py:173
  42.9 0.2 copy.11
  43.1 0.2 copy.12
  43.4 0.2 copy.15
  43.6 0.0 copy-start.5
  43.6 0.0 copy-start.6
  43.6 1.9 %copy.16 = bf16[2,2,384,64]{3,2,1,0:T(8,128)(2,1)} copy(bf16[2,2,384,64]{2,3,1,0:T(8,128)(2,1)} %slice.84) | data formatting | bytes 393216 | tf_op jit(solution)/shard_map/slice | solution.py:173
  45.5 0.9 %copy.9 = bf16[2,2,384,128]{3,2,1,0:T(8,128)(2,1)} copy(bf16[2,2,384,128]{2,3,1,0:T(8,128)(2,1)S(1)} %slice.77) | data formatting | bytes 786432 | tf_op jit(solution)/shard_map/slice | solution.py:173
  46.5 0.0 copy-start.3
  46.5 0.9 %copy.10 = bf16[2,2,384,128]{3,2,1,0:T(8,128)(2,1)} copy(bf16[2,2,384,128]{2,3,1,0:T(8,128)(2,1)S(1)} %slice.78) | data formatting | bytes 786432 | tf_op jit(solution)/shard_map/slice | solution.py:173
  47.4 1.9 %copy.13 = bf16[2,2,384,64]{3,2,1,0:T(8,128)(2,1)} copy(bf16[2,2,384,64]{2,3,1,0:T(8,128)(2,1)} %slice.81) | data formatting | bytes 393216 | tf_op jit(solution)/shard_map/slice | solution.py:173
  49.2 0.0 copy-done.5
  49.2 0.9 %copy.14 = bf16[2,2,384,64]{3,2,1,0:T(8,128)(2,1)} copy(bf16[2,2,384,64]{2,3,1,0:T(8,128)(2,1)S(1)} %copy-done.5) | data formatting | bytes 393216 | tf_op jit(solution)/shard_map/slice | solution.py:173
  50.2 0.0 copy-done.6
  50.2 0.0 copy-done.3
  50.2 0.0 copy-start.2
  50.2 5.0 %concatenate.45.uw_hbm = bf16[2,768,768]{2,1,0:T(8,128)(2,1)} concatenate(bf16[2,768,128]{2,1,0:T(8,128)(2,1)} %bitcast.52, bf16[2,768,128]{2,1,0:T(8,128)(2,1)} %bitcast.53, bf16[2,768,128]{2,1,0:T(8,128)(2,1)S(1)} %bitcast.48, bf16[2,768,128]{2,1,0:T(8,128)(2,1)S(1)} %bitcast.49, bf16[2,768,64]{2,1,0:T(8,128)(2,1)} %bitcast.54, bf16[2,768,64]{2,1,0:T(8,128)(2,1)} %bitcast.55, ...), dimensions={2} | concatenate | bytes 4718592 | tf_op jit(solution)/shard_map/concatenate | solution.py:172
  55.2 0.0 collective-permute-done.7.packed1
  55.2 0.0 copy-done.2
  55.2 0.0 copy-start.1
  55.3 1.5 %copy-done.1 = bf16[3,384,768]{2,1,0:T(8,128)(2,1)S(1)} copy-done((bf16[3,384,768]{2,1,0:T(8,128)(2,1)S(1)}, bf16[3,384,768]{2,1,0:T(8,128)(2,1)}, u32[]{:S(2)}) %copy-start.1) | copy-done | bytes 1769496
  56.7 7.7 %shard_map.83 = bf16[2,4,320,192]{3,2,1,0:T(8,128)(2,1)S(1)} custom-call(s32[3]{0:T(128)S(1)} %pad_add_fusion.place, bf16[2,160,384]{2,1,0:T(8,128)(2,1)S(1)} %get-tuple-element.7.own, bf16[1,160,384]{2,1,0:T(8,128)(2,1)S(1)} %bitcast.37, bf16[2,160,384]{2,1,0:T(8,128)(2,1)S(1)} %collective-permute-done.5.main2, bf16[1,160,384]{2,1,0:T(8,128)(2,1)S(1)} %bitcast.39, ...), custom_call_target="tpu_custom_call" | custom-call | flops 2500000000 | bytes 6000000 | tf_op jit(solution)/shard_map/pallas_call | solution.py:242
  64.4 1.5 %copy.17 = bf16[2,4,320,192]{2,3,1,0:T(8,128)(2,1)} copy(bf16[2,4,320,192]{3,2,1,0:T(8,128)(2,1)S(1)} %shard_map.83) | data formatting | bytes 1966080 | tf_op jit(solution)/shard_map/pallas_call | solution.py:242
  (8 shorter events, 0.2 us)
Async XLA Ops:
  0.0 14.5 %copy-start.4 = (bf16[3,3,384,192]{2,3,1,0:T(8,128)(2,1)S(1)}, bf16[3,3,384,192]{2,3,1,0:T(8,128)(2,1)}, u32[]{:S(2)}) copy-start(bf16[3,3,384,192]{2,3,1,0:T(8,128)(2,1)} %param.14) | copy-start | bytes 3981316
  0.0 13.3 %collective-permute-start.1 = (bf16[2,160,384]{2,1,0:T(8,128)(2,1)}, bf16[2,160,384]{2,1,0:T(8,128)(2,1)S(1)}, u32[]{:S(2)}, u32[]{:S(2)}) collective-permute-start(bf16[2,160,384]{2,1,0:T(8,128)(2,1)} %bitcast.33), channel_id=1, source_target_pairs={{0,4},{2,6},{4,8},{6,10},{8,12},{10,14},{12,16},{14,18},{16,20},{1... | collective-permute-start | bytes 737288 | tf_op jit(solution)/shard_map/ppermute | solution.py:182
  5.9 5.0 %collective-permute-start = (bf16[160,384]{1,0:T(8,128)(2,1)S(1)}, bf16[160,384]{1,0:T(8,128)(2,1)S(1)}, u32[]{:S(2)}, u32[]{:S(2)}) collective-permute-start(bf16[160,384]{1,0:T(8,128)(2,1)S(1)} %dynamic-slice_bitcast_fusion), channel_id=1, source_target_pairs={{0,1},{1,0},{2,3},{3,2},{4,5},{5,4},{6,7},{7,6},{8,9},{9,8},{10,11... | collective-permute-start | bytes 368648 | tf_op jit(solution)/shard_map/ppermute | solution.py:190
  7.5 5.8 %collective-permute-start.2 = (bf16[160,384]{1,0:T(8,128)(2,1)S(1)}, bf16[160,384]{1,0:T(8,128)(2,1)S(1)}, u32[]{:S(2)}, u32[]{:S(2)}) collective-permute-start(bf16[160,384]{1,0:T(8,128)(2,1)S(1)} %dynamic-slice_bitcast_fusion), channel_id=1, source_target_pairs={{0,5},{1,4},{2,7},{3,6},{4,9},{5,8},{6,11},{7,10},{8,13},{9,12},{1... | collective-permute-start | bytes 368648 | tf_op jit(solution)/shard_map/ppermute | solution.py:193
  14.3 1.8 %collective-permute-start.3 = (bf16[3,160,384]{2,1,0:T(8,128)(2,1)S(1)}, bf16[3,160,384]{2,1,0:T(8,128)(2,1)S(1)}, u32[]{:S(2)}, u32[]{:S(2)}) collective-permute-start(bf16[3,160,384]{2,1,0:T(8,128)(2,1)S(1)} %maximum_select_fusion), channel_id=1, source_target_pairs={{0,2},{2,0},{4,6},{6,4},{8,10},{10,8},{12,14},{14,12},{16,18},{18,... | collective-permute-start | bytes 1105928 | tf_op jit(solution)/shard_map/ppermute | solution.py:202
  14.5 0.7 %copy-start.7 = (f32[384]{0:T(512)S(1)}, f32[384]{0:T(512)}, u32[]{:S(2)}) copy-start(f32[384]{0:T(512)} %param.9) | copy-start | bytes 4612
  14.5 0.7 %copy-start.8 = (f32[384]{0:T(512)S(1)}, f32[384]{0:T(512)}, u32[]{:S(2)}) copy-start(f32[384]{0:T(512)} %param.11) | copy-start | bytes 4612
  15.2 0.9 %copy-start = (bf16[1,2,160,384]{3,2,1,0:T(8,128)(2,1)S(1)}, bf16[1,2,160,384]{3,2,1,0:T(8,128)(2,1)}, u32[]{:S(2)}) copy-start(bf16[1,2,160,384]{3,2,1,0:T(8,128)(2,1)} %param.8) | copy-start | bytes 737284
  22.7 11.5 %collective-permute-start.4 = (bf16[160,384]{1,0:T(8,128)(2,1)S(1)}, bf16[160,384]{1,0:T(8,128)(2,1)S(1)}, u32[]{:S(2)}, u32[]{:S(2)}) collective-permute-start(bf16[160,384]{1,0:T(8,128)(2,1)S(1)} %bitcast.45), channel_id=1, source_target_pairs={{0,1},{1,0},{2,3},{3,2},{4,5},{5,4},{6,7},{7,6},{8,9},{9,8},{10,11... | collective-permute-start | bytes 368648 | tf_op jit(solution)/shard_map/ppermute | solution.py:190
  24.2 9.9 %collective-permute-start.6 = (bf16[160,384]{1,0:T(8,128)(2,1)S(1)}, bf16[160,384]{1,0:T(8,128)(2,1)S(1)}, u32[]{:S(2)}, u32[]{:S(2)}) collective-permute-start(bf16[160,384]{1,0:T(8,128)(2,1)S(1)} %bitcast.46), channel_id=1, source_target_pairs={{0,5},{1,4},{2,7},{3,6},{4,9},{5,8},{6,11},{7,10},{8,13},{9,12},{1... | collective-permute-start | bytes 368648 | tf_op jit(solution)/shard_map/ppermute | solution.py:193
  29.5 9.6 %collective-permute-start.5 = (bf16[2,160,384]{2,1,0:T(8,128)(2,1)S(1)}, bf16[2,160,384]{2,1,0:T(8,128)(2,1)S(1)}, u32[]{:S(2)}, u32[]{:S(2)}) collective-permute-start(bf16[2,160,384]{2,1,0:T(8,128)(2,1)S(1)} %get-tuple-element.7.own), channel_id=1, source_target_pairs={{0,4},{2,6},{4,8},{6,10},{8,12},{10,14},{12,16},{14,18},{16,20},{1... | collective-permute-start | bytes 737288 | tf_op jit(solution)/shard_map/ppermute | solution.py:182
  39.9 15.4 %collective-permute-start.7 = (bf16[3,160,384]{2,1,0:T(8,128)(2,1)}, bf16[3,160,384]{2,1,0:T(8,128)(2,1)S(1)}, u32[]{:S(2)}, u32[]{:S(2)}) collective-permute-start(bf16[3,160,384]{2,1,0:T(8,128)(2,1)} %maximum_select_fusion.1), channel_id=1, source_target_pairs={{0,2},{2,0},{4,6},{6,4},{8,10},{10,8},{12,14},{14,12},{16,18},{18,... | collective-permute-start | bytes 1105928 | tf_op jit(solution)/shard_map/ppermute | solution.py:202
  43.6 5.6 %copy-start.5 = (bf16[2,2,384,64]{2,3,1,0:T(8,128)(2,1)S(1)}, bf16[2,2,384,64]{2,3,1,0:T(8,128)(2,1)}, u32[]{:S(2)}) copy-start(bf16[2,2,384,64]{2,3,1,0:T(8,128)(2,1)} %slice.82) | copy-start | bytes 589828
  43.6 6.6 %copy-start.6 = (f32[768]{0:T(1024)S(1)}, f32[768]{0:T(1024)}, u32[]{:S(2)}) copy-start(f32[768]{0:T(1024)} %param.13) | copy-start | bytes 9220
  46.5 3.7 %copy-start.3 = (bf16[2,2,384,64]{3,2,1,0:T(8,128)(2,1)S(1)}, bf16[2,2,384,64]{3,2,1,0:T(8,128)(2,1)}, u32[]{:S(2)}) copy-start(bf16[2,2,384,64]{3,2,1,0:T(8,128)(2,1)} %copy.16) | copy-start | bytes 589828
  50.2 5.0 %copy-start.2 = (f32[192]{0:T(256)S(1)}, f32[192]{0:T(256)}, u32[]{:S(2)}) copy-start(f32[192]{0:T(256)} %param.15) | copy-start | bytes 2308
  55.2 1.5 %copy-start.1 = (bf16[3,384,768]{2,1,0:T(8,128)(2,1)S(1)}, bf16[3,384,768]{2,1,0:T(8,128)(2,1)}, u32[]{:S(2)}) copy-start(bf16[3,384,768]{2,1,0:T(8,128)(2,1)} %param.12) | copy-start | bytes 5308420

commit v2 on v1

v2 whole, which is shorter than its diff:
```python
import functools

import jax
import jax.numpy as jnp
from jax import lax
from jax.experimental import pallas as pl
from jax.experimental.pallas import tpu as pltpu
from jax.sharding import PartitionSpec as P

F32 = jnp.float32
BF16 = jnp.bfloat16
VMEM = pl.BlockSpec(memory_space=pltpu.VMEM)
SMEM = pl.BlockSpec(memory_space=pltpu.SMEM)
ANY = pl.BlockSpec(memory_space=pl.ANY)


def activate(rows, gain):
    values = rows.astype(F32)
    meansq = jnp.mean(values * values, axis=-1, keepdims=True)
    scaled = values * lax.rsqrt(meansq + 1e-06) * gain
    return (scaled * jax.nn.sigmoid(scaled)).astype(BF16)


def moved(rows, step):
    cols = rows.shape[0]
    index = lax.broadcasted_iota(jnp.int32, rows.shape, 0)
    edge = 0 if step == 1 else cols - 1
    return jnp.where(index == edge, 0.0, pltpu.roll(rows, step % cols, 0))


def conv_part(halos, flip, dt, main, edges, gain, weight, act):
    rows, cols, chans = main.shape
    lead = halos - 1
    for q in range(rows):
        act[lead + q] = activate(main[jnp.where(flip == 1, rows - 1 - q, q)], gain)
    for h in range(halos):
        act[0 if h < lead else lead + rows] = activate(edges[h], gain)
    parts = []
    for q in range(rows):
        first = max(lead + q - 1, 0)
        taken = range(first, lead + q + 2)
        left = jnp.concatenate([act[s] for s in taken], axis=-1)
        taps = [s - (lead + q - 1) for s in taken]
        right = jnp.concatenate(
            [
                jnp.concatenate([weight[dt, jnp.where(flip == 1, 2 - dh, dh), dw] for dw in range(3)], axis=-1)
                for dh in taps
            ],
            axis=0,
        )
        total = jnp.dot(left, right, preferred_element_type=F32)
        parts.append(
            total[:, chans : 2 * chans]
            + moved(total[:, :chans], 1)
            + moved(total[:, 2 * chans :], -1)
        )
    return parts


def conv_first(halos, place, own, edges, gain, bias, weight, acc, act):
    flip = place[0]
    rows = own.shape[0]
    for q, part in enumerate(conv_part(halos, flip, 2, own, edges, gain[...], weight, act)):
        acc[q] = part + bias[...] + own[jnp.where(flip == 1, rows - 1 - q, q)].astype(F32)


def conv_second(halos, place, main, edges, before, gain, weight, acc, act):
    for q, part in enumerate(conv_part(halos, place[0], 0, main, edges, gain[...], weight, act)):
        acc[q] = before[q] + part


def conv_third(halos, place, main_a, edges_a, main_b, edges_b, before, gain, weight, block, near, act, main, edges):
    flip = place[0]
    rows = block.shape[0]
    pick(place, main_a, edges_a, main_b, edges_b, main, edges)
    for q, part in enumerate(conv_part(halos, flip, 1, main, edges, gain[...], weight, act)):
        value = (before[q] + part).astype(BF16)
        block[jnp.where(flip == 1, rows - 1 - q, q)] = value
        if q == rows - 1:
            near[halos - 1] = value
        if q == 0 and halos == 2:
            near[0] = value


def pick(place, main_a, edges_a, main_b, edges_b, main, edges):
    @pl.when(place[3] == 0)
    def _():
        main[...] = main_a[...]
        edges[...] = edges_a[...]

    @pl.when(place[3] != 0)
    def _():
        main[...] = main_b[...]
        edges[...] = edges_b[...]


def up_kernel(halos, place, own, edges, main2, edges2, main_a, edges_a, main_b, edges_b, tbias, ubias, tw, uw,
              out_hbm, main1, edges1, doubled, wide, outs, osems):
    flip = place[0]
    rows, cols, chans = own.shape
    lead = halos - 1
    count = rows + halos
    lanes = 128
    rest = ubias.shape[-1] - lanes
    pick(place, main_a, edges_a, main_b, edges_b, main1, edges1)
    mains = (main2, main1, own)
    sides = (edges2, edges1, edges)

    def row_of(dt, s):
        if lead <= s < lead + rows:
            q = s - lead
            return mains[dt][jnp.where(flip == 1, rows - 1 - q, q)]
        return sides[dt][0 if s < lead else halos - 1]

    left = jnp.concatenate(
        [jnp.concatenate([row_of(dt, s) for dt in range(3)], axis=-1) for s in range(count)], axis=0
    )
    mixed = jnp.dot(left, tw[...], preferred_element_type=F32) + tbias[...]
    for s in range(count):
        value = mixed[s * cols : (s + 1) * cols]
        if halos == 2 and s == 0:
            value = jnp.where(place[1] == 1, value, 0.0)
        if halos == 2 and s == count - 1:
            value = jnp.where(place[2] == 1, value, 0.0)
        for f in range(2):
            doubled[f, s] = value[:, f * chans : (f + 1) * chans].astype(BF16)

    lane = lax.broadcasted_iota(jnp.int32, (cols, lanes), 1)
    stores = []
    for q in range(rows):
        for phase in range(2):
            s = lead + q
            taken = [r for r in (s - 1 + phase, s + phase) if r >= 0]
            left = jnp.concatenate(
                [jnp.concatenate([doubled[f, r] for r in taken], axis=-1) for f in range(2)], axis=0
            )
            right = uw[phase, (2 - len(taken)) * chans :, :]
            both = jnp.dot(left, right, preferred_element_type=F32)
            for f in range(2):
                part = both[f * cols : (f + 1) * cols]
                g = [part[:, k * lanes : (k + 1) * lanes] for k in range(6)]
                tail = g[4] + jnp.where(lane < rest, moved(g[5], 1), moved(g[5], -1))
                o = 2 * q + phase
                slot = (2 * o + f) % 2
                wide[slot, 0, pl.ds(0, cols, stride=2), :] = g[0] + moved(g[2], 1) + ubias[:, :lanes]
                wide[slot, 0, pl.ds(1, cols, stride=2), :] = g[1] + moved(g[3], -1) + ubias[:, :lanes]
                wide[slot, 1, pl.ds(0, cols, stride=2), :] = tail
                wide[slot, 1, pl.ds(1, cols, stride=2), :] = pltpu.roll(tail, lanes - rest, 1)
                outs[f, o, :lanes, :] = wide[slot, 0].T.astype(BF16)
                outs[f, o, lanes:, :] = (wide[slot, 1, :, :rest] + ubias[:, lanes:]).T.astype(BF16)
                copy = pltpu.make_async_copy(
                    outs.at[f, o],
                    out_hbm.at[f, jnp.where(flip == 1, 2 * rows - 1 - o, o)],
                    osems.at[f, o],
                )
                copy.start()
                stores.append(copy)
    for copy in stores:
        copy.wait()


def merge_kernel(place, taps, merged):
    flip = place[0]
    lanes = 128
    chans = taps.shape[3]

    def tap(dh, dw):
        return taps[jnp.where(flip == 1, 2 - dh, dh), dw].astype(F32)

    for phase, sets in enumerate((((0,), (1, 2)), ((0, 1), (2,)))):
        for which, rows in enumerate(sets):
            cols = [sum(tap(dh, dw) for dh in rows) for dw in range(3)]
            groups = (cols[1] + cols[2], cols[0] + cols[1], cols[0], cols[2])
            wide = jnp.concatenate([g[:lanes] for g in groups] + [g[lanes:] for g in groups], axis=0)
            merged[phase, which * chans : (which + 1) * chans, :] = wide.T.astype(BF16)


def exchange(main, near, halos):
    frames = lax.axis_size("tm")
    tiles = lax.axis_size("tile")
    later = [(i, i + 2) for i in range(frames - 2)]
    swap = [(i, i ^ 1) for i in range(frames)]
    main2 = lax.ppermute(main, "tm", later)
    if halos == 1:
        sides = [(near[0], [(0, 1), (1, 0)])]
    else:
        sides = [
            (near[1], [(j, j + 1) for j in range(tiles - 1)]),
            (near[0], [(j + 1, j) for j in range(tiles - 1)]),
        ]
    edges = [lax.ppermute(row, "tile", route) for row, route in sides]
    edges2 = [
        lax.ppermute(
            row,
            ("tm", "tile"),
            [(a * tiles + i, b * tiles + j) for a, b in later for i, j in route],
        )
        for row, route in sides
    ]
    stacked = lambda parts: parts[0] if len(parts) == 1 else jnp.concatenate(parts)
    edges, edges2 = stacked(edges), stacked(edges2)
    even = lax.ppermute(main2, "tm", swap), lax.ppermute(edges2, "tm", swap)
    odd = lax.ppermute(main, "tm", swap), lax.ppermute(edges, "tm", swap)
    return (main, edges), (main2, edges2), even + odd


def in_vmem(array):
    return pltpu.with_memory_space_constraint(array, pltpu.VMEM)


def local(latent, gain, conv_weight, conv_bias, time_weight, time_bias, up_weight, up_bias):
    tiles = lax.axis_size("tile")
    tile = lax.axis_index("tile")
    core = lax.axis_index("tm") % 2
    halos = 1 if tiles == 2 else 2
    main = latent[0]
    rows, cols, chans = main.shape
    outs_n = up_weight.shape[3]
    flip = tile if halos == 1 else 0 * tile
    place = jnp.stack([flip, tile > 0, tile < tiles - 1, core]).astype(jnp.int32)
    params = pltpu.CompilerParams(vmem_limit_bytes=20 << 20)
    field = jax.ShapeDtypeStruct((rows, cols, chans), BF16)
    sides = jax.ShapeDtypeStruct((halos, cols, chans), BF16)
    act = pltpu.VMEM((rows + halos, cols, chans), BF16)
    flops = 18 * rows * cols * chans * chans

    def cost(share):
        return pl.CostEstimate(flops=int(flops * share), bytes_accessed=1000000, transcendentals=0)

    def vmem(shape, dtype):
        return pltpu.VMEM(shape, dtype)

    merged = pl.pallas_call(
        merge_kernel,
        out_shape=vmem((2, 2 * chans, 4 * outs_n), BF16),
        in_specs=[SMEM, VMEM],
        out_specs=VMEM,
        compiler_params=params,
        cost_estimate=cost(1),
        name="merge_taps",
    )(place, up_weight.transpose(0, 1, 3, 2))

    if halos == 1:
        near = [lax.dynamic_slice_in_dim(main, (rows - 1) * (1 - tile), 1, 0)]
    else:
        near = [main[:1], main[rows - 1 :]]

    gain, conv_bias, time_bias, up_bias = gain[None], conv_bias[None], time_bias[None], up_bias[None]
    conv_weight = in_vmem(conv_weight)
    time_weight = in_vmem(time_weight.reshape(3 * chans, 2 * chans))
    frame, frame2, frame1 = exchange(main, near, halos)
    total = vmem((rows, cols, chans), F32)
    acc = pl.pallas_call(
        functools.partial(conv_first, halos),
        out_shape=total,
        in_specs=[SMEM] + [VMEM] * 5,
        out_specs=VMEM,
        scratch_shapes=[act],
        compiler_params=params,
        cost_estimate=cost(1),
        name="conv_own_frame",
    )(place, *frame, gain, conv_bias, conv_weight)
    acc = pl.pallas_call(
        functools.partial(conv_second, halos),
        out_shape=total,
        in_specs=[SMEM] + [VMEM] * 5,
        out_specs=VMEM,
        scratch_shapes=[act],
        compiler_params=params,
        cost_estimate=cost(1),
        name="conv_two_back",
    )(place, *frame2, acc, gain, conv_weight)
    block, near = pl.pallas_call(
        functools.partial(conv_third, halos),
        out_shape=(field, sides),
        in_specs=[SMEM] + [VMEM] * 7,
        out_specs=(VMEM, VMEM),
        scratch_shapes=[act, pltpu.VMEM(field.shape, BF16), pltpu.VMEM(sides.shape, BF16)],
        compiler_params=params,
        cost_estimate=cost(1),
        name="conv_one_back",
    )(place, *frame1, acc, gain, conv_weight)

    frame, frame2, frame1 = exchange(block, [near[h : h + 1] for h in range(halos)], halos)
    out = pl.pallas_call(
        functools.partial(up_kernel, halos),
        out_shape=jax.ShapeDtypeStruct((2, 2 * rows, outs_n, 2 * cols), BF16),
        in_specs=[SMEM] + [VMEM] * 12,
        out_specs=ANY,
        scratch_shapes=[
            pltpu.VMEM(field.shape, BF16),
            pltpu.VMEM(sides.shape, BF16),
            pltpu.VMEM((2, rows + halos, cols, chans), BF16),
            pltpu.VMEM((2, 2, 2 * cols, 128), F32),
            pltpu.VMEM((2, 2 * rows, outs_n, 2 * cols), BF16),
            pltpu.SemaphoreType.DMA((2, 2 * rows)),
        ],
        compiler_params=params,
        cost_estimate=cost(2),
        name="time_and_up",
    )(place, *frame, *frame2, *frame1, time_bias, up_bias, time_weight, merged)
    return out.transpose(0, 1, 3, 2)


def solution(mesh):
    placed = (P("tm", "tile", None, None), P(), P(), P(), P(), P(), P(), P())
    return jax.shard_map(
        local, mesh=mesh, in_specs=placed, out_specs=P("tm", "tile", None, None), check_vma=False
    )
```

time: 67.1 us -> 47.6 us (0.71)
  the two profiles are of different devices: /device:TPU:0 before, /device:TPU:13 now
where the time goes in v2:
time: 47.6 us; the launch traced here: 47.2 us
  starting transfers between devices  23 us (48%)
  Pallas kernels  11.5 us (24%)
  local copies, waits for them, and re-layouts  8.05 us (17%)
  waiting for transfers between devices  4.45 us (9%)
    ppermute x2, starting transfers between devices, exchange(): lax.ppermute(row, ('tm', 'tile'), [(a * tiles + i, b * tiles + j) for a,...  9.09 us
    unnamed x14, local copies, waits for them, and re-layouts  5.76 us
    ppermute x2, starting transfers between devices, exchange(): main2 = lax.ppermute(main, 'tm', later)  5.39 us
    pallas_call x1, Pallas kernels, local(): pl.pallas_call(functools.partial(up_kernel, halos), out_shape=jax.ShapeDt...  4.89 us
    ppermute x4, starting transfers between devices, exchange(): even = (lax.ppermute(main2, 'tm', swap), lax.ppermute(edges2, 'tm', swap))  4.22 us
    ppermute x4, starting transfers between devices, exchange(): odd = (lax.ppermute(main, 'tm', swap), lax.ppermute(edges, 'tm', swap))  3.72 us
    ppermute x2, waiting for transfers between devices, exchange(): lax.ppermute(row, ('tm', 'tile'), [(a * tiles + i, b * tiles + j) for a,...  2.44 us
    ppermute x2, waiting for transfers between devices, exchange(): main2 = lax.ppermute(main, 'tm', later)  1.99 us
  transfers between devices with their start and end apart: 14, of which 2 were waited for; matrix products, arithmetic and copies ran while one was open for 5% of the time, Pallas kernels for 10%

profile of v2, /device:TPU:13, one launch (start us, length us, event | category | flops | bytes accessed | tf_op | source)
XLA Modules:
  0.0 47.2 jit_solution(6961712110698513501)
XLA Ops:
  0.0 3.1 %collective-permute-start = (bf16[2,160,384]{2,1,0:T(8,128)(2,1)}, bf16[2,160,384]{2,1,0:T(8,128)(2,1)S(1)}, u32[]{:S(2)}, u32[]{:S(2)}) collective-permute-start(bf16[2,160,384]{2,1,0:T(8,128)(2,1)} %bitcast.13), channel_id=1, source_target_pairs={{0,4},{2,6},{4,8},{6,10},{8,12},{10,14},{12,16},{14,18},{16,20},{1... | collective-permute-start | bytes 737288 | tf_op jit(solution)/shard_map/ppermute | solution.py:183
  3.1 0.9 %dynamic-slice_bitcast_fusion = bf16[1,160,384]{2,1,0:T(8,128)(2,1)S(1)} fusion(bf16[1,2,160,384]{3,2,1,0:T(8,128)(2,1)} %param.8, s32[]{:T(128)S(6)} %select_n.11), kind=kLoop, calls=%fused_computation | loop fusion | bytes 245764 | tf_op jit(solution)/shard_map/dynamic_slice | solution.py:244
  4.0 0.3 collective-permute-start.5
  4.3 4.1 %collective-permute-start.2 = (bf16[1,160,384]{2,1,0:T(8,128)(2,1)S(1)}, bf16[1,160,384]{2,1,0:T(8,128)(2,1)S(1)}, u32[]{:S(2)}, u32[]{:S(2)}) collective-permute-start(bf16[1,160,384]{2,1,0:T(8,128)(2,1)S(1)} %dynamic-slice_bitcast_fusion), channel_id=1, source_target_pairs={{0,5},{1,4},{2,7},{3,6},{4,9},{5,8},{6,11},{7,10},{8,13},{9,12},{1... | collective-permute-start | bytes 368648 | tf_op jit(solution)/shard_map/ppermute | solution.py:193
  8.5 1.6 %collective-permute-start.4 = (bf16[2,160,384]{2,1,0:T(8,128)(2,1)}, bf16[2,160,384]{2,1,0:T(8,128)(2,1)S(1)}, u32[]{:S(2)}, u32[]{:S(2)}) collective-permute-start(bf16[2,160,384]{2,1,0:T(8,128)(2,1)} %bitcast.14), channel_id=1, source_target_pairs={{0,2},{2,0},{4,6},{6,4},{8,10},{10,8},{12,14},{14,12},{16,18},{18,... | collective-permute-start | bytes 737288 | tf_op jit(solution)/shard_map/ppermute | solution.py:203
  10.0 0.7 %broadcast_in_dim.12.gain = f32[1,384]{1,0:T(1,128)S(1)} reshape(f32[384]{0:T(512)} %param.9) | data formatting | bytes 3072 | tf_op jit(solution)/shard_map/broadcast_in_dim | solution.py:248
  10.7 0.7 %broadcast_in_dim.13.bias = f32[1,384]{1,0:T(1,128)S(1)} reshape(f32[384]{0:T(512)} %param.11) | data formatting | bytes 3072 | tf_op jit(solution)/shard_map/broadcast_in_dim | solution.py:248
  11.4 0.0 collective-permute-done.main
  11.4 0.1 collective-permute-start.1
  11.5 0.1 pad_add_fusion.place
  11.6 0.0 collective-permute-done.5.edges
  11.6 0.5 collective-permute-start.6
  12.0 0.0 collective-permute-done.2.edges
  12.0 2.1 %collective-permute-start.3 = (bf16[1,160,384]{2,1,0:T(8,128)(2,1)S(1)}, bf16[1,160,384]{2,1,0:T(8,128)(2,1)S(1)}, u32[]{:S(2)}, u32[]{:S(2)}) collective-permute-start(bf16[1,160,384]{2,1,0:T(8,128)(2,1)S(1)} %collective-permute-done.2.edges), channel_id=1, source_target_pairs={{0,2},{2,0},{4,6},{6,4},{8,10},{10,8},{12,14},{14,12},{16,18},{18,... | collective-permute-start | bytes 368648 | tf_op jit(solution)/shard_map/ppermute | solution.py:202
  14.1 0.0 copy-start
  14.1 3.3 %copy-done = bf16[3,3,3,384,384]{4,3,2,1,0:T(8,128)(2,1)S(1)} copy-done((bf16[3,3,3,384,384]{4,3,2,1,0:T(8,128)(2,1)S(1)}, bf16[3,3,3,384,384]{4,3,2,1,0:T(8,128)(2,1)}, u32[]{:S(2)}) %copy-start) | copy-done | bytes 7962648
  17.4 0.0 copy-start.4
  17.4 0.9 %copy-done.4 = bf16[1,2,160,384]{3,2,1,0:T(8,128)(2,1)S(1)} copy-done((bf16[1,2,160,384]{3,2,1,0:T(8,128)(2,1)S(1)}, bf16[1,2,160,384]{3,2,1,0:T(8,128)(2,1)}, u32[]{:S(2)}) %copy-start.4) | copy-done | bytes 245784
  18.3 0.0 copy-start.1
  18.3 1.8 %conv_own_frame.1.before = f32[2,160,384]{2,1,0:T(8,128)S(1)} custom-call(s32[4]{0:T(128)S(1)} %pad_add_fusion.place, bf16[2,160,384]{2,1,0:T(8,128)(2,1)S(1)} %bitcast.15, bf16[1,160,384]{2,1,0:T(8,128)(2,1)S(1)} %collective-permute-done.5.edges, f32[1,384]{1,0:T(1,128)S(1)} %broadcast_in_dim.12.gain, f32[1,384]{1,0:T(1,128)S(1)} %broadcast_in_dim.13.bias, ...), custom_call_target="tpu_custom_call" | custom-call | flops 849346560 | bytes 1000000 | tf_op jit(solution)/shard_map/conv_own_frame/pallas_call | solution.py:253
  20.1 1.5 %copy-done.1 = bf16[3,3,3,384,384]{4,3,2,1,0:T(8,128)(2,1)S(1)} copy-done((bf16[3,3,3,384,384]{4,3,2,1,0:T(8,128)(2,1)S(1)}, bf16[3,3,3,384,384]{4,3,2,1,0:T(8,128)(2,1)}, u32[]{:S(2)}) %copy-start.1) | copy-done | bytes 7962648
  21.6 1.7 %conv_two_back.1.before = f32[2,160,384]{2,1,0:T(8,128)S(1)} custom-call(s32[4]{0:T(128)S(1)} %pad_add_fusion.place, bf16[2,160,384]{2,1,0:T(8,128)(2,1)S(1)} %collective-permute-done.main, bf16[1,160,384]{2,1,0:T(8,128)(2,1)S(1)} %collective-permute-done.2.edges, f32[2,160,384]{2,1,0:T(8,128)S(1)} %conv_own_frame.1.before, ...), custom_call_target="tpu_custom_call" | custom-call | flops 849346560 | bytes 1000000 | tf_op jit(solution)/shard_map/conv_two_back/pallas_call | solution.py:263
  23.3 0.0 copy-start.6
  23.3 0.0 copy-start.3
  23.3 0.0 collective-permute-done.6.edges_b
  23.3 0.0 collective-permute-done.3.edges_a
  23.3 0.0 collective-permute-done.4.main_b
  23.4 0.0 collective-permute-done.1.main_a
  23.4 1.7 %conv_one_back.1 = (bf16[2,160,384]{2,1,0:T(8,128)(2,1)S(1)}, bf16[1,160,384]{2,1,0:T(8,128)(2,1)S(1)}) custom-call(s32[4]{0:T(128)S(1)} %pad_add_fusion.place, bf16[2,160,384]{2,1,0:T(8,128)(2,1)S(1)} %collective-permute-done.1.main_a, bf16[1,160,384]{2,1,0:T(8,128)(2,1)S(1)} %collective-permute-done.3.edges_a, ...), custom_call_target="tpu_custom_call" | custom-call | flops 849346560 | bytes 1000000 | tf_op jit(solution)/shard_map/conv_one_back/pallas_call | solution.py:273
  25.1 2.3 %collective-permute-start.8 = (bf16[2,160,384]{2,1,0:T(8,128)(2,1)S(1)}, bf16[2,160,384]{2,1,0:T(8,128)(2,1)S(1)}, u32[]{:S(2)}, u32[]{:S(2)}) collective-permute-start(bf16[2,160,384]{2,1,0:T(8,128)(2,1)S(1)} %get-tuple-element.7.own), channel_id=1, source_target_pairs={{0,4},{2,6},{4,8},{6,10},{8,12},{10,14},{12,16},{14,18},{16,20},{1... | collective-permute-start | bytes 737288 | tf_op jit(solution)/shard_map/ppermute | solution.py:183
  27.4 5.0 %collective-permute-start.9 = (bf16[1,160,384]{2,1,0:T(8,128)(2,1)S(1)}, bf16[1,160,384]{2,1,0:T(8,128)(2,1)S(1)}, u32[]{:S(2)}, u32[]{:S(2)}) collective-permute-start(bf16[1,160,384]{2,1,0:T(8,128)(2,1)S(1)} %get-tuple-element.8), channel_id=1, source_target_pairs={{0,5},{1,4},{2,7},{3,6},{4,9},{5,8},{6,11},{7,10},{8,13},{9,12},{1... | collective-permute-start | bytes 368648 | tf_op jit(solution)/shard_map/ppermute | solution.py:193
  32.4 0.3 collective-permute-start.7
  32.7 0.8 %collective-permute-start.12 = (bf16[2,160,384]{2,1,0:T(8,128)(2,1)S(1)}, bf16[2,160,384]{2,1,0:T(8,128)(2,1)S(1)}, u32[]{:S(2)}, u32[]{:S(2)}) collective-permute-start(bf16[2,160,384]{2,1,0:T(8,128)(2,1)S(1)} %get-tuple-element.7.own), channel_id=1, source_target_pairs={{0,2},{2,0},{4,6},{6,4},{8,10},{10,8},{12,14},{14,12},{16,18},{18,... | collective-permute-start | bytes 737288 | tf_op jit(solution)/shard_map/ppermute | solution.py:203
  33.5 2.0 %collective-permute-done.8.main2 = bf16[2,160,384]{2,1,0:T(8,128)(2,1)S(1)} collective-permute-done((bf16[2,160,384]{2,1,0:T(8,128)(2,1)S(1)}, bf16[2,160,384]{2,1,0:T(8,128)(2,1)S(1)}, u32[]{:S(2)}, u32[]{:S(2)}) %collective-permute-start.8) | collective-permute-done | bytes 245792 | tf_op jit(solution)/shard_map/ppermute | solution.py:183
  35.5 1.2 %collective-permute-start.10 = (bf16[2,160,384]{2,1,0:T(8,128)(2,1)S(1)}, bf16[2,160,384]{2,1,0:T(8,128)(2,1)S(1)}, u32[]{:S(2)}, u32[]{:S(2)}) collective-permute-start(bf16[2,160,384]{2,1,0:T(8,128)(2,1)S(1)} %collective-permute-done.8.main2), channel_id=1, source_target_pairs={{0,2},{2,0},{4,6},{6,4},{8,10},{10,8},{12,14},{14,12},{16,18},{18,... | collective-permute-start | bytes 737288 | tf_op jit(solution)/shard_map/ppermute | solution.py:202
  36.7 2.4 %collective-permute-done.9.edges2 = bf16[1,160,384]{2,1,0:T(8,128)(2,1)S(1)} collective-permute-done((bf16[1,160,384]{2,1,0:T(8,128)(2,1)S(1)}, bf16[1,160,384]{2,1,0:T(8,128)(2,1)S(1)}, u32[]{:S(2)}, u32[]{:S(2)}) %collective-permute-start.9) | collective-permute-done | bytes 122912 | tf_op jit(solution)/shard_map/ppermute | solution.py:193
  39.1 0.9 %collective-permute-start.11 = (bf16[1,160,384]{2,1,0:T(8,128)(2,1)S(1)}, bf16[1,160,384]{2,1,0:T(8,128)(2,1)S(1)}, u32[]{:S(2)}, u32[]{:S(2)}) collective-permute-start(bf16[1,160,384]{2,1,0:T(8,128)(2,1)S(1)} %collective-permute-done.9.edges2), channel_id=1, source_target_pairs={{0,2},{2,0},{4,6},{6,4},{8,10},{10,8},{12,14},{14,12},{16,18},{18,... | collective-permute-start | bytes 368648 | tf_op jit(solution)/shard_map/ppermute | solution.py:202
  40.0 0.0 collective-permute-done.7.edges
  40.0 0.8 %collective-permute-start.13 = (bf16[1,160,384]{2,1,0:T(8,128)(2,1)S(1)}, bf16[1,160,384]{2,1,0:T(8,128)(2,1)S(1)}, u32[]{:S(2)}, u32[]{:S(2)}) collective-permute-start(bf16[1,160,384]{2,1,0:T(8,128)(2,1)S(1)} %collective-permute-done.7.edges), channel_id=1, source_target_pairs={{0,2},{2,0},{4,6},{6,4},{8,10},{10,8},{12,14},{14,12},{16,18},{18,... | collective-permute-start | bytes 368648 | tf_op jit(solution)/shard_map/ppermute | solution.py:203
  40.8 0.0 copy-done.6
  40.8 0.0 copy-done.3
  40.8 0.0 copy-start.2
  40.8 0.0 copy-start.5
  40.9 1.4 %merge_taps.1.uw = bf16[2,768,768]{2,1,0:T(8,128)(2,1)S(1)} custom-call(s32[4]{0:T(128)S(1)} %pad_add_fusion.place, bf16[3,3,192,384]{3,2,1,0:T(8,128)(2,1)S(1)} %bitcast.12), custom_call_target="tpu_custom_call" | custom-call | flops 849346560 | bytes 1000000 | tf_op jit(solution)/shard_map/merge_taps/pallas_call | solution.py:233
  42.2 0.0 collective-permute-done.11.edges_a
  42.2 0.0 collective-permute-done.13.edges_b
  42.2 0.0 collective-permute-done.12.main_b
  42.3 0.0 collective-permute-done.10.main_a
  42.3 0.0 copy-done.2
  42.3 0.0 copy-done.5
  42.3 4.9 %time_and_up.1 = bf16[2,4,192,320]{3,2,1,0:T(8,128)(2,1)} custom-call(s32[4]{0:T(128)S(1)} %pad_add_fusion.place, bf16[2,160,384]{2,1,0:T(8,128)(2,1)S(1)} %get-tuple-element.7.own, bf16[1,160,384]{2,1,0:T(8,128)(2,1)S(1)} %collective-permute-done.7.edges, bf16[2,160,384]{2,1,0:T(8,128)(2,1)S(1)} %collective-permute-done.8.main2, ...), custom_call_target="tpu_custom_call" | custom-call | flops 1698693120 | bytes 1000000 | tf_op jit(solution)/shard_map/time_and_up/pallas_call | solution.py:285
  (1 shorter events, 0.0 us)
Async XLA Ops:
  0.0 11.4 %collective-permute-start = (bf16[2,160,384]{2,1,0:T(8,128)(2,1)}, bf16[2,160,384]{2,1,0:T(8,128)(2,1)S(1)}, u32[]{:S(2)}, u32[]{:S(2)}) collective-permute-start(bf16[2,160,384]{2,1,0:T(8,128)(2,1)} %bitcast.13), channel_id=1, source_target_pairs={{0,4},{2,6},{4,8},{6,10},{8,12},{10,14},{12,16},{14,18},{16,20},{1... | collective-permute-start | bytes 737288 | tf_op jit(solution)/shard_map/ppermute | solution.py:183
  4.0 7.5 %collective-permute-start.5 = (bf16[1,160,384]{2,1,0:T(8,128)(2,1)S(1)}, bf16[1,160,384]{2,1,0:T(8,128)(2,1)S(1)}, u32[]{:S(2)}, u32[]{:S(2)}) collective-permute-start(bf16[1,160,384]{2,1,0:T(8,128)(2,1)S(1)} %dynamic-slice_bitcast_fusion), channel_id=1, source_target_pairs={{0,1},{1,0},{2,3},{3,2},{4,5},{5,4},{6,7},{7,6},{8,9},{9,8},{10,11... | collective-permute-start | bytes 368648 | tf_op jit(solution)/shard_map/ppermute | solution.py:191
  4.3 7.7 %collective-permute-start.2 = (bf16[1,160,384]{2,1,0:T(8,128)(2,1)S(1)}, bf16[1,160,384]{2,1,0:T(8,128)(2,1)S(1)}, u32[]{:S(2)}, u32[]{:S(2)}) collective-permute-start(bf16[1,160,384]{2,1,0:T(8,128)(2,1)S(1)} %dynamic-slice_bitcast_fusion), channel_id=1, source_target_pairs={{0,5},{1,4},{2,7},{3,6},{4,9},{5,8},{6,11},{7,10},{8,13},{9,12},{1... | collective-permute-start | bytes 368648 | tf_op jit(solution)/shard_map/ppermute | solution.py:193
  8.5 14.9 %collective-permute-start.4 = (bf16[2,160,384]{2,1,0:T(8,128)(2,1)}, bf16[2,160,384]{2,1,0:T(8,128)(2,1)S(1)}, u32[]{:S(2)}, u32[]{:S(2)}) collective-permute-start(bf16[2,160,384]{2,1,0:T(8,128)(2,1)} %bitcast.14), channel_id=1, source_target_pairs={{0,2},{2,0},{4,6},{6,4},{8,10},{10,8},{12,14},{14,12},{16,18},{18,... | collective-permute-start | bytes 737288 | tf_op jit(solution)/shard_map/ppermute | solution.py:203
  11.4 11.9 %collective-permute-start.1 = (bf16[2,160,384]{2,1,0:T(8,128)(2,1)S(1)}, bf16[2,160,384]{2,1,0:T(8,128)(2,1)S(1)}, u32[]{:S(2)}, u32[]{:S(2)}) collective-permute-start(bf16[2,160,384]{2,1,0:T(8,128)(2,1)S(1)} %collective-permute-done.main), channel_id=1, source_target_pairs={{0,2},{2,0},{4,6},{6,4},{8,10},{10,8},{12,14},{14,12},{16,18},{18,... | collective-permute-start | bytes 737288 | tf_op jit(solution)/shard_map/ppermute | solution.py:202
  11.6 11.8 %collective-permute-start.6 = (bf16[1,160,384]{2,1,0:T(8,128)(2,1)S(1)}, bf16[1,160,384]{2,1,0:T(8,128)(2,1)S(1)}, u32[]{:S(2)}, u32[]{:S(2)}) collective-permute-start(bf16[1,160,384]{2,1,0:T(8,128)(2,1)S(1)} %collective-permute-done.5.edges), channel_id=1, source_target_pairs={{0,2},{2,0},{4,6},{6,4},{8,10},{10,8},{12,14},{14,12},{16,18},{18,... | collective-permute-start | bytes 368648 | tf_op jit(solution)/shard_map/ppermute | solution.py:203
  12.0 11.3 %collective-permute-start.3 = (bf16[1,160,384]{2,1,0:T(8,128)(2,1)S(1)}, bf16[1,160,384]{2,1,0:T(8,128)(2,1)S(1)}, u32[]{:S(2)}, u32[]{:S(2)}) collective-permute-start(bf16[1,160,384]{2,1,0:T(8,128)(2,1)S(1)} %collective-permute-done.2.edges), channel_id=1, source_target_pairs={{0,2},{2,0},{4,6},{6,4},{8,10},{10,8},{12,14},{14,12},{16,18},{18,... | collective-permute-start | bytes 368648 | tf_op jit(solution)/shard_map/ppermute | solution.py:202
  14.1 3.3 %copy-start = (bf16[3,3,3,384,384]{4,3,2,1,0:T(8,128)(2,1)S(1)}, bf16[3,3,3,384,384]{4,3,2,1,0:T(8,128)(2,1)}, u32[]{:S(2)}) copy-start(bf16[3,3,3,384,384]{4,3,2,1,0:T(8,128)(2,1)} %weight.5) | copy-start | bytes 23887876
  17.4 0.9 %copy-start.4 = (bf16[1,2,160,384]{3,2,1,0:T(8,128)(2,1)S(1)}, bf16[1,2,160,384]{3,2,1,0:T(8,128)(2,1)}, u32[]{:S(2)}) copy-start(bf16[1,2,160,384]{3,2,1,0:T(8,128)(2,1)} %param.8) | copy-start | bytes 737284
  18.3 3.3 %copy-start.1 = (bf16[3,3,3,384,384]{4,3,2,1,0:T(8,128)(2,1)S(1)}, bf16[3,3,3,384,384]{4,3,2,1,0:T(8,128)(2,1)}, u32[]{:S(2)}) copy-start(bf16[3,3,3,384,384]{4,3,2,1,0:T(8,128)(2,1)} %weight.5) | copy-start | bytes 23887876
  23.3 17.5 %copy-start.6 = (f32[768]{0:T(1024)S(1)}, f32[768]{0:T(1024)}, u32[]{:S(2)}) copy-start(f32[768]{0:T(1024)} %param.13) | copy-start | bytes 9220
  23.3 17.5 %copy-start.3 = (bf16[3,3,384,192]{2,3,1,0:T(8,128)(2,1)S(1)}, bf16[3,3,384,192]{2,3,1,0:T(8,128)(2,1)}, u32[]{:S(2)}) copy-start(bf16[3,3,384,192]{2,3,1,0:T(8,128)(2,1)} %param.14) | copy-start | bytes 3981316
  25.1 10.4 %collective-permute-start.8 = (bf16[2,160,384]{2,1,0:T(8,128)(2,1)S(1)}, bf16[2,160,384]{2,1,0:T(8,128)(2,1)S(1)}, u32[]{:S(2)}, u32[]{:S(2)}) collective-permute-start(bf16[2,160,384]{2,1,0:T(8,128)(2,1)S(1)} %get-tuple-element.7.own), channel_id=1, source_target_pairs={{0,4},{2,6},{4,8},{6,10},{8,12},{10,14},{12,16},{14,18},{16,20},{1... | collective-permute-start | bytes 737288 | tf_op jit(solution)/shard_map/ppermute | solution.py:183
  27.4 11.7 %collective-permute-start.9 = (bf16[1,160,384]{2,1,0:T(8,128)(2,1)S(1)}, bf16[1,160,384]{2,1,0:T(8,128)(2,1)S(1)}, u32[]{:S(2)}, u32[]{:S(2)}) collective-permute-start(bf16[1,160,384]{2,1,0:T(8,128)(2,1)S(1)} %get-tuple-element.8), channel_id=1, source_target_pairs={{0,5},{1,4},{2,7},{3,6},{4,9},{5,8},{6,11},{7,10},{8,13},{9,12},{1... | collective-permute-start | bytes 368648 | tf_op jit(solution)/shard_map/ppermute | solution.py:193
  32.4 7.6 %collective-permute-start.7 = (bf16[1,160,384]{2,1,0:T(8,128)(2,1)S(1)}, bf16[1,160,384]{2,1,0:T(8,128)(2,1)S(1)}, u32[]{:S(2)}, u32[]{:S(2)}) collective-permute-start(bf16[1,160,384]{2,1,0:T(8,128)(2,1)S(1)} %get-tuple-element.8), channel_id=1, source_target_pairs={{0,1},{1,0},{2,3},{3,2},{4,5},{5,4},{6,7},{7,6},{8,9},{9,8},{10,11... | collective-permute-start | bytes 368648 | tf_op jit(solution)/shard_map/ppermute | solution.py:191
  32.7 9.6 %collective-permute-start.12 = (bf16[2,160,384]{2,1,0:T(8,128)(2,1)S(1)}, bf16[2,160,384]{2,1,0:T(8,128)(2,1)S(1)}, u32[]{:S(2)}, u32[]{:S(2)}) collective-permute-start(bf16[2,160,384]{2,1,0:T(8,128)(2,1)S(1)} %get-tuple-element.7.own), channel_id=1, source_target_pairs={{0,2},{2,0},{4,6},{6,4},{8,10},{10,8},{12,14},{14,12},{16,18},{18,... | collective-permute-start | bytes 737288 | tf_op jit(solution)/shard_map/ppermute | solution.py:203
  35.5 6.8 %collective-permute-start.10 = (bf16[2,160,384]{2,1,0:T(8,128)(2,1)S(1)}, bf16[2,160,384]{2,1,0:T(8,128)(2,1)S(1)}, u32[]{:S(2)}, u32[]{:S(2)}) collective-permute-start(bf16[2,160,384]{2,1,0:T(8,128)(2,1)S(1)} %collective-permute-done.8.main2), channel_id=1, source_target_pairs={{0,2},{2,0},{4,6},{6,4},{8,10},{10,8},{12,14},{14,12},{16,18},{18,... | collective-permute-start | bytes 737288 | tf_op jit(solution)/shard_map/ppermute | solution.py:202
  39.1 3.1 %collective-permute-start.11 = (bf16[1,160,384]{2,1,0:T(8,128)(2,1)S(1)}, bf16[1,160,384]{2,1,0:T(8,128)(2,1)S(1)}, u32[]{:S(2)}, u32[]{:S(2)}) collective-permute-start(bf16[1,160,384]{2,1,0:T(8,128)(2,1)S(1)} %collective-permute-done.9.edges2), channel_id=1, source_target_pairs={{0,2},{2,0},{4,6},{6,4},{8,10},{10,8},{12,14},{14,12},{16,18},{18,... | collective-permute-start | bytes 368648 | tf_op jit(solution)/shard_map/ppermute | solution.py:202
  40.0 2.3 %collective-permute-start.13 = (bf16[1,160,384]{2,1,0:T(8,128)(2,1)S(1)}, bf16[1,160,384]{2,1,0:T(8,128)(2,1)S(1)}, u32[]{:S(2)}, u32[]{:S(2)}) collective-permute-start(bf16[1,160,384]{2,1,0:T(8,128)(2,1)S(1)} %collective-permute-done.7.edges), channel_id=1, source_target_pairs={{0,2},{2,0},{4,6},{6,4},{8,10},{10,8},{12,14},{14,12},{16,18},{18,... | collective-permute-start | bytes 368648 | tf_op jit(solution)/shard_map/ppermute | solution.py:203
  40.8 1.5 %copy-start.2 = (bf16[3,384,768]{2,1,0:T(8,128)(2,1)S(1)}, bf16[3,384,768]{2,1,0:T(8,128)(2,1)}, u32[]{:S(2)}) copy-start(bf16[3,384,768]{2,1,0:T(8,128)(2,1)} %param.12) | copy-start | bytes 5308420
  40.8 1.5 %copy-start.5 = (f32[192]{0:T(256)S(1)}, f32[192]{0:T(256)}, u32[]{:S(2)}) copy-start(f32[192]{0:T(256)} %param.15) | copy-start | bytes 2308

commit v3 on v0

v3 whole, which is shorter than its diff:
```python
import functools

import jax
import jax.numpy as jnp
from jax import lax
from jax.experimental import pallas as pl
from jax.experimental.pallas import tpu as pltpu
from jax.sharding import PartitionSpec as P

F32 = jnp.float32
BF16 = jnp.bfloat16
VMEM = pl.BlockSpec(memory_space=pltpu.VMEM)
SMEM = pl.BlockSpec(memory_space=pltpu.SMEM)
ANY = pl.BlockSpec(memory_space=pl.ANY)
HBM = pl.BlockSpec(memory_space=pltpu.HBM)
LANES = 128
SHARE = 3000000000


def in_order(place, index, count):
    return jnp.where(place[0] == 1, count - 1 - index, index)


def activate(rows, gain):
    values = rows.astype(F32)
    meansq = jnp.mean(values * values, axis=-1, keepdims=True)
    scaled = values * lax.rsqrt(meansq + 1e-06) * gain
    return (scaled * jax.nn.sigmoid(scaled)).astype(BF16)


def moved(rows, step):
    cols = rows.shape[0]
    index = lax.broadcasted_iota(jnp.int32, rows.shape, 0)
    edge = 0 if step == 1 else cols - 1
    return jnp.where(index == edge, 0.0, pltpu.roll(rows, step % cols, 0))


def conv_rows(place, halos, rows, sources):
    lead = halos - 1
    sums = []
    for q in range(rows):
        lefts, rights = [], []
        for weight, field in sources:
            for dh in range(3):
                s = lead + q + dh - 1
                if s in field:
                    lefts.append(field[s]())
                    tap = in_order(place, dh, 3)
                    rights.append(jnp.concatenate([weight[tap, dw] for dw in range(3)], axis=-1))
        if not lefts:
            sums.append(None)
            continue
        total = jnp.dot(
            jnp.concatenate(lefts, axis=-1), jnp.concatenate(rights, axis=0), preferred_element_type=F32
        )
        chans = total.shape[1] // 3
        sums.append(
            total[:, chans : 2 * chans]
            + moved(total[:, :chans], 1)
            + moved(total[:, 2 * chans :], -1)
        )
    return sums


def hold(act, slot, value):
    act[slot] = value
    return lambda: act[slot]


def held_rows(place, halos, main, gain, act):
    rows = main.shape[0]
    return {
        halos - 1 + q: hold(act, q, activate(main[in_order(place, q, rows)], gain)) for q in range(rows)
    }


def held_edges(halos, rows, edges, gain, act, slot, known=True):
    where = (rows,) if halos == 1 else (0, rows + 1)
    return {
        s: hold(act, slot + h, activate(jnp.where(known, edges[h], jnp.zeros_like(edges[h])), gain))
        for h, s in enumerate(where)
    }


def loads(w_hbm, w, sems, dt):
    return [
        pltpu.make_async_copy(w_hbm.at[dt, dh, dw], w.at[dh, dw], sems.at[dh, dw])
        for dh in range(3)
        for dw in range(3)
    ]


def near_row(place, field, row):
    row[0] = field[in_order(place, field.shape[0] - 1, field.shape[0])]


def conv_first(halos, place, own, edges, gain, bias, w_hbm, acc, w0, w1, w2, act, sems):
    rows = own.shape[0]
    now = loads(w_hbm, w2, sems.at[2], 2)
    ahead = loads(w_hbm, w0, sems.at[0], 0) + loads(w_hbm, w1, sems.at[1], 1)
    for copy in now + ahead:
        copy.start()
    field = held_rows(place, halos, own, gain[...][None], act)
    field.update(held_edges(halos, rows, edges, gain[...][None], act, rows))
    for copy in now:
        copy.wait()
    for q, part in enumerate(conv_rows(place, halos, rows, [(w2, field)])):
        acc[q] = part + bias[...][None] + own[in_order(place, q, rows)].astype(F32)
    for copy in ahead:
        copy.wait()


def conv_second(halos, place, main, before, gain, w0, acc, act):
    rows = main.shape[0]

    @pl.when(place[4] == 0)
    def _():
        acc[...] = before[...]

    @pl.when(place[4] != 0)
    def _():
        field = held_rows(place, halos, main, gain[...][None], act)
        for q, part in enumerate(conv_rows(place, halos, rows, [(w0, field)])):
            acc[q] = before[q] + part


def pick(place, even, odd, chosen):
    @pl.when((place[3] == 0) & (place[4] == 0))
    def _():
        chosen[...] = jnp.zeros_like(chosen)

    @pl.when((place[3] == 0) & (place[4] != 0))
    def _():
        chosen[...] = even[...]

    @pl.when(place[3] != 0)
    def _():
        chosen[...] = odd[...]


def conv_third(halos, place, main_a, main_b, edges2, edges_a, edges_b, before, gain, w0, w1,
               block, near, act, main, edges):
    rows = block.shape[0]
    pick(place, main_a, main_b, main)
    pick(place, edges_a, edges_b, edges)
    field = held_rows(place, halos, main, gain[...][None], act)
    field.update(held_edges(halos, rows, edges, gain[...][None], act, rows))
    field2 = held_edges(halos, rows, edges2, gain[...][None], act, rows + halos, place[4] != 0)
    for q, part in enumerate(conv_rows(place, halos, rows, [(w1, field), (w0, field2)])):
        value = (before[q] + part).astype(BF16)
        block[in_order(place, q, rows)] = value
        if q == rows - 1:
            near[halos - 1] = value
        if q == 0 and halos == 2:
            near[0] = value


def up_rows(place, rows, out_rows, pairs, ubias, uw, wide, outs, out_hbm, osems):
    cols = wide.shape[2] // 2
    rest = ubias.shape[-1] - LANES
    chans = uw.shape[1] // 2
    lane = lax.broadcasted_iota(jnp.int32, (cols, LANES), 1)
    stores = []
    for slot_o, o in enumerate(out_rows):
        phase, taken = pairs[o]
        left = jnp.concatenate([jnp.concatenate([r[f] for r in taken], axis=-1) for f in range(2)], axis=0)
        right = uw[phase, (2 - len(taken)) * chans :, :]
        both = jnp.dot(left, right, preferred_element_type=F32)
        for f in range(2):
            part = both[f * cols : (f + 1) * cols]
            g = [part[:, k * LANES : (k + 1) * LANES] for k in range(6)]
            tail = g[4] + jnp.where(lane < rest, moved(g[5], 1), moved(g[5], -1))
            slot = f
            wide[slot, 0, pl.ds(0, cols, stride=2), :] = g[0] + moved(g[2], 1) + ubias[:LANES][None]
            wide[slot, 0, pl.ds(1, cols, stride=2), :] = g[1] + moved(g[3], -1) + ubias[:LANES][None]
            wide[slot, 1, pl.ds(0, cols, stride=2), :] = tail
            wide[slot, 1, pl.ds(1, cols, stride=2), :] = pltpu.roll(tail, LANES - rest, 1)
            outs[f, slot_o, :LANES, :] = wide[slot, 0].T.astype(BF16)
            outs[f, slot_o, LANES:, :] = (wide[slot, 1, :, :rest] + ubias[LANES:][None]).T.astype(BF16)
            copy = pltpu.make_async_copy(
                outs.at[f, slot_o], out_hbm.at[f, in_order(place, o, 2 * rows)], osems.at[f, slot_o]
            )
            copy.start()
            stores.append(copy)
    return stores


def inner_rows(halos, rows):
    inner = list(range(0 if halos == 1 else 1, 2 * rows - 1))
    return inner, [o for o in range(2 * rows) if o not in inner]


def up_main(halos, place, own, main2, main_a, main_b, tbias, ubias, tw, uw,
            out_hbm, kept, main1, doubled, wide, outs, osems):
    rows, cols, chans = own.shape
    pick(place, main_a, main_b, main1)
    lefts = []
    for q in range(rows):
        at = in_order(place, q, rows)
        first = main2[at]
        first = jnp.where(place[4] != 0, first, jnp.zeros_like(first))
        lefts.append(jnp.concatenate([first, main1[at], own[at]], axis=-1))
    mixed = jnp.dot(jnp.concatenate(lefts, axis=0), tw[...], preferred_element_type=F32) + tbias[...][None]
    for q in range(rows):
        for f in range(2):
            value = mixed[q * cols : (q + 1) * cols, f * chans : (f + 1) * chans].astype(BF16)
            doubled[f, q] = value
            if q == rows - 1:
                kept[f, halos - 1] = value
            if q == 0 and halos == 2:
                kept[f, 0] = value

    pairs = {}
    for q in range(rows):
        for phase in range(2):
            sources = [s for s in (q - 1 + phase, q + phase) if 0 <= s < rows]
            pairs[2 * q + phase] = phase, [[doubled[f, s] for f in range(2)] for s in sources]
    out_rows = inner_rows(halos, rows)[0]
    for copy in up_rows(place, rows, out_rows, pairs, ubias, uw, wide, outs, out_hbm, osems):
        copy.wait()


def up_edge(halos, place, edges, edges2, edges_a, edges_b, kept, tbias, ubias, tw, uw, out_so_far,
            out_hbm, edges1, doubled, wide, outs, osems):
    del out_so_far
    cols, chans = edges.shape[1:]
    rows = out_hbm.shape[1] // 2
    pick(place, edges_a, edges_b, edges1)
    first = [jnp.where(place[4] != 0, edges2[h], jnp.zeros_like(edges2[h])) for h in range(halos)]
    left = jnp.concatenate(
        [jnp.concatenate([first[h], edges1[h], edges[h]], axis=-1) for h in range(halos)], axis=0
    )
    mixed = jnp.dot(left, tw[...], preferred_element_type=F32) + tbias[...][None]
    for h in range(halos):
        value = mixed[h * cols : (h + 1) * cols]
        if halos == 2:
            value = jnp.where(place[1 + h] == 1, value, 0.0)
        for f in range(2):
            doubled[f, h] = value[:, f * chans : (f + 1) * chans].astype(BF16)
    last = halos - 1
    pairs = {2 * rows - 1: (1, [[kept[f, last] for f in range(2)], [doubled[f, last] for f in range(2)]])}
    if halos == 2:
        pairs[0] = (0, [[doubled[f, 0] for f in range(2)], [kept[f, 0] for f in range(2)]])
    out_rows = inner_rows(halos, rows)[1]
    for copy in up_rows(place, rows, out_rows, pairs, ubias, uw, wide, outs, out_hbm, osems):
        copy.wait()


def merge_kernel(place, taps_hbm, tw_hbm, merged, tw, taps, sems):
    load = pltpu.make_async_copy(taps_hbm, taps, sems.at[0])
    load.start()
    copy = pltpu.make_async_copy(tw_hbm, tw, sems.at[1])
    copy.start()
    load.wait()
    chans = taps.shape[3]

    def tap(dh, dw):
        return taps[in_order(place, dh, 3), dw].astype(F32)

    for phase, sets in enumerate((((0,), (1, 2)), ((0, 1), (2,)))):
        for which, rows in enumerate(sets):
            cols = [sum(tap(dh, dw) for dh in rows) for dw in range(3)]
            groups = (cols[1] + cols[2], cols[0] + cols[1], cols[0], cols[2])
            wide = jnp.concatenate([g[:LANES] for g in groups] + [g[LANES:] for g in groups], axis=0)
            merged[phase, which * chans : (which + 1) * chans, :] = wide.T.astype(BF16)
    copy.wait()


def in_hbm(array):
    return pltpu.with_memory_space_constraint(array, pltpu.HBM)


def after(array, *others):
    return lax.optimization_barrier((array, *others))[0]


def in_chip(array):
    return lax.ppermute(array, "tm", [(i, i ^ 1) for i in range(lax.axis_size("tm"))])


def two_back(array):
    frames = lax.axis_size("tm")
    return lax.ppermute(array, "tm", [(i, (i + 2) % frames) for i in range(frames)])


def beside(near, halos):
    frames = lax.axis_size("tm")
    tiles = lax.axis_size("tile")
    if halos == 1:
        sides = [(near[0], [(0, 1), (1, 0)])]
    else:
        sides = [
            (near[1], [(j, j + 1) for j in range(tiles - 1)]),
            (near[0], [(j + 1, j) for j in range(tiles - 1)]),
        ]
    edges2 = [
        lax.ppermute(
            row,
            ("tm", "tile"),
            [(a * tiles + i, (a + 2) % frames * tiles + j) for a in range(frames) for i, j in route],
        )
        for row, route in sides
    ]
    edges = [lax.ppermute(row, "tile", route) for row, route in sides]
    if halos == 1:
        return edges[0], edges2[0]
    return jnp.concatenate(edges), jnp.concatenate(edges2)


def local(latent, gain, conv_weight, conv_bias, time_weight, time_bias, up_weight, up_bias):
    tiles = lax.axis_size("tile")
    tile = lax.axis_index("tile")
    frame_at = lax.axis_index("tm")
    halos = 1 if tiles == 2 else 2
    main = latent[0]
    rows, cols, chans = main.shape
    outs_n = up_weight.shape[3]
    flip = tile if halos == 1 else 0 * tile
    place = jnp.stack([flip, tile > 0, tile < tiles - 1, frame_at % 2, frame_at >= 2]).astype(jnp.int32)

    def call(kernel, name, share, ins, outs, scratch, **rest):
        return pl.pallas_call(
            kernel,
            out_shape=tuple(s for s, _ in outs),
            in_specs=[SMEM] + ins,
            out_specs=tuple(s for _, s in outs),
            scratch_shapes=scratch,
            compiler_params=pltpu.CompilerParams(vmem_limit_bytes=20 << 20),
            cost_estimate=pl.CostEstimate(
                flops=int(SHARE * share), bytes_accessed=1000, transcendentals=0
            ),
            name=name,
            **rest,
        )

    field = (rows, cols, chans)
    sides = (halos, cols, chans)
    taps = pltpu.VMEM((3, 3, chans, chans), BF16)
    total = (pltpu.VMEM(field, F32), VMEM)
    taps_t = in_hbm(up_weight.transpose(0, 1, 3, 2))
    merge = call(
        merge_kernel, "merge_taps", 1,
        [HBM, HBM],
        [(pltpu.VMEM((2, 2 * chans, 4 * outs_n), BF16), VMEM), (pltpu.VMEM((3 * chans, 2 * chans), BF16), VMEM)],
        [pltpu.VMEM((3, 3, outs_n, chans), BF16), pltpu.SemaphoreType.DMA((2,))],
    )

    if halos == 1:
        near = call(near_row, "near_row", 3, [VMEM], [(jax.ShapeDtypeStruct(sides, BF16), VMEM)], [])(place, main)
    else:
        near = [main[:1], main[rows - 1 :]]
    main2 = two_back(main)
    edges, edges2 = beside(near, halos)
    odd = in_chip(main)
    even = in_chip(main2)
    acc, w0, w1 = call(
        functools.partial(conv_first, halos), "conv_own_frame", 0.2,
        [VMEM] * 4 + [HBM],
        [total, (taps, VMEM), (taps, VMEM)],
        [taps, pltpu.VMEM((rows + halos, cols, chans), BF16), pltpu.SemaphoreType.DMA((3, 3, 3))],
    )(place, main, edges, gain, conv_bias, in_hbm(conv_weight))
    odd_edges = in_chip(edges)
    own_acc = acc
    (acc,) = call(
        functools.partial(conv_second, halos), "conv_two_back", 1,
        [VMEM] * 4,
        [total],
        [pltpu.VMEM(field, BF16)],
    )(place, main2, acc, gain, w0)
    even_edges = in_chip(after(edges2, own_acc))
    block, near = call(
        functools.partial(conv_third, halos), "conv_one_back", 1,
        [VMEM] * 9,
        [(jax.ShapeDtypeStruct(field, BF16), VMEM), (jax.ShapeDtypeStruct(sides, BF16), VMEM)],
        [
            pltpu.VMEM((rows + 2 * halos, cols, chans), BF16),
            pltpu.VMEM(field, BF16),
            pltpu.VMEM(sides, BF16),
        ],
    )(place, even, odd, edges2, even_edges, odd_edges, acc, gain, w0, w1)

    near = [near[h : h + 1] for h in range(halos)]
    main = block
    main2 = two_back(main)
    edges, edges2 = beside(near, halos)
    odd = in_chip(main)
    merged, tw = merge(place, after(taps_t, block), in_hbm(time_weight.reshape(3 * chans, 2 * chans)))
    even = in_chip(main2)
    mains = main, main2, even, odd
    edges = edges, edges2, in_chip(after(edges2, merged)), in_chip(edges)
    inner, outer = (len(o) for o in inner_rows(halos, rows))
    out_shape = (jax.ShapeDtypeStruct((2, 2 * rows, outs_n, 2 * cols), BF16), ANY)

    def scratch(count, held):
        return [
            pltpu.VMEM((2, held, cols, chans), BF16),
            pltpu.VMEM((2, 2, 2 * cols, LANES), F32),
            pltpu.VMEM((2, count, outs_n, 2 * cols), BF16),
            pltpu.SemaphoreType.DMA((2, count)),
        ]

    out, kept = call(
        functools.partial(up_main, halos), "time_and_up", 2,
        [VMEM] * 8,
        [out_shape, (pltpu.VMEM((2,) + sides, BF16), VMEM)],
        [pltpu.VMEM(field, BF16)] + scratch(inner, rows),
    )(place, *mains, time_bias, up_bias, tw, merged)
    (out,) = call(
        functools.partial(up_edge, halos), "time_and_up_edge", 1,
        [VMEM] * 9 + [ANY],
        [out_shape],
        [pltpu.VMEM(sides, BF16)] + scratch(outer, halos),
        input_output_aliases={10: 0},
    )(place, *edges, kept, time_bias, up_bias, tw, merged, out)
    return out.transpose(0, 1, 3, 2)


def solution(mesh):
    placed = (P("tm", "tile", None, None), P(), P(), P(), P(), P(), P(), P())
    return jax.shard_map(
        local, mesh=mesh, in_specs=placed, out_specs=P("tm", "tile", None, None), check_vma=False
    )
```

time: 96.6 us -> 41.3 us (0.43)
  local copies, waits for them, and re-layouts: 31.1 us -> 0.1 us
  Pallas kernels: 0 us -> 17.1 us
  matrix products: 13.6 us -> 0 us
  waiting for transfers between devices: 23.7 us -> 13.7 us
  starting transfers between devices: 20 us -> 10.1 us
  other arithmetic: 6.79 us -> 0 us
    pallas_call x0 -> x7, Pallas kernels: none -> 17.1 us  [the longest x1 4.44 us: local(): call(functools.partial(conv_first, halos), 'conv_own_frame', 0.2, [VMEM]...]
    dot_general x18 -> x0, matrix products: 13.6 us -> none  [the longest x3 6.32 us: upsample_conv(): jnp.dot(wide.reshape(-1, 3 * chans), up_weight[step_h].reshape(3 * chans,...]
    slice x16 -> x0, local copies, waits for them, and re-layouts: 13.4 us -> none  [the longest x2 5.14 us: upsample_conv(): slab[:, :, shift_w:shift_w + cols2]]
    reshape x3 -> x0, local copies, waits for them, and re-layouts: 11.5 us -> none  [the longest x1 9.07 us: upsample_conv(): jnp.repeat(jnp.repeat(edged, 2, axis=1), 2, axis=2)[:, 1:2 * rows_n + 3]]
    ppermute x8 -> x14, waiting for transfers between devices: 23.7 us -> 13.7 us  [the longest x2 8.59 us: two_back(): lax.ppermute(array, 'tm', [(i, (i + 2) % frames) for i in range(frames)])]
    ppermute x8 -> x14, starting transfers between devices: 20 us -> 10.1 us  [the longest x2 3.33 us: beside(): lax.ppermute(row, ('tm', 'tile'), [(a * tiles + i, (a + 2) % frames * til...]
    concatenate x15 -> x0, other arithmetic: 4.39 us -> none  [the longest x3 3.11 us: upsample_conv(): jnp.concatenate([slab[:, :, shift_w:shift_w + cols2] for shift_w in range...]
    broadcast_in_dim x2 -> x0, local copies, waits for them, and re-layouts: 3.68 us -> none  [the longest x1 3.49 us: upsample_conv(): jnp.repeat(jnp.repeat(edged, 2, axis=1), 2, axis=2)[:, 1:2 * rows_n + 3]]
  transfers between devices with their start and end apart: 8 -> 14, of which waited for: 6 -> 6; matrix products, arithmetic and copies ran while one was open for 8% -> 0% of each run, Pallas kernels for 0% -> 31%
where the time goes in v3:
time: 41.3 us; the launch traced here: 41.1 us
  Pallas kernels  17.1 us (41%)
  waiting for transfers between devices  13.7 us (33%)
  starting transfers between devices  10.1 us (24%)
    ppermute x2, waiting for transfers between devices, two_back(): lax.ppermute(array, 'tm', [(i, (i + 2) % frames) for i in range(frames)])  8.59 us
    pallas_call x1, Pallas kernels, local(): call(functools.partial(conv_first, halos), 'conv_own_frame', 0.2, [VMEM]...  4.44 us
    pallas_call x1, Pallas kernels, local(): call(functools.partial(up_main, halos), 'time_and_up', 2, [VMEM] * 8, [ou...  3.95 us
    ppermute x2, starting transfers between devices, beside(): lax.ppermute(row, ('tm', 'tile'), [(a * tiles + i, (a + 2) % frames * til...  3.33 us
    ppermute x2, starting transfers between devices, two_back(): lax.ppermute(array, 'tm', [(i, (i + 2) % frames) for i in range(frames)])  3 us
    pallas_call x1, Pallas kernels, local(): merge(place, after(taps_t, block), in_hbm(time_weight.reshape(3 * chans,...  2.65 us
    pallas_call x1, Pallas kernels, local(): call(functools.partial(up_edge, halos), 'time_and_up_edge', 1, [VMEM] * 9...  2.51 us
    ppermute x2, starting transfers between devices, beside(): edges = [lax.ppermute(row, 'tile', route) for row, route in sides]  2.41 us
  transfers between devices with their start and end apart: 14, of which 6 were waited for; matrix products, arithmetic and copies ran while one was open for 0% of the time, Pallas kernels for 31%

profile of v3, /device:TPU:0, one launch (start us, length us, event | category | flops | bytes accessed | tf_op | source)
XLA Modules:
  0.0 41.1 jit_solution(12204036342633419226)
XLA Ops:
  0.0 2.9 %collective-permute-start = (bf16[2,160,384]{2,1,0:T(8,128)(2,1)}, bf16[2,160,384]{2,1,0:T(8,128)(2,1)S(1)}, u32[]{:S(2)}, u32[]{:S(2)}) collective-permute-start(bf16[2,160,384]{2,1,0:T(8,128)(2,1)} %bitcast.5.field.own), channel_id=1, source_target_pairs={{0,4},{2,6},{4,8},{6,10},{8,12},{10,14},{12,16},{14,18},{16,20},{1... | collective-permute-start | bytes 737288 | tf_op jit(solution)/shard_map/ppermute | solution.py:283
  2.9 0.1 stack.35.place
  3.0 0.0 copy-start
  3.0 0.0 copy-start.1
  3.0 1.0 %near_row.1 = bf16[1,160,384]{2,1,0:T(8,128)(2,1)S(1)} custom-call(s32[5]{0:T(128)S(1)} %stack.35.place, bf16[2,160,384]{2,1,0:T(8,128)(2,1)} %bitcast.5.field.own), custom_call_target="tpu_custom_call" | custom-call | flops 8999999488 | bytes 1000 | tf_op jit(solution)/shard_map/near_row/pallas_call | solution.py:349
  4.0 1.6 %collective-permute-start.4 = (bf16[1,160,384]{2,1,0:T(8,128)(2,1)S(1)}, bf16[1,160,384]{2,1,0:T(8,128)(2,1)S(1)}, u32[]{:S(2)}, u32[]{:S(2)}) collective-permute-start(bf16[1,160,384]{2,1,0:T(8,128)(2,1)S(1)} %near_row.1), channel_id=1, source_target_pairs={{0,1},{1,0},{2,3},{3,2},{4,5},{5,4},{6,7},{7,6},{8,9},{9,8},{10,11... | collective-permute-start | bytes 368648 | tf_op jit(solution)/shard_map/ppermute | solution.py:304
  5.6 1.5 %collective-permute-start.3 = (bf16[1,160,384]{2,1,0:T(8,128)(2,1)S(1)}, bf16[1,160,384]{2,1,0:T(8,128)(2,1)S(1)}, u32[]{:S(2)}, u32[]{:S(2)}) collective-permute-start(bf16[1,160,384]{2,1,0:T(8,128)(2,1)S(1)} %near_row.1), channel_id=1, source_target_pairs={{0,5},{1,4},{2,7},{3,6},{4,9},{5,8},{6,11},{7,10},{8,13},{9,12},{1... | collective-permute-start | bytes 368648 | tf_op jit(solution)/shard_map/ppermute | solution.py:297
  7.1 0.0 collective-permute-start.2
  7.1 1.9 %collective-permute-done.4.edges = bf16[1,160,384]{2,1,0:T(8,128)(2,1)S(1)} collective-permute-done((bf16[1,160,384]{2,1,0:T(8,128)(2,1)S(1)}, bf16[1,160,384]{2,1,0:T(8,128)(2,1)S(1)}, u32[]{:S(2)}, u32[]{:S(2)}) %collective-permute-start.4) | collective-permute-done | bytes 122912 | tf_op jit(solution)/shard_map/ppermute | solution.py:304
  9.0 0.0 copy-done
  9.0 0.0 copy-done.1
  9.0 4.4 %conv_own_frame.1 = (f32[2,160,384]{2,1,0:T(8,128)S(1)}, bf16[3,3,384,384]{3,2,1,0:T(8,128)(2,1)S(1)}, bf16[3,3,384,384]{3,2,1,0:T(8,128)(2,1)S(1)}) custom-call(s32[5]{0:T(128)S(1)} %stack.35.place, bf16[2,160,384]{2,1,0:T(8,128)(2,1)} %bitcast.5.field.own, bf16[1,160,384]{2,1,0:T(8,128)(2,1)S(1)} %collective-permute-done.4.edges, f32[384]{0:T(512)S(1)} %copy-done.1, ...), custom_call_target="tpu_custom_call" | custom-call | flops 600000000 | bytes 1000 | tf_op jit(solution)/shard_map/conv_own_frame/pallas_call | solution.py:356
  13.4 2.3 %collective-permute-done.3.edges2 = bf16[1,160,384]{2,1,0:T(8,128)(2,1)S(1)} collective-permute-done((bf16[1,160,384]{2,1,0:T(8,128)(2,1)S(1)}, bf16[1,160,384]{2,1,0:T(8,128)(2,1)S(1)}, u32[]{:S(2)}, u32[]{:S(2)}) %collective-permute-start.3) | collective-permute-done | bytes 122912 | tf_op jit(solution)/shard_map/ppermute | solution.py:297
  15.7 0.0 collective-permute-start.5
  15.7 0.5 %collective-permute-start.6 = (bf16[1,160,384]{2,1,0:T(8,128)(2,1)S(1)}, bf16[1,160,384]{2,1,0:T(8,128)(2,1)S(1)}, u32[]{:S(2)}, u32[]{:S(2)}) collective-permute-start(bf16[1,160,384]{2,1,0:T(8,128)(2,1)S(1)} %collective-permute-done.4.edges), channel_id=1, source_target_pairs={{0,2},{2,0},{4,6},{6,4},{8,10},{10,8},{12,14},{14,12},{16,18},{18,... | collective-permute-start | bytes 368648 | tf_op jit(solution)/shard_map/ppermute | solution.py:278
  16.2 0.0 collective-permute-done.main
  16.2 0.0 collective-permute-start.1
  16.2 0.6 %conv_two_back.1.before = f32[2,160,384]{2,1,0:T(8,128)S(1)} custom-call(s32[5]{0:T(128)S(1)} %stack.35.place, bf16[2,160,384]{2,1,0:T(8,128)(2,1)S(1)} %collective-permute-done.main, f32[2,160,384]{2,1,0:T(8,128)S(1)} %get-tuple-element.17.before, f32[384]{0:T(512)S(1)} %copy-done.1, bf16[3,3,384,384]{3,2,1,0:T(8,128)(2,1)S(1)} %get-tuple-element.19.w0), custom_call_target="tpu_custom_call" | custom-call | flops 3000000000 | bytes 1000 | tf_op jit(solution)/shard_map/conv_two_back/pallas_call | solution.py:364
  16.8 0.2 collective-permute-done.5.edges_a
  17.1 0.2 collective-permute-done.6.edges_b
  17.2 0.0 collective-permute-done.2.main_b
  17.2 0.5 %collective-permute-done.1.main_a = bf16[2,160,384]{2,1,0:T(8,128)(2,1)S(1)} collective-permute-done((bf16[2,160,384]{2,1,0:T(8,128)(2,1)S(1)}, bf16[2,160,384]{2,1,0:T(8,128)(2,1)S(1)}, u32[]{:S(2)}, u32[]{:S(2)}) %collective-permute-start.1) | collective-permute-done | bytes 245792 | tf_op jit(solution)/shard_map/ppermute | solution.py:278
  17.8 2.0 %conv_one_back.1 = (bf16[2,160,384]{2,1,0:T(8,128)(2,1)S(1)}, bf16[1,160,384]{2,1,0:T(8,128)(2,1)S(1)}) custom-call(s32[5]{0:T(128)S(1)} %stack.35.place, bf16[2,160,384]{2,1,0:T(8,128)(2,1)S(1)} %collective-permute-done.1.main_a, bf16[2,160,384]{2,1,0:T(8,128)(2,1)S(1)} %collective-permute-done.2.main_b, ...), custom_call_target="tpu_custom_call" | custom-call | flops 3000000000 | bytes 1000 | tf_op jit(solution)/shard_map/conv_one_back/pallas_call | solution.py:371
  19.7 0.1 collective-permute-start.11
  19.8 0.2 collective-permute-start.13
  20.0 1.8 %collective-permute-start.8 = (bf16[1,160,384]{2,1,0:T(8,128)(2,1)S(1)}, bf16[1,160,384]{2,1,0:T(8,128)(2,1)S(1)}, u32[]{:S(2)}, u32[]{:S(2)}) collective-permute-start(bf16[1,160,384]{2,1,0:T(8,128)(2,1)S(1)} %get-tuple-element.21), channel_id=1, source_target_pairs={{0,5},{1,4},{2,7},{3,6},{4,9},{5,8},{6,11},{7,10},{8,13},{9,12},{1... | collective-permute-start | bytes 368648 | tf_op jit(solution)/shard_map/ppermute | solution.py:297
  21.9 0.8 %collective-permute-start.7 = (bf16[1,160,384]{2,1,0:T(8,128)(2,1)S(1)}, bf16[1,160,384]{2,1,0:T(8,128)(2,1)S(1)}, u32[]{:S(2)}, u32[]{:S(2)}) collective-permute-start(bf16[1,160,384]{2,1,0:T(8,128)(2,1)S(1)} %get-tuple-element.21), channel_id=1, source_target_pairs={{0,1},{1,0},{2,3},{3,2},{4,5},{5,4},{6,7},{7,6},{8,9},{9,8},{10,11... | collective-permute-start | bytes 368648 | tf_op jit(solution)/shard_map/ppermute | solution.py:304
  22.7 8.6 %collective-permute-done.11.main2 = bf16[2,160,384]{2,1,0:T(8,128)(2,1)S(1)} collective-permute-done((bf16[2,160,384]{2,1,0:T(8,128)(2,1)S(1)}, bf16[2,160,384]{2,1,0:T(8,128)(2,1)S(1)}, u32[]{:S(2)}, u32[]{:S(2)}) %collective-permute-start.11) | collective-permute-done | bytes 245792 | tf_op jit(solution)/shard_map/ppermute | solution.py:283
  31.3 0.0 collective-permute-start.12
  31.3 0.0 copy-start.2
  31.3 0.0 copy-start.3
  31.3 2.7 %merge_taps.1 = (bf16[2,768,768]{2,1,0:T(8,128)(2,1)S(1)}, bf16[1152,768]{1,0:T(8,128)(2,1)S(1)}) custom-call(s32[5]{0:T(128)S(1)} %stack.35.place, bf16[3,3,192,384]{3,2,1,0:T(8,128)(2,1)} %bitcast.10, bf16[1152,768]{1,0:T(8,128)(2,1)} %bitcast.9), custom_call_target="tpu_custom_call" | custom-call | flops 3000000000 | bytes 1000 | tf_op jit(solution)/shard_map/merge_taps/pallas_call | solution.py:387
  33.9 0.0 collective-permute-done.8.edges2
  34.0 0.6 %collective-permute-start.9 = (bf16[1,160,384]{2,1,0:T(8,128)(2,1)S(1)}, bf16[1,160,384]{2,1,0:T(8,128)(2,1)S(1)}, u32[]{:S(2)}, u32[]{:S(2)}) collective-permute-start(bf16[1,160,384]{2,1,0:T(8,128)(2,1)S(1)} %collective-permute-done.8.edges2), channel_id=1, source_target_pairs={{0,2},{2,0},{4,6},{6,4},{8,10},{10,8},{12,14},{14,12},{16,18},{18,... | collective-permute-start | bytes 368648 | tf_op jit(solution)/shard_map/ppermute | solution.py:278
  34.5 0.0 collective-permute-done.7.edges
  34.5 0.1 collective-permute-start.10
  34.6 0.0 collective-permute-done.13.main_b
  34.6 0.0 collective-permute-done.12.main_a
  34.6 0.0 copy-done.2
  34.6 0.0 copy-done.3
  34.6 4.0 %time_and_up.1 = (bf16[2,4,192,320]{3,2,1,0:T(8,128)(2,1)}, bf16[2,1,160,384]{3,2,1,0:T(8,128)(2,1)S(1)}) custom-call(s32[5]{0:T(128)S(1)} %stack.35.place, bf16[2,160,384]{2,1,0:T(8,128)(2,1)S(1)} %get-tuple-element.22.own, bf16[2,160,384]{2,1,0:T(8,128)(2,1)S(1)} %collective-permute-done.11.main2, bf16[2,160,384]{2,1,0:T(8,128)(2,1)S(1)} %collective-permute-done.12.main_a, ...), custom_call_target="tpu_custom_call" | custom-call | flops 6000000000 | bytes 1000 | tf_op jit(solution)/shard_map/time_and_up/pallas_call | solution.py:402
  38.6 0.0 collective-permute-done.9.edges_a
  38.6 0.0 collective-permute-done.10.edges_b
  38.6 2.5 %time_and_up_edge.1 = bf16[2,4,192,320]{3,2,1,0:T(8,128)(2,1)} custom-call(s32[5]{0:T(128)S(1)} %stack.35.place, bf16[1,160,384]{2,1,0:T(8,128)(2,1)S(1)} %collective-permute-done.7.edges, bf16[1,160,384]{2,1,0:T(8,128)(2,1)S(1)} %collective-permute-done.8.edges2, ...), custom_call_target="tpu_custom_call", output_to_operand_aliasing={{}: (10, {})} | custom-call | flops 3000000000 | bytes 1000 | tf_op jit(solution)/shard_map/time_and_up_edge/pallas_call | solution.py:408
Async XLA Ops:
  0.0 16.2 %collective-permute-start = (bf16[2,160,384]{2,1,0:T(8,128)(2,1)}, bf16[2,160,384]{2,1,0:T(8,128)(2,1)S(1)}, u32[]{:S(2)}, u32[]{:S(2)}) collective-permute-start(bf16[2,160,384]{2,1,0:T(8,128)(2,1)} %bitcast.5.field.own), channel_id=1, source_target_pairs={{0,4},{2,6},{4,8},{6,10},{8,12},{10,14},{12,16},{14,18},{16,20},{1... | collective-permute-start | bytes 737288 | tf_op jit(solution)/shard_map/ppermute | solution.py:283
  3.0 6.0 %copy-start = (f32[384]{0:T(512)S(1)}, f32[384]{0:T(512)}, u32[]{:S(2)}) copy-start(f32[384]{0:T(512)} %bias.1) | copy-start | bytes 4612
  3.0 6.0 %copy-start.1 = (f32[384]{0:T(512)S(1)}, f32[384]{0:T(512)}, u32[]{:S(2)}) copy-start(f32[384]{0:T(512)} %gain.5) | copy-start | bytes 4612
  4.0 4.9 %collective-permute-start.4 = (bf16[1,160,384]{2,1,0:T(8,128)(2,1)S(1)}, bf16[1,160,384]{2,1,0:T(8,128)(2,1)S(1)}, u32[]{:S(2)}, u32[]{:S(2)}) collective-permute-start(bf16[1,160,384]{2,1,0:T(8,128)(2,1)S(1)} %near_row.1), channel_id=1, source_target_pairs={{0,1},{1,0},{2,3},{3,2},{4,5},{5,4},{6,7},{7,6},{8,9},{9,8},{10,11... | collective-permute-start | bytes 368648 | tf_op jit(solution)/shard_map/ppermute | solution.py:304
  5.6 10.1 %collective-permute-start.3 = (bf16[1,160,384]{2,1,0:T(8,128)(2,1)S(1)}, bf16[1,160,384]{2,1,0:T(8,128)(2,1)S(1)}, u32[]{:S(2)}, u32[]{:S(2)}) collective-permute-start(bf16[1,160,384]{2,1,0:T(8,128)(2,1)S(1)} %near_row.1), channel_id=1, source_target_pairs={{0,5},{1,4},{2,7},{3,6},{4,9},{5,8},{6,11},{7,10},{8,13},{9,12},{1... | collective-permute-start | bytes 368648 | tf_op jit(solution)/shard_map/ppermute | solution.py:297
  7.1 10.1 %collective-permute-start.2 = (bf16[2,160,384]{2,1,0:T(8,128)(2,1)}, bf16[2,160,384]{2,1,0:T(8,128)(2,1)S(1)}, u32[]{:S(2)}, u32[]{:S(2)}) collective-permute-start(bf16[2,160,384]{2,1,0:T(8,128)(2,1)} %bitcast.5.field.own), channel_id=1, source_target_pairs={{0,2},{2,0},{4,6},{6,4},{8,10},{10,8},{12,14},{14,12},{16,18},{18,... | collective-permute-start | bytes 737288 | tf_op jit(solution)/shard_map/ppermute | solution.py:278
  15.7 1.3 %collective-permute-start.5 = (bf16[1,160,384]{2,1,0:T(8,128)(2,1)S(1)}, bf16[1,160,384]{2,1,0:T(8,128)(2,1)S(1)}, u32[]{:S(2)}, u32[]{:S(2)}) collective-permute-start(bf16[1,160,384]{2,1,0:T(8,128)(2,1)S(1)} %collective-permute-done.3.edges2), channel_id=1, source_target_pairs={{0,2},{2,0},{4,6},{6,4},{8,10},{10,8},{12,14},{14,12},{16,18},{18,... | collective-permute-start | bytes 368648 | tf_op jit(solution)/shard_map/ppermute | solution.py:278
  15.7 1.5 %collective-permute-start.6 = (bf16[1,160,384]{2,1,0:T(8,128)(2,1)S(1)}, bf16[1,160,384]{2,1,0:T(8,128)(2,1)S(1)}, u32[]{:S(2)}, u32[]{:S(2)}) collective-permute-start(bf16[1,160,384]{2,1,0:T(8,128)(2,1)S(1)} %collective-permute-done.4.edges), channel_id=1, source_target_pairs={{0,2},{2,0},{4,6},{6,4},{8,10},{10,8},{12,14},{14,12},{16,18},{18,... | collective-permute-start | bytes 368648 | tf_op jit(solution)/shard_map/ppermute | solution.py:278
  16.2 1.5 %collective-permute-start.1 = (bf16[2,160,384]{2,1,0:T(8,128)(2,1)S(1)}, bf16[2,160,384]{2,1,0:T(8,128)(2,1)S(1)}, u32[]{:S(2)}, u32[]{:S(2)}) collective-permute-start(bf16[2,160,384]{2,1,0:T(8,128)(2,1)S(1)} %collective-permute-done.main), channel_id=1, source_target_pairs={{0,2},{2,0},{4,6},{6,4},{8,10},{10,8},{12,14},{14,12},{16,18},{18,... | collective-permute-start | bytes 737288 | tf_op jit(solution)/shard_map/ppermute | solution.py:278
  19.7 11.6 %collective-permute-start.11 = (bf16[2,160,384]{2,1,0:T(8,128)(2,1)S(1)}, bf16[2,160,384]{2,1,0:T(8,128)(2,1)S(1)}, u32[]{:S(2)}, u32[]{:S(2)}) collective-permute-start(bf16[2,160,384]{2,1,0:T(8,128)(2,1)S(1)} %get-tuple-element.22.own), channel_id=1, source_target_pairs={{0,4},{2,6},{4,8},{6,10},{8,12},{10,14},{12,16},{14,18},{16,20},{1... | collective-permute-start | bytes 737288 | tf_op jit(solution)/shard_map/ppermute | solution.py:283
  19.8 14.8 %collective-permute-start.13 = (bf16[2,160,384]{2,1,0:T(8,128)(2,1)S(1)}, bf16[2,160,384]{2,1,0:T(8,128)(2,1)S(1)}, u32[]{:S(2)}, u32[]{:S(2)}) collective-permute-start(bf16[2,160,384]{2,1,0:T(8,128)(2,1)S(1)} %get-tuple-element.22.own), channel_id=1, source_target_pairs={{0,2},{2,0},{4,6},{6,4},{8,10},{10,8},{12,14},{14,12},{16,18},{18,... | collective-permute-start | bytes 737288 | tf_op jit(solution)/shard_map/ppermute | solution.py:278
  20.0 13.9 %collective-permute-start.8 = (bf16[1,160,384]{2,1,0:T(8,128)(2,1)S(1)}, bf16[1,160,384]{2,1,0:T(8,128)(2,1)S(1)}, u32[]{:S(2)}, u32[]{:S(2)}) collective-permute-start(bf16[1,160,384]{2,1,0:T(8,128)(2,1)S(1)} %get-tuple-element.21), channel_id=1, source_target_pairs={{0,5},{1,4},{2,7},{3,6},{4,9},{5,8},{6,11},{7,10},{8,13},{9,12},{1... | collective-permute-start | bytes 368648 | tf_op jit(solution)/shard_map/ppermute | solution.py:297
  21.9 12.7 %collective-permute-start.7 = (bf16[1,160,384]{2,1,0:T(8,128)(2,1)S(1)}, bf16[1,160,384]{2,1,0:T(8,128)(2,1)S(1)}, u32[]{:S(2)}, u32[]{:S(2)}) collective-permute-start(bf16[1,160,384]{2,1,0:T(8,128)(2,1)S(1)} %get-tuple-element.21), channel_id=1, source_target_pairs={{0,1},{1,0},{2,3},{3,2},{4,5},{5,4},{6,7},{7,6},{8,9},{9,8},{10,11... | collective-permute-start | bytes 368648 | tf_op jit(solution)/shard_map/ppermute | solution.py:304
  31.3 3.3 %collective-permute-start.12 = (bf16[2,160,384]{2,1,0:T(8,128)(2,1)S(1)}, bf16[2,160,384]{2,1,0:T(8,128)(2,1)S(1)}, u32[]{:S(2)}, u32[]{:S(2)}) collective-permute-start(bf16[2,160,384]{2,1,0:T(8,128)(2,1)S(1)} %collective-permute-done.11.main2), channel_id=1, source_target_pairs={{0,2},{2,0},{4,6},{6,4},{8,10},{10,8},{12,14},{14,12},{16,18},{18,... | collective-permute-start | bytes 737288 | tf_op jit(solution)/shard_map/ppermute | solution.py:278
  31.3 3.3 %copy-start.2 = (f32[768]{0:T(1024)S(1)}, f32[768]{0:T(1024)}, u32[]{:S(2)}) copy-start(f32[768]{0:T(1024)} %tbias.3) | copy-start | bytes 9220
  31.3 3.3 %copy-start.3 = (f32[192]{0:T(256)S(1)}, f32[192]{0:T(256)}, u32[]{:S(2)}) copy-start(f32[192]{0:T(256)} %ubias.3) | copy-start | bytes 2308
  34.0 4.6 %collective-permute-start.9 = (bf16[1,160,384]{2,1,0:T(8,128)(2,1)S(1)}, bf16[1,160,384]{2,1,0:T(8,128)(2,1)S(1)}, u32[]{:S(2)}, u32[]{:S(2)}) collective-permute-start(bf16[1,160,384]{2,1,0:T(8,128)(2,1)S(1)} %collective-permute-done.8.edges2), channel_id=1, source_target_pairs={{0,2},{2,0},{4,6},{6,4},{8,10},{10,8},{12,14},{14,12},{16,18},{18,... | collective-permute-start | bytes 368648 | tf_op jit(solution)/shard_map/ppermute | solution.py:278
  34.5 4.1 %collective-permute-start.10 = (bf16[1,160,384]{2,1,0:T(8,128)(2,1)S(1)}, bf16[1,160,384]{2,1,0:T(8,128)(2,1)S(1)}, u32[]{:S(2)}, u32[]{:S(2)}) collective-permute-start(bf16[1,160,384]{2,1,0:T(8,128)(2,1)S(1)} %collective-permute-done.7.edges), channel_id=1, source_target_pairs={{0,2},{2,0},{4,6},{6,4},{8,10},{10,8},{12,14},{14,12},{16,18},{18,... | collective-permute-start | bytes 368648 | tf_op jit(solution)/shard_map/ppermute | solution.py:278

commit v4 on v3

v4 whole, which is shorter than its diff:
```python
import functools

import jax
import jax.numpy as jnp
from jax import lax
from jax.experimental import pallas as pl
from jax.experimental.pallas import tpu as pltpu
from jax.sharding import PartitionSpec as P

F32 = jnp.float32
BF16 = jnp.bfloat16
VMEM = pl.BlockSpec(memory_space=pltpu.VMEM)
SMEM = pl.BlockSpec(memory_space=pltpu.SMEM)
ANY = pl.BlockSpec(memory_space=pl.ANY)
HBM = pl.BlockSpec(memory_space=pltpu.HBM)
LANES = 128
SHARE = 3000000000
SPLIT = 1
OWN = 0.2
TWO = 0.2
THREE = 1
MERGE = 0.2
FIRST = 0.01


def in_order(place, index, count):
    return jnp.where(place[0] == 1, count - 1 - index, index)


def activate(rows, gain):
    values = rows.astype(F32)
    meansq = jnp.mean(values * values, axis=-1, keepdims=True)
    scaled = values * lax.rsqrt(meansq + 1e-06) * gain
    return (scaled * jax.nn.sigmoid(scaled)).astype(BF16)


def moved(rows, step):
    cols = rows.shape[0]
    index = lax.broadcasted_iota(jnp.int32, rows.shape, 0)
    edge = 0 if step == 1 else cols - 1
    return jnp.where(index == edge, 0.0, pltpu.roll(rows, step % cols, 0))


def conv_rows(place, halos, rows, sources):
    lead = halos - 1
    sums = []
    for q in range(rows):
        lefts, rights = [], []
        for weight, field in sources:
            for dh in range(3):
                s = lead + q + dh - 1
                if s in field:
                    lefts.append(field[s]())
                    tap = in_order(place, dh, 3)
                    rights.append(jnp.concatenate([weight[tap, dw] for dw in range(3)], axis=-1))
        if not lefts:
            sums.append(None)
            continue
        total = jnp.dot(
            jnp.concatenate(lefts, axis=-1), jnp.concatenate(rights, axis=0), preferred_element_type=F32
        )
        chans = total.shape[1] // 3
        sums.append(
            total[:, chans : 2 * chans]
            + moved(total[:, :chans], 1)
            + moved(total[:, 2 * chans :], -1)
        )
    return sums


def hold(act, slot, value):
    act[slot] = value
    return lambda: act[slot]


def parts_row(halos, rows, near, rest, q):
    if halos == 1:
        return near[0] if q == rows - 1 else rest[q]
    if q in (0, rows - 1):
        return near[0 if q == 0 else 1]
    return rest[q - 1]


def held_rows(halos, rows, row, gain, act):
    return {halos - 1 + q: hold(act, q, activate(row(q), gain)) for q in range(rows)}


def held_edges(halos, rows, edges, gain, act, slot, known=True):
    where = (rows,) if halos == 1 else (0, rows + 1)
    return {
        s: hold(act, slot + h, activate(jnp.where(known, edges[h], jnp.zeros_like(edges[h])), gain))
        for h, s in enumerate(where)
    }


def split_rows(halos, place, field, near, rest):
    rows = field.shape[0]
    if halos == 2:
        near[0] = field[0]
    near[halos - 1] = field[in_order(place, rows - 1, rows)]
    for i in range(rows - halos):
        rest[i] = field[in_order(place, halos - 1 + i, rows)]


def conv_first(halos, place, own, gain, bias, weight, acc, act):
    rows = own.shape[0]
    row = lambda q: own[in_order(place, q, rows)]
    field = held_rows(halos, rows, row, gain[...][None], act)
    for q, part in enumerate(conv_rows(place, halos, rows, [(weight.at[2], field)])):
        acc[q] = part + bias[...][None] + row(q).astype(F32)


def conv_second(halos, place, near2, rest2, before, gain, weight, acc, act):
    rows = before.shape[0]

    @pl.when(place[4] == 0)
    def _():
        acc[...] = before[...]

    @pl.when(place[4] != 0)
    def _():
        row = lambda q: parts_row(halos, rows, near2, rest2, q)
        field = held_rows(halos, rows, row, gain[...][None], act)
        for q, part in enumerate(conv_rows(place, halos, rows, [(weight.at[0], field)])):
            acc[q] = before[q] + part


def one_back(place, even, odd):
    none = jnp.zeros_like(odd)
    return jnp.where(place[3] != 0, odd, jnp.where(place[4] != 0, even, none))


def conv_third(halos, place, even_near, even_rest, odd, before, gain, weight, acc, act):
    rows = before.shape[0]

    def row(q):
        return one_back(place, parts_row(halos, rows, even_near, even_rest, q), odd[in_order(place, q, rows)])

    field = held_rows(halos, rows, row, gain[...][None], act)
    for q, part in enumerate(conv_rows(place, halos, rows, [(weight.at[1], field)])):
        acc[q] = before[q] + part


def conv_edges(halos, place, edges, edges2, even_edges, odd_edges, before, gain, weight, block, near, rest, act):
    rows = block.shape[0]
    sides = [one_back(place, even_edges[h], odd_edges[h]) for h in range(halos)]
    fields = [
        (weight.at[dt], held_edges(halos, rows, field, gain[...][None], act, dt * halos, known))
        for dt, field, known in ((2, edges, True), (1, sides, True), (0, edges2, place[4] != 0))
    ]
    for q, part in enumerate(conv_rows(place, halos, rows, fields)):
        value = (before[q] if part is None else before[q] + part).astype(BF16)
        block[in_order(place, q, rows)] = value
        if q == rows - 1:
            near[halos - 1] = value
        elif q == 0 and halos == 2:
            near[0] = value
        else:
            rest[q - (halos - 1)] = value


def up_rows(place, rows, out_rows, pairs, ubias, uw, wide, outs, out_hbm, osems):
    cols = wide.shape[2] // 2
    rest = ubias.shape[-1] - LANES
    chans = uw.shape[1] // 2
    lane = lax.broadcasted_iota(jnp.int32, (cols, LANES), 1)
    stores = []
    for slot_o, o in enumerate(out_rows):
        phase, taken = pairs[o]
        left = jnp.concatenate([jnp.concatenate([r[f] for r in taken], axis=-1) for f in range(2)], axis=0)
        right = uw[phase, (2 - len(taken)) * chans :, :]
        both = jnp.dot(left, right, preferred_element_type=F32)
        for f in range(2):
            part = both[f * cols : (f + 1) * cols]
            g = [part[:, k * LANES : (k + 1) * LANES] for k in range(6)]
            tail = g[4] + jnp.where(lane < rest, moved(g[5], 1), moved(g[5], -1))
            slot = f
            wide[slot, 0, pl.ds(0, cols, stride=2), :] = g[0] + moved(g[2], 1) + ubias[:LANES][None]
            wide[slot, 0, pl.ds(1, cols, stride=2), :] = g[1] + moved(g[3], -1) + ubias[:LANES][None]
            wide[slot, 1, pl.ds(0, cols, stride=2), :] = tail
            wide[slot, 1, pl.ds(1, cols, stride=2), :] = pltpu.roll(tail, LANES - rest, 1)
            outs[f, slot_o, :LANES, :] = wide[slot, 0].T.astype(BF16)
            outs[f, slot_o, LANES:, :] = (wide[slot, 1, :, :rest] + ubias[LANES:][None]).T.astype(BF16)
            copy = pltpu.make_async_copy(
                outs.at[f, slot_o], out_hbm.at[f, in_order(place, o, 2 * rows)], osems.at[f, slot_o]
            )
            copy.start()
            stores.append(copy)
    return stores


def doubled_rows(lefts, tw, tbias, keep):
    cols = lefts[0].shape[0]
    chans = tw.shape[1] // 2
    mixed = jnp.dot(jnp.concatenate(lefts, axis=0), tw[...], preferred_element_type=F32) + tbias[...][None]
    for i in range(len(lefts)):
        for f in range(2):
            keep(i, f, mixed[i * cols : (i + 1) * cols, f * chans : (f + 1) * chans])


def inside(place, halos, h, value):
    return jnp.where(place[1 + h] == 1, value, 0.0) if halos == 2 else value


def row_pairs(halos, rows, at, out_rows):
    lead = halos - 1
    pairs = {}
    for o in out_rows:
        q, phase = divmod(o, 2)
        sources = [s for s in (lead + q - 1 + phase, lead + q + phase) if s >= 0]
        pairs[o] = phase, [[at(s, f) for f in range(2)] for s in sources]
    return pairs


def inner_rows(halos, rows):
    inner = list(range(0 if halos == 1 else 1, 2 * rows - 1))
    return inner, [o for o in range(2 * rows) if o not in inner]


def first_inner(halos, place, own, odd, tbias, ubias, tw, uw, out_hbm, kept, doubled, wide, outs, osems):
    @pl.when(place[4] == 0)
    def _():
        rows = own.shape[0]
        lead = halos - 1
        lefts = []
        for q in range(rows):
            now, before = own[in_order(place, q, rows)], odd[in_order(place, q, rows)]
            none = jnp.zeros_like(now)
            lefts.append(jnp.concatenate([none, jnp.where(place[3] == 0, none, before), now], axis=-1))

        def keep(q, f, value):
            value = value.astype(BF16)
            doubled[f, q] = value
            if q == rows - 1:
                kept[f, halos - 1] = value
            elif q == 0 and halos == 2:
                kept[f, 0] = value

        doubled_rows(lefts, tw, tbias, keep)
        out_rows = inner_rows(halos, rows)[0]
        pairs = row_pairs(halos, rows, lambda s, f: doubled[f, s - lead], out_rows)
        for copy in up_rows(place, rows, out_rows, pairs, ubias, uw, wide, outs, out_hbm, osems):
            copy.wait()


def first_edges(halos, place, edges, odd_edges, kept, tbias, ubias, tw, uw, out_so_far,
                out_hbm, token, doubled, wide, outs, osems):
    del out_so_far
    token[...] = jnp.zeros_like(token)

    @pl.when(place[4] == 0)
    def _():
        rows = out_hbm.shape[1] // 2
        lead = halos - 1
        lefts = []
        for h in range(halos):
            none = jnp.zeros_like(edges[h])
            lefts.append(jnp.concatenate([none, jnp.where(place[3] == 0, none, odd_edges[h]), edges[h]], axis=-1))

        def keep(h, f, value):
            doubled[f, h] = inside(place, halos, h, value).astype(BF16)

        doubled_rows(lefts, tw, tbias, keep)

        def at(s, f):
            if lead <= s < lead + rows:
                return kept[f, 0 if s == lead and halos == 2 else halos - 1]
            return doubled[f, 0 if s < lead else halos - 1]

        out_rows = inner_rows(halos, rows)[1]
        pairs = row_pairs(halos, rows, at, out_rows)
        for copy in up_rows(place, rows, out_rows, pairs, ubias, uw, wide, outs, out_hbm, osems):
            copy.wait()


def up_kernel(halos, place, own, near2, rest2, even_near, even_rest, odd, edges, edges2, even_edges, odd_edges,
              tbias, ubias, tw, uw, token, out_so_far, out_hbm, doubled, wide, outs, osems):
    del token, out_so_far

    @pl.when(place[4] != 0)
    def _():
        rows = own.shape[0]
        lead = halos - 1
        lefts = []
        for s in range(rows + halos):
            if lead <= s < lead + rows:
                q = s - lead
                now, mine = own[in_order(place, q, rows)], odd[in_order(place, q, rows)]
                theirs = parts_row(halos, rows, even_near, even_rest, q)
                first = parts_row(halos, rows, near2, rest2, q)
            else:
                h = 0 if s < lead else halos - 1
                now, mine, theirs, first = edges[h], odd_edges[h], even_edges[h], edges2[h]
            lefts.append(jnp.concatenate([first, jnp.where(place[3] == 0, theirs, mine), now], axis=-1))

        def keep(s, f, value):
            if not lead <= s < lead + rows:
                value = inside(place, halos, 0 if s < lead else halos - 1, value)
            doubled[f, s] = value.astype(BF16)

        doubled_rows(lefts, tw, tbias, keep)
        out_rows = range(2 * rows)
        pairs = row_pairs(halos, rows, lambda s, f: doubled[f, s], out_rows)
        for copy in up_rows(place, rows, out_rows, pairs, ubias, uw, wide, outs, out_hbm, osems):
            copy.wait()


def merge_kernel(place, taps, merged):
    chans = taps.shape[3]

    def tap(dh, dw):
        return taps[in_order(place, dh, 3), dw].astype(F32)

    for phase, sets in enumerate((((0,), (1, 2)), ((0, 1), (2,)))):
        for which, rows in enumerate(sets):
            cols = [sum(tap(dh, dw) for dh in rows) for dw in range(3)]
            groups = (cols[1] + cols[2], cols[0] + cols[1], cols[0], cols[2])
            wide = jnp.concatenate([g[:LANES] for g in groups] + [g[LANES:] for g in groups], axis=0)
            merged[phase, which * chans : (which + 1) * chans, :] = wide.T.astype(BF16)


def in_hbm(array):
    return pltpu.with_memory_space_constraint(array, pltpu.HBM)


def together(*arrays):
    return lax.optimization_barrier(arrays)


def in_chip(array):
    return lax.ppermute(array, "tm", [(i, i ^ 1) for i in range(lax.axis_size("tm"))])


def two_back(array):
    frames = lax.axis_size("tm")
    return lax.ppermute(array, "tm", [(i, (i + 2) % frames) for i in range(frames)])


def beside(near):
    tiles = lax.axis_size("tile")
    if tiles == 2:
        return lax.ppermute(near, "tile", [(0, 1), (1, 0)])
    return jnp.concatenate(
        [
            lax.ppermute(near[1:], "tile", [(j, j + 1) for j in range(tiles - 1)]),
            lax.ppermute(near[:1], "tile", [(j + 1, j) for j in range(tiles - 1)]),
        ]
    )


def local(latent, gain, conv_weight, conv_bias, time_weight, time_bias, up_weight, up_bias):
    tiles = lax.axis_size("tile")
    tile = lax.axis_index("tile")
    frame_at = lax.axis_index("tm")
    halos = 1 if tiles == 2 else 2
    main = latent[0]
    rows, cols, chans = main.shape
    outs_n = up_weight.shape[3]
    flip = tile if halos == 1 else 0 * tile
    place = jnp.stack([flip, tile > 0, tile < tiles - 1, frame_at % 2, frame_at >= 2]).astype(jnp.int32)

    def call(kernel, name, share, ins, outs, scratch, **rest):
        return pl.pallas_call(
            kernel,
            out_shape=tuple(s for s, _ in outs),
            in_specs=[SMEM] + ins,
            out_specs=tuple(s for _, s in outs),
            scratch_shapes=scratch,
            compiler_params=pltpu.CompilerParams(vmem_limit_bytes=20 << 20),
            cost_estimate=pl.CostEstimate(
                flops=int(SHARE * share), bytes_accessed=1000, transcendentals=0
            ),
            name=name,
            **rest,
        )

    field = (rows, cols, chans)
    sides = (halos, cols, chans)

    def conv(kernel, name, share, count):
        step = call(
            functools.partial(kernel, halos), name, share,
            [VMEM] * count,
            [(pltpu.VMEM(field, F32), VMEM)],
            [pltpu.VMEM(field, BF16)],
        )
        return lambda *arrays: step(*arrays)[0]

    taps_t = up_weight.transpose(0, 1, 3, 2)
    merge = call(
        merge_kernel, "merge_taps", MERGE,
        [VMEM],
        [(pltpu.VMEM((2, 2 * chans, 4 * outs_n), BF16), VMEM)],
        [],
    )
    near_rest = [
        (jax.ShapeDtypeStruct(sides, BF16), VMEM),
        (jax.ShapeDtypeStruct((max(rows - halos, 1), cols, chans), BF16), VMEM),
    ]
    if rows == halos:
        other = lambda near, rest, move: near
    else:
        other = lambda near, rest, move: move(rest)

    near, rest = call(functools.partial(split_rows, halos), "split_rows", SPLIT, [VMEM], near_rest, [])(place, main)
    near2 = two_back(near)
    edges = beside(near)
    odd = in_chip(main)
    rest2 = other(near2, rest, two_back)
    edges2 = beside(near2)
    even_near = in_chip(near2)
    acc = conv(conv_first, "conv_own_frame", OWN, 4)(place, main, gain, conv_bias, conv_weight)
    rest2, acc = together(rest2, acc)
    even_rest = other(even_near, rest2, in_chip)
    odd_edges = in_chip(edges)
    acc = conv(conv_second, "conv_two_back", TWO, 5)(place, near2, rest2, acc, gain, conv_weight)
    edges2, acc = together(edges2, acc)
    even_edges = in_chip(edges2)
    acc = conv(conv_third, "conv_one_back", THREE, 6)(place, even_near, even_rest, odd, acc, gain, conv_weight)
    block, near, rest = call(
        functools.partial(conv_edges, halos), "conv_edge_rows", 1,
        [VMEM] * 7,
        [(jax.ShapeDtypeStruct(field, BF16), VMEM)] + near_rest,
        [pltpu.VMEM((3 * halos, cols, chans), BF16)],
    )(place, edges, edges2, even_edges, odd_edges, acc, gain, conv_weight)

    near2 = two_back(near)
    edges = beside(near)
    odd = in_chip(block)
    taps_t, main = together(taps_t, block)
    (merged,) = merge(place, taps_t)
    tw = time_weight.reshape(3 * chans, 2 * chans)
    out_shape = (jax.ShapeDtypeStruct((2, 2 * rows, outs_n, 2 * cols), BF16), ANY)

    def scratch(count, held):
        return [
            pltpu.VMEM((2, held, cols, chans), BF16),
            pltpu.VMEM((2, 2, 2 * cols, LANES), F32),
            pltpu.VMEM((2, count, outs_n, 2 * cols), BF16),
            pltpu.SemaphoreType.DMA((2, count)),
        ]

    rest, merged = together(rest, merged)
    rest2 = other(near2, rest, two_back)
    common = (time_bias, up_bias, tw, merged)
    inner, outer = (len(o) for o in inner_rows(halos, rows))
    out, kept = call(
        functools.partial(first_inner, halos), "first_chip_inner_rows", FIRST,
        [VMEM] * 6,
        [out_shape, (pltpu.VMEM((2,) + sides, BF16), VMEM)],
        scratch(inner, rows),
    )(place, main, odd, *common)
    near2, kept = together(near2, kept)
    edges2 = beside(near2)
    even_near = in_chip(near2)
    odd_edges = in_chip(edges)
    out, token = call(
        functools.partial(first_edges, halos), "first_chip_edge_rows", FIRST,
        [VMEM] * 7 + [ANY],
        [out_shape, (jax.ShapeDtypeStruct((8, LANES), F32), VMEM)],
        scratch(outer, halos),
        input_output_aliases={8: 0},
    )(place, edges, odd_edges, kept, *common, out)
    rest2, token = together(rest2, token)
    even_rest = other(even_near, rest2, in_chip)
    even_edges = in_chip(edges2)
    (out,) = call(
        functools.partial(up_kernel, halos), "time_and_up", 1,
        [VMEM] * 14 + [ANY] * 2,
        [out_shape],
        scratch(2 * rows, rows + halos),
        input_output_aliases={16: 0},
    )(place, main, near2, rest2, even_near, even_rest, odd, edges, edges2, even_edges, odd_edges,
      *common, token, out)
    return out.transpose(0, 1, 3, 2)


def solution(mesh):
    placed = (P("tm", "tile", None, None), P(), P(), P(), P(), P(), P(), P())
    return jax.shard_map(
        local, mesh=mesh, in_specs=placed, out_specs=P("tm", "tile", None, None), check_vma=False
    )
```

time: 41.3 us -> 37.5 us (0.908)
  waiting for transfers between devices: 13.7 us -> 9.13 us
  starting transfers between devices: 10.1 us -> 13 us
  Pallas kernels: 17.1 us -> 14.9 us
    ppermute x2 -> x4, waiting for transfers between devices: 8.59 us -> 5.07 us  [two_back(): lax.ppermute(array, 'tm', [(i, (i + 2) % frames) for i in range(frames)])]
    ppermute x2 -> x4, starting transfers between devices: 3 us -> 5.83 us  [two_back(): lax.ppermute(array, 'tm', [(i, (i + 2) % frames) for i in range(frames)])]
    pallas_call x7 -> x9, Pallas kernels: 17.1 us -> 14.9 us  [the longest x3 4.02 us: conv(): return lambda *arrays: step(*arrays)[0]]
    ppermute x4, waiting for transfers between devices: 4.16 us -> 2.72 us  [beside(): return lax.ppermute(near, 'tile', [(0, 1), (1, 0)])]
    ppermute x8 -> x10, starting transfers between devices: 1.41 us -> 1.92 us  [in_chip(): lax.ppermute(array, 'tm', [(i, i ^ 1) for i in range(lax.axis_size('tm'))])]
    ppermute x4, starting transfers between devices: 5.74 us -> 5.26 us  [beside(): return lax.ppermute(near, 'tile', [(0, 1), (1, 0)])]
    ppermute x8 -> x10, waiting for transfers between devices: 0.93 us -> 1.35 us  [in_chip(): lax.ppermute(array, 'tm', [(i, i ^ 1) for i in range(lax.axis_size('tm'))])]
  transfers between devices with their start and end apart: 14 -> 18, of which waited for: 6 -> 5; matrix products, arithmetic and copies ran while one was open for 0% -> 0% of each run, Pallas kernels for 31% -> 31%
where the time goes in v4:
time: 37.5 us; the launch traced here: 37.3 us
  Pallas kernels  14.9 us (40%)
  starting transfers between devices  13 us (35%)
  waiting for transfers between devices  9.13 us (24%)
    ppermute x4, starting transfers between devices, two_back(): lax.ppermute(array, 'tm', [(i, (i + 2) % frames) for i in range(frames)])  5.83 us
    ppermute x4, starting transfers between devices, beside(): return lax.ppermute(near, 'tile', [(0, 1), (1, 0)])  5.26 us
    ppermute x4, waiting for transfers between devices, two_back(): lax.ppermute(array, 'tm', [(i, (i + 2) % frames) for i in range(frames)])  5.07 us
    pallas_call x3, Pallas kernels, conv(): return lambda *arrays: step(*arrays)[0]  4.02 us
    pallas_call x1, Pallas kernels, local(): call(functools.partial(first_inner, halos), 'first_chip_inner_rows', FIRS...  3.87 us
    ppermute x4, waiting for transfers between devices, beside(): return lax.ppermute(near, 'tile', [(0, 1), (1, 0)])  2.72 us
    pallas_call x1, Pallas kernels, local(): call(functools.partial(first_edges, halos), 'first_chip_edge_rows', FIRST...  2.49 us
    ppermute x10, starting transfers between devices, in_chip(): lax.ppermute(array, 'tm', [(i, i ^ 1) for i in range(lax.axis_size('tm'))])  1.92 us
  transfers between devices with their start and end apart: 18, of which 5 were waited for; matrix products, arithmetic and copies ran while one was open for 0% of the time, Pallas kernels for 31%

profile of v4, /device:TPU:0, one launch (start us, length us, event | category | flops | bytes accessed | tf_op | source)
XLA Modules:
  0.0 37.3 jit_solution(10776624389748935995)
XLA Ops:
  0.0 0.1 stack.35.place
  0.1 0.0 copy-start
  0.1 0.0 copy-start.4
  0.1 0.0 copy-start.6
  0.1 1.1 %split_rows.1 = (bf16[1,160,384]{2,1,0:T(8,128)(2,1)S(1)}, bf16[1,160,384]{2,1,0:T(8,128)(2,1)S(1)}) custom-call(s32[5]{0:T(128)S(1)} %stack.35.place, bf16[2,160,384]{2,1,0:T(8,128)(2,1)} %bitcast.6.field.own), custom_call_target="tpu_custom_call" | custom-call | flops 3000000000 | bytes 1000 | tf_op jit(solution)/shard_map/split_rows/pallas_call | solution.py:405
  1.2 3.0 %collective-permute-start.1 = (bf16[1,160,384]{2,1,0:T(8,128)(2,1)S(1)}, bf16[1,160,384]{2,1,0:T(8,128)(2,1)S(1)}, u32[]{:S(2)}, u32[]{:S(2)}) collective-permute-start(bf16[1,160,384]{2,1,0:T(8,128)(2,1)S(1)} %get-tuple-element.26), channel_id=1, source_target_pairs={{0,4},{2,6},{4,8},{6,10},{8,12},{10,14},{12,16},{14,18},{16,20},{1... | collective-permute-start | bytes 368648 | tf_op jit(solution)/shard_map/ppermute | solution.py:336
  4.2 1.5 %collective-permute-start.3 = (bf16[1,160,384]{2,1,0:T(8,128)(2,1)S(1)}, bf16[1,160,384]{2,1,0:T(8,128)(2,1)S(1)}, u32[]{:S(2)}, u32[]{:S(2)}) collective-permute-start(bf16[1,160,384]{2,1,0:T(8,128)(2,1)S(1)} %get-tuple-element.27), channel_id=1, source_target_pairs={{0,4},{2,6},{4,8},{6,10},{8,12},{10,14},{12,16},{14,18},{16,20},{1... | collective-permute-start | bytes 368648 | tf_op jit(solution)/shard_map/ppermute | solution.py:336
  5.8 0.0 collective-permute-start.8
  5.8 1.5 %collective-permute-start = (bf16[1,160,384]{2,1,0:T(8,128)(2,1)S(1)}, bf16[1,160,384]{2,1,0:T(8,128)(2,1)S(1)}, u32[]{:S(2)}, u32[]{:S(2)}) collective-permute-start(bf16[1,160,384]{2,1,0:T(8,128)(2,1)S(1)} %get-tuple-element.26), channel_id=1, source_target_pairs={{0,1},{1,0},{2,3},{3,2},{4,5},{5,4},{6,7},{7,6},{8,9},{9,8},{10,11... | collective-permute-start | bytes 368648 | tf_op jit(solution)/shard_map/ppermute | solution.py:342
  7.3 4.1 %collective-permute-done.1.near2 = bf16[1,160,384]{2,1,0:T(8,128)(2,1)S(1)} collective-permute-done((bf16[1,160,384]{2,1,0:T(8,128)(2,1)S(1)}, bf16[1,160,384]{2,1,0:T(8,128)(2,1)S(1)}, u32[]{:S(2)}, u32[]{:S(2)}) %collective-permute-start.1) | collective-permute-done | bytes 122912 | tf_op jit(solution)/shard_map/ppermute | solution.py:336
  11.4 1.7 %collective-permute-start.2 = (bf16[1,160,384]{2,1,0:T(8,128)(2,1)S(1)}, bf16[1,160,384]{2,1,0:T(8,128)(2,1)S(1)}, u32[]{:S(2)}, u32[]{:S(2)}) collective-permute-start(bf16[1,160,384]{2,1,0:T(8,128)(2,1)S(1)} %collective-permute-done.1.near2), channel_id=1, source_target_pairs={{0,1},{1,0},{2,3},{3,2},{4,5},{5,4},{6,7},{7,6},{8,9},{9,8},{10,11... | collective-permute-start | bytes 368648 | tf_op jit(solution)/shard_map/ppermute | solution.py:342
  13.1 0.0 copy-done
  13.2 0.0 copy-done.4
  13.2 0.0 copy-done.6
  13.2 1.9 %conv_own_frame.1.before = f32[2,160,384]{2,1,0:T(8,128)S(1)} custom-call(s32[5]{0:T(128)S(1)} %stack.35.place, bf16[2,160,384]{2,1,0:T(8,128)(2,1)} %bitcast.6.field.own, f32[384]{0:T(512)S(1)} %copy-done.4, f32[384]{0:T(512)S(1)} %copy-done.6, bf16[3,3,3,384,384]{4,3,2,1,0:T(8,128)(2,1)S(1)} %copy-done), custom_call_target="tpu_custom_call" | custom-call | flops 600000000 | bytes 1000 | tf_op jit(solution)/shard_map/conv_own_frame/pallas_call | solution.py:387
  15.1 0.0 collective-permute-done.3.rest2
  15.1 0.1 collective-permute-start.6
  15.2 0.5 %collective-permute-start.7 = (bf16[1,160,384]{2,1,0:T(8,128)(2,1)S(1)}, bf16[1,160,384]{2,1,0:T(8,128)(2,1)S(1)}, u32[]{:S(2)}, u32[]{:S(2)}) collective-permute-start(bf16[1,160,384]{2,1,0:T(8,128)(2,1)S(1)} %collective-permute-done.3.rest2), channel_id=1, source_target_pairs={{0,2},{2,0},{4,6},{6,4},{8,10},{10,8},{12,14},{14,12},{16,18},{18,... | collective-permute-start | bytes 368648 | tf_op jit(solution)/shard_map/ppermute | solution.py:331
  15.7 0.0 collective-permute-done.edges
  15.7 0.1 collective-permute-start.5
  15.8 0.6 %conv_two_back.1.before = f32[2,160,384]{2,1,0:T(8,128)S(1)} custom-call(s32[5]{0:T(128)S(1)} %stack.35.place, bf16[1,160,384]{2,1,0:T(8,128)(2,1)S(1)} %collective-permute-done.1.near2, bf16[1,160,384]{2,1,0:T(8,128)(2,1)S(1)} %collective-permute-done.3.rest2, f32[2,160,384]{2,1,0:T(8,128)S(1)} %conv_own_frame.1.before, f32[384]{0:T(512)S(1)} %copy-done.4, ...), custom_call_target="tpu_custom_call" | custom-call | flops 600000000 | bytes 1000 | tf_op jit(solution)/shard_map/conv_two_back/pallas_call | solution.py:387
  16.3 0.0 collective-permute-done.2.edges2
  16.4 0.5 %collective-permute-start.4 = (bf16[1,160,384]{2,1,0:T(8,128)(2,1)S(1)}, bf16[1,160,384]{2,1,0:T(8,128)(2,1)S(1)}, u32[]{:S(2)}, u32[]{:S(2)}) collective-permute-start(bf16[1,160,384]{2,1,0:T(8,128)(2,1)S(1)} %collective-permute-done.2.edges2), channel_id=1, source_target_pairs={{0,2},{2,0},{4,6},{6,4},{8,10},{10,8},{12,14},{14,12},{16,18},{18,... | collective-permute-start | bytes 368648 | tf_op jit(solution)/shard_map/ppermute | solution.py:331
  16.9 0.0 collective-permute-done.6.even_near
  16.9 0.0 collective-permute-done.8.odd
  16.9 0.0 collective-permute-done.7.even_rest
  16.9 1.5 %conv_one_back.1.before = f32[2,160,384]{2,1,0:T(8,128)S(1)} custom-call(s32[5]{0:T(128)S(1)} %stack.35.place, bf16[1,160,384]{2,1,0:T(8,128)(2,1)S(1)} %collective-permute-done.6.even_near, bf16[1,160,384]{2,1,0:T(8,128)(2,1)S(1)} %collective-permute-done.7.even_rest, bf16[2,160,384]{2,1,0:T(8,128)(2,1)S(1)} %collective-permute-done.8.odd, ...), custom_call_target="tpu_custom_call" | custom-call | flops 3000000000 | bytes 1000 | tf_op jit(solution)/shard_map/conv_one_back/pallas_call | solution.py:387
  18.4 0.0 copy-start.2
  18.4 0.0 collective-permute-done.5.odd_edges
  18.4 0.0 collective-permute-done.4.even_edges
  18.4 1.4 %conv_edge_rows.1 = (bf16[2,160,384]{2,1,0:T(8,128)(2,1)S(1)}, bf16[1,160,384]{2,1,0:T(8,128)(2,1)S(1)}, bf16[1,160,384]{2,1,0:T(8,128)(2,1)S(1)}) custom-call(s32[5]{0:T(128)S(1)} %stack.35.place, bf16[1,160,384]{2,1,0:T(8,128)(2,1)S(1)} %collective-permute-done.edges, bf16[1,160,384]{2,1,0:T(8,128)(2,1)S(1)} %collective-permute-done.2.edges2, ...), custom_call_target="tpu_custom_call" | custom-call | flops 3000000000 | bytes 1000 | tf_op jit(solution)/shard_map/conv_edge_rows/pallas_call | solution.py:420
  19.8 0.2 collective-permute-start.10
  20.0 1.5 %collective-permute-start.12 = (bf16[1,160,384]{2,1,0:T(8,128)(2,1)S(1)}, bf16[1,160,384]{2,1,0:T(8,128)(2,1)S(1)}, u32[]{:S(2)}, u32[]{:S(2)}) collective-permute-start(bf16[1,160,384]{2,1,0:T(8,128)(2,1)S(1)} %get-tuple-element.34), channel_id=1, source_target_pairs={{0,1},{1,0},{2,3},{3,2},{4,5},{5,4},{6,7},{7,6},{8,9},{9,8},{10,11... | collective-permute-start | bytes 368648 | tf_op jit(solution)/shard_map/ppermute | solution.py:342
  21.6 0.0 collective-permute-start.9
  21.6 0.0 copy-done.2
  21.6 0.0 copy-start.1
  21.6 0.0 copy-start.3
  21.6 0.0 copy-start.5
  21.6 1.4 %merge_taps.1.uw = bf16[2,768,768]{2,1,0:T(8,128)(2,1)S(1)} custom-call(s32[5]{0:T(128)S(1)} %stack.35.place, bf16[3,3,192,384]{3,2,1,0:T(8,128)(2,1)S(1)} %bitcast.12), custom_call_target="tpu_custom_call" | custom-call | flops 600000000 | bytes 1000 | tf_op jit(solution)/shard_map/merge_taps/pallas_call | solution.py:431
  23.0 1.3 %collective-permute-start.11 = (bf16[1,160,384]{2,1,0:T(8,128)(2,1)S(1)}, bf16[1,160,384]{2,1,0:T(8,128)(2,1)S(1)}, u32[]{:S(2)}, u32[]{:S(2)}) collective-permute-start(bf16[1,160,384]{2,1,0:T(8,128)(2,1)S(1)} %get-tuple-element.40), channel_id=1, source_target_pairs={{0,4},{2,6},{4,8},{6,10},{8,12},{10,14},{12,16},{14,18},{16,20},{1... | collective-permute-start | bytes 368648 | tf_op jit(solution)/shard_map/ppermute | solution.py:336
  24.3 1.4 %collective-permute-done.12.edges = bf16[1,160,384]{2,1,0:T(8,128)(2,1)S(1)} collective-permute-done((bf16[1,160,384]{2,1,0:T(8,128)(2,1)S(1)}, bf16[1,160,384]{2,1,0:T(8,128)(2,1)S(1)}, u32[]{:S(2)}, u32[]{:S(2)}) %collective-permute-start.12) | collective-permute-done | bytes 122912 | tf_op jit(solution)/shard_map/ppermute | solution.py:342
  25.6 0.0 collective-permute-start.13
  25.6 0.0 collective-permute-done.10.odd
  25.6 0.0 copy-done.1
  25.6 0.0 copy-done.3
  25.7 0.0 copy-done.5
  25.7 3.9 %first_chip_inner_rows.1 = (bf16[2,4,192,320]{3,2,1,0:T(8,128)(2,1)}, bf16[2,1,160,384]{3,2,1,0:T(8,128)(2,1)S(1)}) custom-call(s32[5]{0:T(128)S(1)} %stack.35.place, bf16[2,160,384]{2,1,0:T(8,128)(2,1)S(1)} %get-tuple-element.33.own, bf16[2,160,384]{2,1,0:T(8,128)(2,1)S(1)} %collective-permute-done.10.odd, f32[768]{0:T(1024)S(1)} %copy-done.3, ...), custom_call_target="tpu_custom_call" | custom-call | flops 30000000 | bytes 1000 | tf_op jit(solution)/shard_map/first_chip_inner_rows/pallas_call | solution.py:447
  29.5 0.9 %collective-permute-done.9.near2 = bf16[1,160,384]{2,1,0:T(8,128)(2,1)S(1)} collective-permute-done((bf16[1,160,384]{2,1,0:T(8,128)(2,1)S(1)}, bf16[1,160,384]{2,1,0:T(8,128)(2,1)S(1)}, u32[]{:S(2)}, u32[]{:S(2)}) %collective-permute-start.9) | collective-permute-done | bytes 122912 | tf_op jit(solution)/shard_map/ppermute | solution.py:336
  30.5 0.5 %collective-permute-start.16 = (bf16[1,160,384]{2,1,0:T(8,128)(2,1)S(1)}, bf16[1,160,384]{2,1,0:T(8,128)(2,1)S(1)}, u32[]{:S(2)}, u32[]{:S(2)}) collective-permute-start(bf16[1,160,384]{2,1,0:T(8,128)(2,1)S(1)} %collective-permute-done.9.near2), channel_id=1, source_target_pairs={{0,1},{1,0},{2,3},{3,2},{4,5},{5,4},{6,7},{7,6},{8,9},{9,8},{10,11... | collective-permute-start | bytes 368648 | tf_op jit(solution)/shard_map/ppermute | solution.py:342
  30.9 0.2 collective-permute-start.14
  31.1 0.0 collective-permute-done.13.odd_edges
  31.1 2.5 %first_chip_edge_rows.1 = (bf16[2,4,192,320]{3,2,1,0:T(8,128)(2,1)}, f32[8,128]{1,0:T(8,128)S(1)}) custom-call(s32[5]{0:T(128)S(1)} %stack.35.place, bf16[1,160,384]{2,1,0:T(8,128)(2,1)S(1)} %collective-permute-done.12.edges, bf16[1,160,384]{2,1,0:T(8,128)(2,1)S(1)} %collective-permute-done.13.odd_edges, ...), custom_call_target="tpu_custom_call", output_to_operand_aliasing={{0}: (8, {})} | custom-call | flops 30000000 | bytes 1000 | tf_op jit(solution)/shard_map/first_chip_edge_rows/pallas_call | solution.py:457
  33.6 0.0 collective-permute-done.11.rest2
  33.6 0.4 %collective-permute-start.15 = (bf16[1,160,384]{2,1,0:T(8,128)(2,1)S(1)}, bf16[1,160,384]{2,1,0:T(8,128)(2,1)S(1)}, u32[]{:S(2)}, u32[]{:S(2)}) collective-permute-start(bf16[1,160,384]{2,1,0:T(8,128)(2,1)S(1)} %collective-permute-done.11.rest2), channel_id=1, source_target_pairs={{0,2},{2,0},{4,6},{6,4},{8,10},{10,8},{12,14},{14,12},{16,18},{18,... | collective-permute-start | bytes 368648 | tf_op jit(solution)/shard_map/ppermute | solution.py:331
  34.0 1.3 %collective-permute-done.16.edges2 = bf16[1,160,384]{2,1,0:T(8,128)(2,1)S(1)} collective-permute-done((bf16[1,160,384]{2,1,0:T(8,128)(2,1)S(1)}, bf16[1,160,384]{2,1,0:T(8,128)(2,1)S(1)}, u32[]{:S(2)}, u32[]{:S(2)}) %collective-permute-start.16) | collective-permute-done | bytes 122912 | tf_op jit(solution)/shard_map/ppermute | solution.py:342
  35.4 0.0 collective-permute-start.17
  35.4 0.0 collective-permute-done.15.even_rest
  35.4 0.0 collective-permute-done.14.even_near
  35.4 1.3 %collective-permute-done.17.even_edges = bf16[1,160,384]{2,1,0:T(8,128)(2,1)S(1)} collective-permute-done((bf16[1,160,384]{2,1,0:T(8,128)(2,1)S(1)}, bf16[1,160,384]{2,1,0:T(8,128)(2,1)S(1)}, u32[]{:S(2)}, u32[]{:S(2)}) %collective-permute-start.17) | collective-permute-done | bytes 122912 | tf_op jit(solution)/shard_map/ppermute | solution.py:331
  36.7 0.6 %time_and_up.1 = bf16[2,4,192,320]{3,2,1,0:T(8,128)(2,1)} custom-call(s32[5]{0:T(128)S(1)} %stack.35.place, bf16[2,160,384]{2,1,0:T(8,128)(2,1)S(1)} %get-tuple-element.33.own, bf16[1,160,384]{2,1,0:T(8,128)(2,1)S(1)} %collective-permute-done.9.near2, bf16[1,160,384]{2,1,0:T(8,128)(2,1)S(1)} %collective-permute-done.11.rest2, ...), custom_call_target="tpu_custom_call", output_to_operand_aliasing={{}: (16, {})} | custom-call | flops 3000000000 | bytes 1000 | tf_op jit(solution)/shard_map/time_and_up/pallas_call | solution.py:467
Async XLA Ops:
  0.1 13.1 %copy-start = (bf16[3,3,3,384,384]{4,3,2,1,0:T(8,128)(2,1)S(1)}, bf16[3,3,3,384,384]{4,3,2,1,0:T(8,128)(2,1)}, u32[]{:S(2)}) copy-start(bf16[3,3,3,384,384]{4,3,2,1,0:T(8,128)(2,1)} %weight.7) | copy-start | bytes 23887876
  0.1 13.1 %copy-start.4 = (f32[384]{0:T(512)S(1)}, f32[384]{0:T(512)}, u32[]{:S(2)}) copy-start(f32[384]{0:T(512)} %gain.7) | copy-start | bytes 4612
  0.1 13.1 %copy-start.6 = (f32[384]{0:T(512)S(1)}, f32[384]{0:T(512)}, u32[]{:S(2)}) copy-start(f32[384]{0:T(512)} %bias.1) | copy-start | bytes 4612
  1.2 10.2 %collective-permute-start.1 = (bf16[1,160,384]{2,1,0:T(8,128)(2,1)S(1)}, bf16[1,160,384]{2,1,0:T(8,128)(2,1)S(1)}, u32[]{:S(2)}, u32[]{:S(2)}) collective-permute-start(bf16[1,160,384]{2,1,0:T(8,128)(2,1)S(1)} %get-tuple-element.26), channel_id=1, source_target_pairs={{0,4},{2,6},{4,8},{6,10},{8,12},{10,14},{12,16},{14,18},{16,20},{1... | collective-permute-start | bytes 368648 | tf_op jit(solution)/shard_map/ppermute | solution.py:336
  4.2 10.9 %collective-permute-start.3 = (bf16[1,160,384]{2,1,0:T(8,128)(2,1)S(1)}, bf16[1,160,384]{2,1,0:T(8,128)(2,1)S(1)}, u32[]{:S(2)}, u32[]{:S(2)}) collective-permute-start(bf16[1,160,384]{2,1,0:T(8,128)(2,1)S(1)} %get-tuple-element.27), channel_id=1, source_target_pairs={{0,4},{2,6},{4,8},{6,10},{8,12},{10,14},{12,16},{14,18},{16,20},{1... | collective-permute-start | bytes 368648 | tf_op jit(solution)/shard_map/ppermute | solution.py:336
  5.8 11.1 %collective-permute-start.8 = (bf16[2,160,384]{2,1,0:T(8,128)(2,1)}, bf16[2,160,384]{2,1,0:T(8,128)(2,1)S(1)}, u32[]{:S(2)}, u32[]{:S(2)}) collective-permute-start(bf16[2,160,384]{2,1,0:T(8,128)(2,1)} %bitcast.6.field.own), channel_id=1, source_target_pairs={{0,2},{2,0},{4,6},{6,4},{8,10},{10,8},{12,14},{14,12},{16,18},{18,... | collective-permute-start | bytes 737288 | tf_op jit(solution)/shard_map/ppermute | solution.py:331
  5.8 9.9 %collective-permute-start = (bf16[1,160,384]{2,1,0:T(8,128)(2,1)S(1)}, bf16[1,160,384]{2,1,0:T(8,128)(2,1)S(1)}, u32[]{:S(2)}, u32[]{:S(2)}) collective-permute-start(bf16[1,160,384]{2,1,0:T(8,128)(2,1)S(1)} %get-tuple-element.26), channel_id=1, source_target_pairs={{0,1},{1,0},{2,3},{3,2},{4,5},{5,4},{6,7},{7,6},{8,9},{9,8},{10,11... | collective-permute-start | bytes 368648 | tf_op jit(solution)/shard_map/ppermute | solution.py:342
  11.4 4.9 %collective-permute-start.2 = (bf16[1,160,384]{2,1,0:T(8,128)(2,1)S(1)}, bf16[1,160,384]{2,1,0:T(8,128)(2,1)S(1)}, u32[]{:S(2)}, u32[]{:S(2)}) collective-permute-start(bf16[1,160,384]{2,1,0:T(8,128)(2,1)S(1)} %collective-permute-done.1.near2), channel_id=1, source_target_pairs={{0,1},{1,0},{2,3},{3,2},{4,5},{5,4},{6,7},{7,6},{8,9},{9,8},{10,11... | collective-permute-start | bytes 368648 | tf_op jit(solution)/shard_map/ppermute | solution.py:342
  15.1 1.8 %collective-permute-start.6 = (bf16[1,160,384]{2,1,0:T(8,128)(2,1)S(1)}, bf16[1,160,384]{2,1,0:T(8,128)(2,1)S(1)}, u32[]{:S(2)}, u32[]{:S(2)}) collective-permute-start(bf16[1,160,384]{2,1,0:T(8,128)(2,1)S(1)} %collective-permute-done.1.near2), channel_id=1, source_target_pairs={{0,2},{2,0},{4,6},{6,4},{8,10},{10,8},{12,14},{14,12},{16,18},{18,... | collective-permute-start | bytes 368648 | tf_op jit(solution)/shard_map/ppermute | solution.py:331
  15.2 1.7 %collective-permute-start.7 = (bf16[1,160,384]{2,1,0:T(8,128)(2,1)S(1)}, bf16[1,160,384]{2,1,0:T(8,128)(2,1)S(1)}, u32[]{:S(2)}, u32[]{:S(2)}) collective-permute-start(bf16[1,160,384]{2,1,0:T(8,128)(2,1)S(1)} %collective-permute-done.3.rest2), channel_id=1, source_target_pairs={{0,2},{2,0},{4,6},{6,4},{8,10},{10,8},{12,14},{14,12},{16,18},{18,... | collective-permute-start | bytes 368648 | tf_op jit(solution)/shard_map/ppermute | solution.py:331
  15.7 2.7 %collective-permute-start.5 = (bf16[1,160,384]{2,1,0:T(8,128)(2,1)S(1)}, bf16[1,160,384]{2,1,0:T(8,128)(2,1)S(1)}, u32[]{:S(2)}, u32[]{:S(2)}) collective-permute-start(bf16[1,160,384]{2,1,0:T(8,128)(2,1)S(1)} %collective-permute-done.edges), channel_id=1, source_target_pairs={{0,2},{2,0},{4,6},{6,4},{8,10},{10,8},{12,14},{14,12},{16,18},{18,... | collective-permute-start | bytes 368648 | tf_op jit(solution)/shard_map/ppermute | solution.py:331
  16.4 2.1 %collective-permute-start.4 = (bf16[1,160,384]{2,1,0:T(8,128)(2,1)S(1)}, bf16[1,160,384]{2,1,0:T(8,128)(2,1)S(1)}, u32[]{:S(2)}, u32[]{:S(2)}) collective-permute-start(bf16[1,160,384]{2,1,0:T(8,128)(2,1)S(1)} %collective-permute-done.2.edges2), channel_id=1, source_target_pairs={{0,2},{2,0},{4,6},{6,4},{8,10},{10,8},{12,14},{14,12},{16,18},{18,... | collective-permute-start | bytes 368648 | tf_op jit(solution)/shard_map/ppermute | solution.py:331
  18.4 3.2 %copy-start.2 = (bf16[3,3,384,192]{2,3,1,0:T(8,128)(2,1)S(1)}, bf16[3,3,384,192]{2,3,1,0:T(8,128)(2,1)}, u32[]{:S(2)}) copy-start(bf16[3,3,384,192]{2,3,1,0:T(8,128)(2,1)} %param.14) | copy-start | bytes 3981316
  19.8 5.8 %collective-permute-start.10 = (bf16[2,160,384]{2,1,0:T(8,128)(2,1)S(1)}, bf16[2,160,384]{2,1,0:T(8,128)(2,1)S(1)}, u32[]{:S(2)}, u32[]{:S(2)}) collective-permute-start(bf16[2,160,384]{2,1,0:T(8,128)(2,1)S(1)} %get-tuple-element.33.own), channel_id=1, source_target_pairs={{0,2},{2,0},{4,6},{6,4},{8,10},{10,8},{12,14},{14,12},{16,18},{18,... | collective-permute-start | bytes 737288 | tf_op jit(solution)/shard_map/ppermute | solution.py:331
  20.0 5.6 %collective-permute-start.12 = (bf16[1,160,384]{2,1,0:T(8,128)(2,1)S(1)}, bf16[1,160,384]{2,1,0:T(8,128)(2,1)S(1)}, u32[]{:S(2)}, u32[]{:S(2)}) collective-permute-start(bf16[1,160,384]{2,1,0:T(8,128)(2,1)S(1)} %get-tuple-element.34), channel_id=1, source_target_pairs={{0,1},{1,0},{2,3},{3,2},{4,5},{5,4},{6,7},{7,6},{8,9},{9,8},{10,11... | collective-permute-start | bytes 368648 | tf_op jit(solution)/shard_map/ppermute | solution.py:342
  21.6 8.9 %collective-permute-start.9 = (bf16[1,160,384]{2,1,0:T(8,128)(2,1)S(1)}, bf16[1,160,384]{2,1,0:T(8,128)(2,1)S(1)}, u32[]{:S(2)}, u32[]{:S(2)}) collective-permute-start(bf16[1,160,384]{2,1,0:T(8,128)(2,1)S(1)} %get-tuple-element.34), channel_id=1, source_target_pairs={{0,4},{2,6},{4,8},{6,10},{8,12},{10,14},{12,16},{14,18},{16,20},{1... | collective-permute-start | bytes 368648 | tf_op jit(solution)/shard_map/ppermute | solution.py:336
  21.6 4.1 %copy-start.1 = (bf16[3,384,768]{2,1,0:T(8,128)(2,1)S(1)}, bf16[3,384,768]{2,1,0:T(8,128)(2,1)}, u32[]{:S(2)}) copy-start(bf16[3,384,768]{2,1,0:T(8,128)(2,1)} %param.12) | copy-start | bytes 5308420
  21.6 4.1 %copy-start.3 = (f32[768]{0:T(1024)S(1)}, f32[768]{0:T(1024)}, u32[]{:S(2)}) copy-start(f32[768]{0:T(1024)} %tbias.5) | copy-start | bytes 9220
  21.6 4.1 %copy-start.5 = (f32[192]{0:T(256)S(1)}, f32[192]{0:T(256)}, u32[]{:S(2)}) copy-start(f32[192]{0:T(256)} %ubias.5) | copy-start | bytes 2308
  23.0 10.6 %collective-permute-start.11 = (bf16[1,160,384]{2,1,0:T(8,128)(2,1)S(1)}, bf16[1,160,384]{2,1,0:T(8,128)(2,1)S(1)}, u32[]{:S(2)}, u32[]{:S(2)}) collective-permute-start(bf16[1,160,384]{2,1,0:T(8,128)(2,1)S(1)} %get-tuple-element.40), channel_id=1, source_target_pairs={{0,4},{2,6},{4,8},{6,10},{8,12},{10,14},{12,16},{14,18},{16,20},{1... | collective-permute-start | bytes 368648 | tf_op jit(solution)/shard_map/ppermute | solution.py:336
  25.6 5.5 %collective-permute-start.13 = (bf16[1,160,384]{2,1,0:T(8,128)(2,1)S(1)}, bf16[1,160,384]{2,1,0:T(8,128)(2,1)S(1)}, u32[]{:S(2)}, u32[]{:S(2)}) collective-permute-start(bf16[1,160,384]{2,1,0:T(8,128)(2,1)S(1)} %collective-permute-done.12.edges), channel_id=1, source_target_pairs={{0,2},{2,0},{4,6},{6,4},{8,10},{10,8},{12,14},{14,12},{16,18},{18,... | collective-permute-start | bytes 368648 | tf_op jit(solution)/shard_map/ppermute | solution.py:331
  30.5 4.9 %collective-permute-start.16 = (bf16[1,160,384]{2,1,0:T(8,128)(2,1)S(1)}, bf16[1,160,384]{2,1,0:T(8,128)(2,1)S(1)}, u32[]{:S(2)}, u32[]{:S(2)}) collective-permute-start(bf16[1,160,384]{2,1,0:T(8,128)(2,1)S(1)} %collective-permute-done.9.near2), channel_id=1, source_target_pairs={{0,1},{1,0},{2,3},{3,2},{4,5},{5,4},{6,7},{7,6},{8,9},{9,8},{10,11... | collective-permute-start | bytes 368648 | tf_op jit(solution)/shard_map/ppermute | solution.py:342
  30.9 4.4 %collective-permute-start.14 = (bf16[1,160,384]{2,1,0:T(8,128)(2,1)S(1)}, bf16[1,160,384]{2,1,0:T(8,128)(2,1)S(1)}, u32[]{:S(2)}, u32[]{:S(2)}) collective-permute-start(bf16[1,160,384]{2,1,0:T(8,128)(2,1)S(1)} %collective-permute-done.9.near2), channel_id=1, source_target_pairs={{0,2},{2,0},{4,6},{6,4},{8,10},{10,8},{12,14},{14,12},{16,18},{18,... | collective-permute-start | bytes 368648 | tf_op jit(solution)/shard_map/ppermute | solution.py:331
  33.6 1.8 %collective-permute-start.15 = (bf16[1,160,384]{2,1,0:T(8,128)(2,1)S(1)}, bf16[1,160,384]{2,1,0:T(8,128)(2,1)S(1)}, u32[]{:S(2)}, u32[]{:S(2)}) collective-permute-start(bf16[1,160,384]{2,1,0:T(8,128)(2,1)S(1)} %collective-permute-done.11.rest2), channel_id=1, source_target_pairs={{0,2},{2,0},{4,6},{6,4},{8,10},{10,8},{12,14},{14,12},{16,18},{18,... | collective-permute-start | bytes 368648 | tf_op jit(solution)/shard_map/ppermute | solution.py:331
  35.4 1.3 %collective-permute-start.17 = (bf16[1,160,384]{2,1,0:T(8,128)(2,1)S(1)}, bf16[1,160,384]{2,1,0:T(8,128)(2,1)S(1)}, u32[]{:S(2)}, u32[]{:S(2)}) collective-permute-start(bf16[1,160,384]{2,1,0:T(8,128)(2,1)S(1)} %collective-permute-done.16.edges2), channel_id=1, source_target_pairs={{0,2},{2,0},{4,6},{6,4},{8,10},{10,8},{12,14},{14,12},{16,18},{18,... | collective-permute-start | bytes 368648 | tf_op jit(solution)/shard_map/ppermute | solution.py:331

commit v5 on v4

--- a/solution.py
+++ b/solution.py
@@ -407,10 +407,10 @@
     edges = beside(near)
     odd = in_chip(main)
     rest2 = other(near2, rest, two_back)
+    acc = conv(conv_first, "conv_own_frame", OWN, 4)(place, main, gain, conv_bias, conv_weight)
+    near2, edges, acc = together(near2, edges, acc)
     edges2 = beside(near2)
     even_near = in_chip(near2)
-    acc = conv(conv_first, "conv_own_frame", OWN, 4)(place, main, gain, conv_bias, conv_weight)
-    rest2, acc = together(rest2, acc)
     even_rest = other(even_near, rest2, in_chip)
     odd_edges = in_chip(edges)
     acc = conv(conv_second, "conv_two_back", TWO, 5)(place, near2, rest2, acc, gain, conv_weight)
@@ -452,8 +452,10 @@
     )(place, main, odd, *common)
     near2, kept = together(near2, kept)
     edges2 = beside(near2)
+    edges, near2, rest2 = together(edges, near2, rest2)
     even_near = in_chip(near2)
     odd_edges = in_chip(edges)
+    even_rest = other(even_near, rest2, in_chip)
     out, token = call(
         functools.partial(first_edges, halos), "first_chip_edge_rows", FIRST,
         [VMEM] * 7 + [ANY],
@@ -461,8 +463,6 @@
         scratch(outer, halos),
         input_output_aliases={8: 0},
     )(place, edges, odd_edges, kept, *common, out)
-    rest2, token = together(rest2, token)
-    even_rest = other(even_near, rest2, in_chip)
     even_edges = in_chip(edges2)
     (out,) = call(
         functools.partial(up_kernel, halos), "time_and_up", 1,

time: 37.5 us -> 36.7 us (0.979)
  waiting for transfers between devices: 9.13 us -> 5.67 us
  starting transfers between devices: 13 us -> 15.6 us
    ppermute x4, waiting for transfers between devices: 5.07 us -> 2.06 us  [two_back(): lax.ppermute(array, 'tm', [(i, (i + 2) % frames) for i in range(frames)])]
    ppermute x4, starting transfers between devices: 5.26 us -> 7.67 us  [beside(): return lax.ppermute(near, 'tile', [(0, 1), (1, 0)])]
    ppermute x10, waiting for transfers between devices: 1.35 us -> 0.03 us  [in_chip(): lax.ppermute(array, 'tm', [(i, i ^ 1) for i in range(lax.axis_size('tm'))])]
    ppermute x4, waiting for transfers between devices: 2.72 us -> 3.58 us  [beside(): return lax.ppermute(near, 'tile', [(0, 1), (1, 0)])]
    ppermute x4, starting transfers between devices: 5.83 us -> 6.37 us  [two_back(): lax.ppermute(array, 'tm', [(i, (i + 2) % frames) for i in range(frames)])]
  transfers between devices with their start and end apart: 18 -> 18, of which waited for: 5 -> 5; matrix products, arithmetic and copies ran while one was open for 0% -> 0% of each run, Pallas kernels for 31% -> 32%
where the time goes in v5:
time: 36.7 us; the launch traced here: 36.5 us
  starting transfers between devices  15.6 us (43%)
  Pallas kernels  14.9 us (41%)
  waiting for transfers between devices  5.67 us (15%)
    ppermute x4, starting transfers between devices, beside(): return lax.ppermute(near, 'tile', [(0, 1), (1, 0)])  7.67 us
    ppermute x4, starting transfers between devices, two_back(): lax.ppermute(array, 'tm', [(i, (i + 2) % frames) for i in range(frames)])  6.37 us
    pallas_call x3, Pallas kernels, conv(): return lambda *arrays: step(*arrays)[0]  4.02 us
    pallas_call x1, Pallas kernels, local(): call(functools.partial(first_inner, halos), 'first_chip_inner_rows', FIRS...  3.87 us
    ppermute x4, waiting for transfers between devices, beside(): return lax.ppermute(near, 'tile', [(0, 1), (1, 0)])  3.58 us
    pallas_call x1, Pallas kernels, local(): call(functools.partial(first_edges, halos), 'first_chip_edge_rows', FIRST...  2.49 us
    ppermute x4, waiting for transfers between devices, two_back(): lax.ppermute(array, 'tm', [(i, (i + 2) % frames) for i in range(frames)])  2.06 us
    ppermute x10, starting transfers between devices, in_chip(): lax.ppermute(array, 'tm', [(i, i ^ 1) for i in range(lax.axis_size('tm'))])  1.59 us
  transfers between devices with their start and end apart: 18, of which 5 were waited for; matrix products, arithmetic and copies ran while one was open for 0% of the time, Pallas kernels for 32%

profile of v5, /device:TPU:0, one launch (start us, length us, event | category | flops | bytes accessed | tf_op | source)
XLA Modules:
  0.0 36.5 jit_solution(14083219265448110455)
XLA Ops:
  0.0 0.1 stack.35.place
  0.1 0.0 copy-start
  0.1 0.0 copy-start.4
  0.1 0.0 copy-start.6
  0.1 1.1 %split_rows.1 = (bf16[1,160,384]{2,1,0:T(8,128)(2,1)S(1)}, bf16[1,160,384]{2,1,0:T(8,128)(2,1)S(1)}) custom-call(s32[5]{0:T(128)S(1)} %stack.35.place, bf16[2,160,384]{2,1,0:T(8,128)(2,1)} %bitcast.6.field.own), custom_call_target="tpu_custom_call" | custom-call | flops 3000000000 | bytes 1000 | tf_op jit(solution)/shard_map/split_rows/pallas_call | solution.py:405
  1.2 3.0 %collective-permute-start = (bf16[1,160,384]{2,1,0:T(8,128)(2,1)S(1)}, bf16[1,160,384]{2,1,0:T(8,128)(2,1)S(1)}, u32[]{:S(2)}, u32[]{:S(2)}) collective-permute-start(bf16[1,160,384]{2,1,0:T(8,128)(2,1)S(1)} %get-tuple-element.28), channel_id=1, source_target_pairs={{0,4},{2,6},{4,8},{6,10},{8,12},{10,14},{12,16},{14,18},{16,20},{1... | collective-permute-start | bytes 368648 | tf_op jit(solution)/shard_map/ppermute | solution.py:336
  4.2 1.5 %collective-permute-start.1 = (bf16[1,160,384]{2,1,0:T(8,128)(2,1)S(1)}, bf16[1,160,384]{2,1,0:T(8,128)(2,1)S(1)}, u32[]{:S(2)}, u32[]{:S(2)}) collective-permute-start(bf16[1,160,384]{2,1,0:T(8,128)(2,1)S(1)} %get-tuple-element.28), channel_id=1, source_target_pairs={{0,1},{1,0},{2,3},{3,2},{4,5},{5,4},{6,7},{7,6},{8,9},{9,8},{10,11... | collective-permute-start | bytes 368648 | tf_op jit(solution)/shard_map/ppermute | solution.py:342
  5.7 1.5 %collective-permute-start.3 = (bf16[1,160,384]{2,1,0:T(8,128)(2,1)S(1)}, bf16[1,160,384]{2,1,0:T(8,128)(2,1)S(1)}, u32[]{:S(2)}, u32[]{:S(2)}) collective-permute-start(bf16[1,160,384]{2,1,0:T(8,128)(2,1)S(1)} %get-tuple-element.31), channel_id=1, source_target_pairs={{0,4},{2,6},{4,8},{6,10},{8,12},{10,14},{12,16},{14,18},{16,20},{1... | collective-permute-start | bytes 368648 | tf_op jit(solution)/shard_map/ppermute | solution.py:336
  7.3 0.0 collective-permute-start.8
  7.3 0.0 copy-done
  7.3 0.0 copy-done.4
  7.3 0.0 copy-done.6
  7.3 1.9 %conv_own_frame.1.before = f32[2,160,384]{2,1,0:T(8,128)S(1)} custom-call(s32[5]{0:T(128)S(1)} %stack.35.place, bf16[2,160,384]{2,1,0:T(8,128)(2,1)} %bitcast.6.field.own, f32[384]{0:T(512)S(1)} %copy-done.4, f32[384]{0:T(512)S(1)} %copy-done.6, bf16[3,3,3,384,384]{4,3,2,1,0:T(8,128)(2,1)S(1)} %copy-done), custom_call_target="tpu_custom_call" | custom-call | flops 600000000 | bytes 1000 | tf_op jit(solution)/shard_map/conv_own_frame/pallas_call | solution.py:387
  9.2 1.5 %collective-permute-done.near2 = bf16[1,160,384]{2,1,0:T(8,128)(2,1)S(1)} collective-permute-done((bf16[1,160,384]{2,1,0:T(8,128)(2,1)S(1)}, bf16[1,160,384]{2,1,0:T(8,128)(2,1)S(1)}, u32[]{:S(2)}, u32[]{:S(2)}) %collective-permute-start) | collective-permute-done | bytes 122912 | tf_op jit(solution)/shard_map/ppermute | solution.py:336
  10.8 0.0 collective-permute-done.1.edges
  10.8 2.4 %collective-permute-start.2 = (bf16[1,160,384]{2,1,0:T(8,128)(2,1)S(1)}, bf16[1,160,384]{2,1,0:T(8,128)(2,1)S(1)}, u32[]{:S(2)}, u32[]{:S(2)}) collective-permute-start(bf16[1,160,384]{2,1,0:T(8,128)(2,1)S(1)} %collective-permute-done.near2), channel_id=1, source_target_pairs={{0,1},{1,0},{2,3},{3,2},{4,5},{5,4},{6,7},{7,6},{8,9},{9,8},{10,11... | collective-permute-start | bytes 368648 | tf_op jit(solution)/shard_map/ppermute | solution.py:342
  13.2 0.0 collective-permute-start.6
  13.2 0.2 collective-permute-done.3.rest2
  13.3 0.3 collective-permute-start.7
  13.7 0.2 collective-permute-start.5
  13.8 0.6 %conv_two_back.1.before = f32[2,160,384]{2,1,0:T(8,128)S(1)} custom-call(s32[5]{0:T(128)S(1)} %stack.35.place, bf16[1,160,384]{2,1,0:T(8,128)(2,1)S(1)} %collective-permute-done.near2, bf16[1,160,384]{2,1,0:T(8,128)(2,1)S(1)} %collective-permute-done.3.rest2, f32[2,160,384]{2,1,0:T(8,128)S(1)} %conv_own_frame.1.before, f32[384]{0:T(512)S(1)} %copy-done.4, ...), custom_call_target="tpu_custom_call" | custom-call | flops 600000000 | bytes 1000 | tf_op jit(solution)/shard_map/conv_two_back/pallas_call | solution.py:387
  14.4 1.6 %collective-permute-done.2.edges2 = bf16[1,160,384]{2,1,0:T(8,128)(2,1)S(1)} collective-permute-done((bf16[1,160,384]{2,1,0:T(8,128)(2,1)S(1)}, bf16[1,160,384]{2,1,0:T(8,128)(2,1)S(1)}, u32[]{:S(2)}, u32[]{:S(2)}) %collective-permute-start.2) | collective-permute-done | bytes 122912 | tf_op jit(solution)/shard_map/ppermute | solution.py:342
  16.0 0.0 collective-permute-start.4
  16.0 0.0 collective-permute-done.6.even_near
  16.0 0.0 collective-permute-done.7.even_rest
  16.0 0.0 collective-permute-done.8.odd
  16.0 1.5 %conv_one_back.1.before = f32[2,160,384]{2,1,0:T(8,128)S(1)} custom-call(s32[5]{0:T(128)S(1)} %stack.35.place, bf16[1,160,384]{2,1,0:T(8,128)(2,1)S(1)} %collective-permute-done.6.even_near, bf16[1,160,384]{2,1,0:T(8,128)(2,1)S(1)} %collective-permute-done.7.even_rest, bf16[2,160,384]{2,1,0:T(8,128)(2,1)S(1)} %collective-permute-done.8.odd, ...), custom_call_target="tpu_custom_call" | custom-call | flops 3000000000 | bytes 1000 | tf_op jit(solution)/shard_map/conv_one_back/pallas_call | solution.py:387
  17.6 0.0 copy-start.2
  17.6 0.0 collective-permute-done.5.odd_edges
  17.6 0.0 collective-permute-done.4.even_edges
  17.6 1.4 %conv_edge_rows.1 = (bf16[2,160,384]{2,1,0:T(8,128)(2,1)S(1)}, bf16[1,160,384]{2,1,0:T(8,128)(2,1)S(1)}, bf16[1,160,384]{2,1,0:T(8,128)(2,1)S(1)}) custom-call(s32[5]{0:T(128)S(1)} %stack.35.place, bf16[1,160,384]{2,1,0:T(8,128)(2,1)S(1)} %collective-permute-done.1.edges, bf16[1,160,384]{2,1,0:T(8,128)(2,1)S(1)} %collective-permute-done.2.edges2, ...), custom_call_target="tpu_custom_call" | custom-call | flops 3000000000 | bytes 1000 | tf_op jit(solution)/shard_map/conv_edge_rows/pallas_call | solution.py:420
  19.0 0.6 %collective-permute-start.11 = (bf16[2,160,384]{2,1,0:T(8,128)(2,1)S(1)}, bf16[2,160,384]{2,1,0:T(8,128)(2,1)S(1)}, u32[]{:S(2)}, u32[]{:S(2)}) collective-permute-start(bf16[2,160,384]{2,1,0:T(8,128)(2,1)S(1)} %get-tuple-element.36.own), channel_id=1, source_target_pairs={{0,2},{2,0},{4,6},{6,4},{8,10},{10,8},{12,14},{14,12},{16,18},{18,... | collective-permute-start | bytes 737288 | tf_op jit(solution)/shard_map/ppermute | solution.py:331
  19.6 0.5 %collective-permute-start.10 = (bf16[1,160,384]{2,1,0:T(8,128)(2,1)S(1)}, bf16[1,160,384]{2,1,0:T(8,128)(2,1)S(1)}, u32[]{:S(2)}, u32[]{:S(2)}) collective-permute-start(bf16[1,160,384]{2,1,0:T(8,128)(2,1)S(1)} %get-tuple-element.37), channel_id=1, source_target_pairs={{0,4},{2,6},{4,8},{6,10},{8,12},{10,14},{12,16},{14,18},{16,20},{1... | collective-permute-start | bytes 368648 | tf_op jit(solution)/shard_map/ppermute | solution.py:336
  20.1 1.5 %collective-permute-start.9 = (bf16[1,160,384]{2,1,0:T(8,128)(2,1)S(1)}, bf16[1,160,384]{2,1,0:T(8,128)(2,1)S(1)}, u32[]{:S(2)}, u32[]{:S(2)}) collective-permute-start(bf16[1,160,384]{2,1,0:T(8,128)(2,1)S(1)} %get-tuple-element.37), channel_id=1, source_target_pairs={{0,1},{1,0},{2,3},{3,2},{4,5},{5,4},{6,7},{7,6},{8,9},{9,8},{10,11... | collective-permute-start | bytes 368648 | tf_op jit(solution)/shard_map/ppermute | solution.py:342
  21.6 0.0 copy-done.2
  21.6 0.0 copy-start.1
  21.6 0.0 copy-start.3
  21.6 0.0 copy-start.5
  21.6 1.4 %merge_taps.1.uw = bf16[2,768,768]{2,1,0:T(8,128)(2,1)S(1)} custom-call(s32[5]{0:T(128)S(1)} %stack.35.place, bf16[3,3,192,384]{3,2,1,0:T(8,128)(2,1)S(1)} %bitcast.12), custom_call_target="tpu_custom_call" | custom-call | flops 600000000 | bytes 1000 | tf_op jit(solution)/shard_map/merge_taps/pallas_call | solution.py:431
  23.0 1.3 %collective-permute-start.12 = (bf16[1,160,384]{2,1,0:T(8,128)(2,1)S(1)}, bf16[1,160,384]{2,1,0:T(8,128)(2,1)S(1)}, u32[]{:S(2)}, u32[]{:S(2)}) collective-permute-start(bf16[1,160,384]{2,1,0:T(8,128)(2,1)S(1)} %get-tuple-element.43), channel_id=1, source_target_pairs={{0,4},{2,6},{4,8},{6,10},{8,12},{10,14},{12,16},{14,18},{16,20},{1... | collective-permute-start | bytes 368648 | tf_op jit(solution)/shard_map/ppermute | solution.py:336
  24.3 0.0 collective-permute-done.11.odd
  24.3 0.0 copy-done.1
  24.3 0.0 copy-done.3
  24.3 0.0 copy-done.5
  24.3 3.9 %first_chip_inner_rows.1 = (bf16[2,4,192,320]{3,2,1,0:T(8,128)(2,1)}, bf16[2,1,160,384]{3,2,1,0:T(8,128)(2,1)S(1)}) custom-call(s32[5]{0:T(128)S(1)} %stack.35.place, bf16[2,160,384]{2,1,0:T(8,128)(2,1)S(1)} %get-tuple-element.36.own, bf16[2,160,384]{2,1,0:T(8,128)(2,1)S(1)} %collective-permute-done.11.odd, f32[768]{0:T(1024)S(1)} %copy-done.3, ...), custom_call_target="tpu_custom_call" | custom-call | flops 30000000 | bytes 1000 | tf_op jit(solution)/shard_map/first_chip_inner_rows/pallas_call | solution.py:447
  28.2 0.0 collective-permute-done.10.near2
  28.2 2.3 %collective-permute-start.15 = (bf16[1,160,384]{2,1,0:T(8,128)(2,1)S(1)}, bf16[1,160,384]{2,1,0:T(8,128)(2,1)S(1)}, u32[]{:S(2)}, u32[]{:S(2)}) collective-permute-start(bf16[1,160,384]{2,1,0:T(8,128)(2,1)S(1)} %collective-permute-done.10.near2), channel_id=1, source_target_pairs={{0,1},{1,0},{2,3},{3,2},{4,5},{5,4},{6,7},{7,6},{8,9},{9,8},{10,11... | collective-permute-start | bytes 368648 | tf_op jit(solution)/shard_map/ppermute | solution.py:342
  30.5 0.3 collective-permute-done.12.rest2
  30.8 0.0 collective-permute-done.9.edges
  30.8 0.0 collective-permute-start.17
  30.8 0.5 %collective-permute-start.13 = (bf16[1,160,384]{2,1,0:T(8,128)(2,1)S(1)}, bf16[1,160,384]{2,1,0:T(8,128)(2,1)S(1)}, u32[]{:S(2)}, u32[]{:S(2)}) collective-permute-start(bf16[1,160,384]{2,1,0:T(8,128)(2,1)S(1)} %collective-permute-done.10.near2), channel_id=1, source_target_pairs={{0,2},{2,0},{4,6},{6,4},{8,10},{10,8},{12,14},{14,12},{16,18},{18,... | collective-permute-start | bytes 368648 | tf_op jit(solution)/shard_map/ppermute | solution.py:331
  31.3 0.0 collective-permute-start.14
  31.3 2.0 %collective-permute-done.15.edges2 = bf16[1,160,384]{2,1,0:T(8,128)(2,1)S(1)} collective-permute-done((bf16[1,160,384]{2,1,0:T(8,128)(2,1)S(1)}, bf16[1,160,384]{2,1,0:T(8,128)(2,1)S(1)}, u32[]{:S(2)}, u32[]{:S(2)}) %collective-permute-start.15) | collective-permute-done | bytes 122912 | tf_op jit(solution)/shard_map/ppermute | solution.py:342
  33.3 0.0 collective-permute-start.16
  33.3 0.0 collective-permute-done.17.odd_edges
  33.3 2.5 %first_chip_edge_rows.1 = (bf16[2,4,192,320]{3,2,1,0:T(8,128)(2,1)}, f32[8,128]{1,0:T(8,128)S(1)}) custom-call(s32[5]{0:T(128)S(1)} %stack.35.place, bf16[1,160,384]{2,1,0:T(8,128)(2,1)S(1)} %collective-permute-done.9.edges, bf16[1,160,384]{2,1,0:T(8,128)(2,1)S(1)} %collective-permute-done.17.odd_edges, ...), custom_call_target="tpu_custom_call", output_to_operand_aliasing={{0}: (8, {})} | custom-call | flops 30000000 | bytes 1000 | tf_op jit(solution)/shard_map/first_chip_edge_rows/pallas_call | solution.py:459
  35.8 0.0 collective-permute-done.13.even_near
  35.8 0.0 collective-permute-done.14.even_rest
  35.8 0.0 collective-permute-done.16.even_edges
  35.8 0.6 %time_and_up.1 = bf16[2,4,192,320]{3,2,1,0:T(8,128)(2,1)} custom-call(s32[5]{0:T(128)S(1)} %stack.35.place, bf16[2,160,384]{2,1,0:T(8,128)(2,1)S(1)} %get-tuple-element.36.own, bf16[1,160,384]{2,1,0:T(8,128)(2,1)S(1)} %collective-permute-done.10.near2, bf16[1,160,384]{2,1,0:T(8,128)(2,1)S(1)} %collective-permute-done.12.rest2, ...), custom_call_target="tpu_custom_call", output_to_operand_aliasing={{}: (16, {})} | custom-call | flops 3000000000 | bytes 1000 | tf_op jit(solution)/shard_map/time_and_up/pallas_call | solution.py:467
Async XLA Ops:
  0.1 7.2 %copy-start = (bf16[3,3,3,384,384]{4,3,2,1,0:T(8,128)(2,1)S(1)}, bf16[3,3,3,384,384]{4,3,2,1,0:T(8,128)(2,1)}, u32[]{:S(2)}) copy-start(bf16[3,3,3,384,384]{4,3,2,1,0:T(8,128)(2,1)} %weight.7) | copy-start | bytes 23887876
  0.1 7.2 %copy-start.4 = (f32[384]{0:T(512)S(1)}, f32[384]{0:T(512)}, u32[]{:S(2)}) copy-start(f32[384]{0:T(512)} %gain.7) | copy-start | bytes 4612
  0.1 7.2 %copy-start.6 = (f32[384]{0:T(512)S(1)}, f32[384]{0:T(512)}, u32[]{:S(2)}) copy-start(f32[384]{0:T(512)} %bias.1) | copy-start | bytes 4612
  1.2 9.6 %collective-permute-start = (bf16[1,160,384]{2,1,0:T(8,128)(2,1)S(1)}, bf16[1,160,384]{2,1,0:T(8,128)(2,1)S(1)}, u32[]{:S(2)}, u32[]{:S(2)}) collective-permute-start(bf16[1,160,384]{2,1,0:T(8,128)(2,1)S(1)} %get-tuple-element.28), channel_id=1, source_target_pairs={{0,4},{2,6},{4,8},{6,10},{8,12},{10,14},{12,16},{14,18},{16,20},{1... | collective-permute-start | bytes 368648 | tf_op jit(solution)/shard_map/ppermute | solution.py:336
  4.2 6.6 %collective-permute-start.1 = (bf16[1,160,384]{2,1,0:T(8,128)(2,1)S(1)}, bf16[1,160,384]{2,1,0:T(8,128)(2,1)S(1)}, u32[]{:S(2)}, u32[]{:S(2)}) collective-permute-start(bf16[1,160,384]{2,1,0:T(8,128)(2,1)S(1)} %get-tuple-element.28), channel_id=1, source_target_pairs={{0,1},{1,0},{2,3},{3,2},{4,5},{5,4},{6,7},{7,6},{8,9},{9,8},{10,11... | collective-permute-start | bytes 368648 | tf_op jit(solution)/shard_map/ppermute | solution.py:342
  5.7 7.6 %collective-permute-start.3 = (bf16[1,160,384]{2,1,0:T(8,128)(2,1)S(1)}, bf16[1,160,384]{2,1,0:T(8,128)(2,1)S(1)}, u32[]{:S(2)}, u32[]{:S(2)}) collective-permute-start(bf16[1,160,384]{2,1,0:T(8,128)(2,1)S(1)} %get-tuple-element.31), channel_id=1, source_target_pairs={{0,4},{2,6},{4,8},{6,10},{8,12},{10,14},{12,16},{14,18},{16,20},{1... | collective-permute-start | bytes 368648 | tf_op jit(solution)/shard_map/ppermute | solution.py:336
  7.3 8.7 %collective-permute-start.8 = (bf16[2,160,384]{2,1,0:T(8,128)(2,1)}, bf16[2,160,384]{2,1,0:T(8,128)(2,1)S(1)}, u32[]{:S(2)}, u32[]{:S(2)}) collective-permute-start(bf16[2,160,384]{2,1,0:T(8,128)(2,1)} %bitcast.6.field.own), channel_id=1, source_target_pairs={{0,2},{2,0},{4,6},{6,4},{8,10},{10,8},{12,14},{14,12},{16,18},{18,... | collective-permute-start | bytes 737288 | tf_op jit(solution)/shard_map/ppermute | solution.py:331
  10.8 5.2 %collective-permute-start.2 = (bf16[1,160,384]{2,1,0:T(8,128)(2,1)S(1)}, bf16[1,160,384]{2,1,0:T(8,128)(2,1)S(1)}, u32[]{:S(2)}, u32[]{:S(2)}) collective-permute-start(bf16[1,160,384]{2,1,0:T(8,128)(2,1)S(1)} %collective-permute-done.near2), channel_id=1, source_target_pairs={{0,1},{1,0},{2,3},{3,2},{4,5},{5,4},{6,7},{7,6},{8,9},{9,8},{10,11... | collective-permute-start | bytes 368648 | tf_op jit(solution)/shard_map/ppermute | solution.py:342
  13.2 2.9 %collective-permute-start.6 = (bf16[1,160,384]{2,1,0:T(8,128)(2,1)S(1)}, bf16[1,160,384]{2,1,0:T(8,128)(2,1)S(1)}, u32[]{:S(2)}, u32[]{:S(2)}) collective-permute-start(bf16[1,160,384]{2,1,0:T(8,128)(2,1)S(1)} %collective-permute-done.near2), channel_id=1, source_target_pairs={{0,2},{2,0},{4,6},{6,4},{8,10},{10,8},{12,14},{14,12},{16,18},{18,... | collective-permute-start | bytes 368648 | tf_op jit(solution)/shard_map/ppermute | solution.py:331
  13.3 2.7 %collective-permute-start.7 = (bf16[1,160,384]{2,1,0:T(8,128)(2,1)S(1)}, bf16[1,160,384]{2,1,0:T(8,128)(2,1)S(1)}, u32[]{:S(2)}, u32[]{:S(2)}) collective-permute-start(bf16[1,160,384]{2,1,0:T(8,128)(2,1)S(1)} %collective-permute-done.3.rest2), channel_id=1, source_target_pairs={{0,2},{2,0},{4,6},{6,4},{8,10},{10,8},{12,14},{14,12},{16,18},{18,... | collective-permute-start | bytes 368648 | tf_op jit(solution)/shard_map/ppermute | solution.py:331
  13.7 3.9 %collective-permute-start.5 = (bf16[1,160,384]{2,1,0:T(8,128)(2,1)S(1)}, bf16[1,160,384]{2,1,0:T(8,128)(2,1)S(1)}, u32[]{:S(2)}, u32[]{:S(2)}) collective-permute-start(bf16[1,160,384]{2,1,0:T(8,128)(2,1)S(1)} %collective-permute-done.1.edges), channel_id=1, source_target_pairs={{0,2},{2,0},{4,6},{6,4},{8,10},{10,8},{12,14},{14,12},{16,18},{18,... | collective-permute-start | bytes 368648 | tf_op jit(solution)/shard_map/ppermute | solution.py:331
  16.0 1.6 %collective-permute-start.4 = (bf16[1,160,384]{2,1,0:T(8,128)(2,1)S(1)}, bf16[1,160,384]{2,1,0:T(8,128)(2,1)S(1)}, u32[]{:S(2)}, u32[]{:S(2)}) collective-permute-start(bf16[1,160,384]{2,1,0:T(8,128)(2,1)S(1)} %collective-permute-done.2.edges2), channel_id=1, source_target_pairs={{0,2},{2,0},{4,6},{6,4},{8,10},{10,8},{12,14},{14,12},{16,18},{18,... | collective-permute-start | bytes 368648 | tf_op jit(solution)/shard_map/ppermute | solution.py:331
  17.6 4.0 %copy-start.2 = (bf16[3,3,384,192]{2,3,1,0:T(8,128)(2,1)S(1)}, bf16[3,3,384,192]{2,3,1,0:T(8,128)(2,1)}, u32[]{:S(2)}) copy-start(bf16[3,3,384,192]{2,3,1,0:T(8,128)(2,1)} %param.14) | copy-start | bytes 3981316
  19.0 5.3 %collective-permute-start.11 = (bf16[2,160,384]{2,1,0:T(8,128)(2,1)S(1)}, bf16[2,160,384]{2,1,0:T(8,128)(2,1)S(1)}, u32[]{:S(2)}, u32[]{:S(2)}) collective-permute-start(bf16[2,160,384]{2,1,0:T(8,128)(2,1)S(1)} %get-tuple-element.36.own), channel_id=1, source_target_pairs={{0,2},{2,0},{4,6},{6,4},{8,10},{10,8},{12,14},{14,12},{16,18},{18,... | collective-permute-start | bytes 737288 | tf_op jit(solution)/shard_map/ppermute | solution.py:331
  19.6 8.6 %collective-permute-start.10 = (bf16[1,160,384]{2,1,0:T(8,128)(2,1)S(1)}, bf16[1,160,384]{2,1,0:T(8,128)(2,1)S(1)}, u32[]{:S(2)}, u32[]{:S(2)}) collective-permute-start(bf16[1,160,384]{2,1,0:T(8,128)(2,1)S(1)} %get-tuple-element.37), channel_id=1, source_target_pairs={{0,4},{2,6},{4,8},{6,10},{8,12},{10,14},{12,16},{14,18},{16,20},{1... | collective-permute-start | bytes 368648 | tf_op jit(solution)/shard_map/ppermute | solution.py:336
  20.1 10.7 %collective-permute-start.9 = (bf16[1,160,384]{2,1,0:T(8,128)(2,1)S(1)}, bf16[1,160,384]{2,1,0:T(8,128)(2,1)S(1)}, u32[]{:S(2)}, u32[]{:S(2)}) collective-permute-start(bf16[1,160,384]{2,1,0:T(8,128)(2,1)S(1)} %get-tuple-element.37), channel_id=1, source_target_pairs={{0,1},{1,0},{2,3},{3,2},{4,5},{5,4},{6,7},{7,6},{8,9},{9,8},{10,11... | collective-permute-start | bytes 368648 | tf_op jit(solution)/shard_map/ppermute | solution.py:342
  21.6 2.7 %copy-start.1 = (bf16[3,384,768]{2,1,0:T(8,128)(2,1)S(1)}, bf16[3,384,768]{2,1,0:T(8,128)(2,1)}, u32[]{:S(2)}) copy-start(bf16[3,384,768]{2,1,0:T(8,128)(2,1)} %param.12) | copy-start | bytes 5308420
  21.6 2.7 %copy-start.3 = (f32[768]{0:T(1024)S(1)}, f32[768]{0:T(1024)}, u32[]{:S(2)}) copy-start(f32[768]{0:T(1024)} %tbias.5) | copy-start | bytes 9220
  21.6 2.7 %copy-start.5 = (f32[192]{0:T(256)S(1)}, f32[192]{0:T(256)}, u32[]{:S(2)}) copy-start(f32[192]{0:T(256)} %ubias.5) | copy-start | bytes 2308
  23.0 7.8 %collective-permute-start.12 = (bf16[1,160,384]{2,1,0:T(8,128)(2,1)S(1)}, bf16[1,160,384]{2,1,0:T(8,128)(2,1)S(1)}, u32[]{:S(2)}, u32[]{:S(2)}) collective-permute-start(bf16[1,160,384]{2,1,0:T(8,128)(2,1)S(1)} %get-tuple-element.43), channel_id=1, source_target_pairs={{0,4},{2,6},{4,8},{6,10},{8,12},{10,14},{12,16},{14,18},{16,20},{1... | collective-permute-start | bytes 368648 | tf_op jit(solution)/shard_map/ppermute | solution.py:336
  28.2 5.1 %collective-permute-start.15 = (bf16[1,160,384]{2,1,0:T(8,128)(2,1)S(1)}, bf16[1,160,384]{2,1,0:T(8,128)(2,1)S(1)}, u32[]{:S(2)}, u32[]{:S(2)}) collective-permute-start(bf16[1,160,384]{2,1,0:T(8,128)(2,1)S(1)} %collective-permute-done.10.near2), channel_id=1, source_target_pairs={{0,1},{1,0},{2,3},{3,2},{4,5},{5,4},{6,7},{7,6},{8,9},{9,8},{10,11... | collective-permute-start | bytes 368648 | tf_op jit(solution)/shard_map/ppermute | solution.py:342
  30.8 2.5 %collective-permute-start.17 = (bf16[1,160,384]{2,1,0:T(8,128)(2,1)S(1)}, bf16[1,160,384]{2,1,0:T(8,128)(2,1)S(1)}, u32[]{:S(2)}, u32[]{:S(2)}) collective-permute-start(bf16[1,160,384]{2,1,0:T(8,128)(2,1)S(1)} %collective-permute-done.9.edges), channel_id=1, source_target_pairs={{0,2},{2,0},{4,6},{6,4},{8,10},{10,8},{12,14},{14,12},{16,18},{18,... | collective-permute-start | bytes 368648 | tf_op jit(solution)/shard_map/ppermute | solution.py:331
  30.8 5.0 %collective-permute-start.13 = (bf16[1,160,384]{2,1,0:T(8,128)(2,1)S(1)}, bf16[1,160,384]{2,1,0:T(8,128)(2,1)S(1)}, u32[]{:S(2)}, u32[]{:S(2)}) collective-permute-start(bf16[1,160,384]{2,1,0:T(8,128)(2,1)S(1)} %collective-permute-done.10.near2), channel_id=1, source_target_pairs={{0,2},{2,0},{4,6},{6,4},{8,10},{10,8},{12,14},{14,12},{16,18},{18,... | collective-permute-start | bytes 368648 | tf_op jit(solution)/shard_map/ppermute | solution.py:331
  31.3 4.5 %collective-permute-start.14 = (bf16[1,160,384]{2,1,0:T(8,128)(2,1)S(1)}, bf16[1,160,384]{2,1,0:T(8,128)(2,1)S(1)}, u32[]{:S(2)}, u32[]{:S(2)}) collective-permute-start(bf16[1,160,384]{2,1,0:T(8,128)(2,1)S(1)} %collective-permute-done.12.rest2), channel_id=1, source_target_pairs={{0,2},{2,0},{4,6},{6,4},{8,10},{10,8},{12,14},{14,12},{16,18},{18,... | collective-permute-start | bytes 368648 | tf_op jit(solution)/shard_map/ppermute | solution.py:331
  33.3 2.5 %collective-permute-start.16 = (bf16[1,160,384]{2,1,0:T(8,128)(2,1)S(1)}, bf16[1,160,384]{2,1,0:T(8,128)(2,1)S(1)}, u32[]{:S(2)}, u32[]{:S(2)}) collective-permute-start(bf16[1,160,384]{2,1,0:T(8,128)(2,1)S(1)} %collective-permute-done.15.edges2), channel_id=1, source_target_pairs={{0,2},{2,0},{4,6},{6,4},{8,10},{10,8},{12,14},{14,12},{16,18},{18,... | collective-permute-start | bytes 368648 | tf_op jit(solution)/shard_map/ppermute | solution.py:331

commit v6 on v5

--- a/solution.py
+++ b/solution.py
@@ -110,12 +110,18 @@
         acc[q] = part + bias[...][None] + row(q).astype(F32)
 
 
-def conv_second(halos, place, near2, rest2, before, gain, weight, acc, act):
+def conv_second(halos, place, near2, rest2, odd, edges, odd_edges, before, gain, weight, acc, act):
     rows = before.shape[0]
 
     @pl.when(place[4] == 0)
     def _():
-        acc[...] = before[...]
+        sides = [one_back(place, odd_edges[h], odd_edges[h]) for h in range(halos)]
+        row = lambda q: one_back(place, odd[q], odd[in_order(place, q, rows)])
+        field = held_rows(halos, rows, row, gain[...][None], act)
+        field.update(held_edges(halos, rows, sides, gain[...][None], act, rows))
+        field2 = held_edges(halos, rows, edges, gain[...][None], act, rows + halos)
+        for q, part in enumerate(conv_rows(place, halos, rows, [(weight.at[1], field), (weight.at[2], field2)])):
+            acc[q] = before[q] + part
 
     @pl.when(place[4] != 0)
     def _():
@@ -133,23 +139,24 @@
 def conv_third(halos, place, even_near, even_rest, odd, before, gain, weight, acc, act):
     rows = before.shape[0]
 
-    def row(q):
-        return one_back(place, parts_row(halos, rows, even_near, even_rest, q), odd[in_order(place, q, rows)])
-
-    field = held_rows(halos, rows, row, gain[...][None], act)
-    for q, part in enumerate(conv_rows(place, halos, rows, [(weight.at[1], field)])):
-        acc[q] = before[q] + part
+    @pl.when(place[4] == 0)
+    def _():
+        acc[...] = before[...]
+
+    @pl.when(place[4] != 0)
+    def _():
+        def row(q):
+            return one_back(place, parts_row(halos, rows, even_near, even_rest, q), odd[in_order(place, q, rows)])
+
+        field = held_rows(halos, rows, row, gain[...][None], act)
+        for q, part in enumerate(conv_rows(place, halos, rows, [(weight.at[1], field)])):
+            acc[q] = before[q] + part
 
 
 def conv_edges(halos, place, edges, edges2, even_edges, odd_edges, before, gain, weight, block, near, rest, act):
     rows = block.shape[0]
-    sides = [one_back(place, even_edges[h], odd_edges[h]) for h in range(halos)]
-    fields = [
-        (weight.at[dt], held_edges(halos, rows, field, gain[...][None], act, dt * halos, known))
-        for dt, field, known in ((2, edges, True), (1, sides, True), (0, edges2, place[4] != 0))
-    ]
-    for q, part in enumerate(conv_rows(place, halos, rows, fields)):
-        value = (before[q] if part is None else before[q] + part).astype(BF16)
+
+    def give(q, value):
         block[in_order(place, q, rows)] = value
         if q == rows - 1:
             near[halos - 1] = value
@@ -157,6 +164,21 @@
             near[0] = value
         else:
             rest[q - (halos - 1)] = value
+
+    @pl.when(place[4] == 0)
+    def _():
+        for q in range(rows):
+            give(q, before[q].astype(BF16))
+
+    @pl.when(place[4] != 0)
+    def _():
+        sides = [one_back(place, even_edges[h], odd_edges[h]) for h in range(halos)]
+        fields = [
+            (weight.at[dt], held_edges(halos, rows, field, gain[...][None], act, dt * halos))
+            for dt, field in ((2, edges), (1, sides), (0, edges2))
+        ]
+        for q, part in enumerate(conv_rows(place, halos, rows, fields)):
+            give(q, (before[q] if part is None else before[q] + part).astype(BF16))
 
 
 def up_rows(place, rows, out_rows, pairs, ubias, uw, wide, outs, out_hbm, osems):
@@ -217,7 +239,13 @@
     return inner, [o for o in range(2 * rows) if o not in inner]
 
 
-def first_inner(halos, place, own, odd, tbias, ubias, tw, uw, out_hbm, kept, doubled, wide, outs, osems):
+def first_rows(halos, rows):
+    inner, outer = inner_rows(halos, rows)
+    half = (len(inner) + 1) // 2
+    return inner[:half], inner[half:] + outer
+
+
+def first_inner(halos, place, own, odd, tbias, ubias, tw, uw, out_hbm, kept, wide, outs, osems):
     @pl.when(place[4] == 0)
     def _():
         rows = own.shape[0]
@@ -229,16 +257,11 @@
             lefts.append(jnp.concatenate([none, jnp.where(place[3] == 0, none, before), now], axis=-1))
 
         def keep(q, f, value):
-            value = value.astype(BF16)
-            doubled[f, q] = value
-            if q == rows - 1:
-                kept[f, halos - 1] = value
-            elif q == 0 and halos == 2:
-                kept[f, 0] = value
+            kept[f, q] = value.astype(BF16)
 
         doubled_rows(lefts, tw, tbias, keep)
-        out_rows = inner_rows(halos, rows)[0]
-        pairs = row_pairs(halos, rows, lambda s, f: doubled[f, s - lead], out_rows)
+        out_rows = first_rows(halos, rows)[0]
+        pairs = row_pairs(halos, rows, lambda s, f: kept[f, s - lead], out_rows)
         for copy in up_rows(place, rows, out_rows, pairs, ubias, uw, wide, outs, out_hbm, osems):
             copy.wait()
 
@@ -264,10 +287,10 @@
 
         def at(s, f):
             if lead <= s < lead + rows:
-                return kept[f, 0 if s == lead and halos == 2 else halos - 1]
+                return kept[f, s - lead]
             return doubled[f, 0 if s < lead else halos - 1]
 
-        out_rows = inner_rows(halos, rows)[1]
+        out_rows = first_rows(halos, rows)[1]
         pairs = row_pairs(halos, rows, at, out_rows)
         for copy in up_rows(place, rows, out_rows, pairs, ubias, uw, wide, outs, out_hbm, osems):
             copy.wait()
@@ -377,12 +400,12 @@
     field = (rows, cols, chans)
     sides = (halos, cols, chans)
 
-    def conv(kernel, name, share, count):
+    def conv(kernel, name, share, count, more=0):
         step = call(
             functools.partial(kernel, halos), name, share,
             [VMEM] * count,
             [(pltpu.VMEM(field, F32), VMEM)],
-            [pltpu.VMEM(field, BF16)],
+            [pltpu.VMEM((rows + more, cols, chans), BF16)],
         )
         return lambda *arrays: step(*arrays)[0]
 
@@ -402,7 +425,7 @@
     else:
         other = lambda near, rest, move: move(rest)
 
-    near, rest = call(functools.partial(split_rows, halos), "split_rows", SPLIT, [VMEM], near_rest, [])(place, main)
+    near, rest = call(functools.partial(split_rows, halos), "split_rows", SPLIT, [VMEM], near_rest, [])(place, in_hbm(main))
     near2 = two_back(near)
     edges = beside(near)
     odd = in_chip(main)
@@ -410,10 +433,12 @@
     acc = conv(conv_first, "conv_own_frame", OWN, 4)(place, main, gain, conv_bias, conv_weight)
     near2, edges, acc = together(near2, edges, acc)
     edges2 = beside(near2)
+    odd_edges = in_chip(edges)
     even_near = in_chip(near2)
     even_rest = other(even_near, rest2, in_chip)
-    odd_edges = in_chip(edges)
-    acc = conv(conv_second, "conv_two_back", TWO, 5)(place, near2, rest2, acc, gain, conv_weight)
+    acc = conv(conv_second, "conv_two_back", TWO, 8, 2 * halos)(
+        place, near2, rest2, odd, edges, odd_edges, acc, gain, conv_weight
+    )
     edges2, acc = together(edges2, acc)
     even_edges = in_chip(edges2)
     acc = conv(conv_third, "conv_one_back", THREE, 6)(place, even_near, even_rest, odd, acc, gain, conv_weight)
@@ -443,26 +468,28 @@
     rest, merged = together(rest, merged)
     rest2 = other(near2, rest, two_back)
     common = (time_bias, up_bias, tw, merged)
-    inner, outer = (len(o) for o in inner_rows(halos, rows))
+    one, two = (len(o) for o in first_rows(halos, rows))
     out, kept = call(
         functools.partial(first_inner, halos), "first_chip_inner_rows", FIRST,
         [VMEM] * 6,
-        [out_shape, (pltpu.VMEM((2,) + sides, BF16), VMEM)],
-        scratch(inner, rows),
+        [out_shape, (pltpu.VMEM((2,) + field, BF16), VMEM)],
+        scratch(one, rows)[1:],
     )(place, main, odd, *common)
     near2, kept = together(near2, kept)
     edges2 = beside(near2)
-    edges, near2, rest2 = together(edges, near2, rest2)
+    edges, near2 = together(edges, near2)
+    odd_edges = in_chip(edges)
+    near2, rest2, kept = together(near2, rest2, kept)
     even_near = in_chip(near2)
-    odd_edges = in_chip(edges)
     even_rest = other(even_near, rest2, in_chip)
     out, token = call(
         functools.partial(first_edges, halos), "first_chip_edge_rows", FIRST,
         [VMEM] * 7 + [ANY],
         [out_shape, (jax.ShapeDtypeStruct((8, LANES), F32), VMEM)],
-        scratch(outer, halos),
+        scratch(two, halos),
         input_output_aliases={8: 0},
     )(place, edges, odd_edges, kept, *common, out)
+    edges2, token = together(edges2, token)
     even_edges = in_chip(edges2)
     (out,) = call(
         functools.partial(up_kernel, halos), "time_and_up", 1,

time: 36.7 us -> 36.4 us (level)
  waiting for transfers between devices: 5.67 us -> 7.78 us
  starting transfers between devices: 15.6 us -> 14.2 us
  Pallas kernels: 14.9 us -> 13.8 us
    ppermute x4, waiting for transfers between devices: 2.06 us -> 5.82 us  [two_back(): lax.ppermute(array, 'tm', [(i, (i + 2) % frames) for i in range(frames)])]
    ppermute x4, waiting for transfers between devices: 3.58 us -> 0.25 us  [beside(): return lax.ppermute(near, 'tile', [(0, 1), (1, 0)])]
    ppermute x4, starting transfers between devices: 7.67 us -> 5.18 us  [beside(): return lax.ppermute(near, 'tile', [(0, 1), (1, 0)])]
    ppermute x10, waiting for transfers between devices: 0.03 us -> 1.71 us  [in_chip(): lax.ppermute(array, 'tm', [(i, i ^ 1) for i in range(lax.axis_size('tm'))])]
    ppermute x4, starting transfers between devices: 6.37 us -> 7.38 us  [two_back(): lax.ppermute(array, 'tm', [(i, (i + 2) % frames) for i in range(frames)])]
    pallas_call x1, Pallas kernels: 1.39 us -> 0.6 us  [local(): call(functools.partial(conv_edges, halos), 'conv_edge_rows', 1, [VMEM] *...]
    pallas_call x1, Pallas kernels: 3.87 us -> 3.14 us  [local(): call(functools.partial(first_inner, halos), 'first_chip_inner_rows', FIRS...]
  transfers between devices with their start and end apart: 18 -> 18, of which waited for: 5 -> 6; matrix products, arithmetic and copies ran while one was open for 0% -> 0% of each run, Pallas kernels for 32% -> 31%
where the time goes in v6:
time: 36.4 us; the launch traced here: 36.2 us
  starting transfers between devices  14.2 us (39%)
  Pallas kernels  13.8 us (38%)
  waiting for transfers between devices  7.78 us (21%)
    ppermute x4, starting transfers between devices, two_back(): lax.ppermute(array, 'tm', [(i, (i + 2) % frames) for i in range(frames)])  7.38 us
    ppermute x4, waiting for transfers between devices, two_back(): lax.ppermute(array, 'tm', [(i, (i + 2) % frames) for i in range(frames)])  5.82 us
    ppermute x4, starting transfers between devices, beside(): return lax.ppermute(near, 'tile', [(0, 1), (1, 0)])  5.18 us
    pallas_call x3, Pallas kernels, conv(): return lambda *arrays: step(*arrays)[0]  3.98 us
    pallas_call x1, Pallas kernels, local(): call(functools.partial(first_inner, halos), 'first_chip_inner_rows', FIRS...  3.14 us
    pallas_call x1, Pallas kernels, local(): call(functools.partial(first_edges, halos), 'first_chip_edge_rows', FIRST...  2.77 us
    ppermute x10, waiting for transfers between devices, in_chip(): lax.ppermute(array, 'tm', [(i, i ^ 1) for i in range(lax.axis_size('tm'))])  1.71 us
    ppermute x10, starting transfers between devices, in_chip(): lax.ppermute(array, 'tm', [(i, i ^ 1) for i in range(lax.axis_size('tm'))])  1.63 us
  transfers between devices with their start and end apart: 18, of which 6 were waited for; matrix products, arithmetic and copies ran while one was open for 0% of the time, Pallas kernels for 31%

profile of v6, /device:TPU:0, one launch (start us, length us, event | category | flops | bytes accessed | tf_op | source)
XLA Modules:
  0.0 36.2 jit_solution(1585019303058758545)
XLA Ops:
  0.0 0.1 stack.35.place
  0.1 0.0 copy-start.3
  0.1 0.0 copy-start
  0.1 0.0 copy-start.5
  0.1 0.0 copy-start.7
  0.1 1.1 %split_rows.1 = (bf16[1,160,384]{2,1,0:T(8,128)(2,1)S(1)}, bf16[1,160,384]{2,1,0:T(8,128)(2,1)S(1)}) custom-call(s32[5]{0:T(128)S(1)} %stack.35.place, bf16[2,160,384]{2,1,0:T(8,128)(2,1)} %bitcast.13), custom_call_target="tpu_custom_call" | custom-call | flops 3000000000 | bytes 1000 | tf_op jit(solution)/shard_map/split_rows/pallas_call | solution.py:428
  1.2 3.0 %collective-permute-start = (bf16[1,160,384]{2,1,0:T(8,128)(2,1)S(1)}, bf16[1,160,384]{2,1,0:T(8,128)(2,1)S(1)}, u32[]{:S(2)}, u32[]{:S(2)}) collective-permute-start(bf16[1,160,384]{2,1,0:T(8,128)(2,1)S(1)} %get-tuple-element.32), channel_id=1, source_target_pairs={{0,4},{2,6},{4,8},{6,10},{8,12},{10,14},{12,16},{14,18},{16,20},{1... | collective-permute-start | bytes 368648 | tf_op jit(solution)/shard_map/ppermute | solution.py:359
  4.2 1.5 %collective-permute-start.1 = (bf16[1,160,384]{2,1,0:T(8,128)(2,1)S(1)}, bf16[1,160,384]{2,1,0:T(8,128)(2,1)S(1)}, u32[]{:S(2)}, u32[]{:S(2)}) collective-permute-start(bf16[1,160,384]{2,1,0:T(8,128)(2,1)S(1)} %get-tuple-element.32), channel_id=1, source_target_pairs={{0,1},{1,0},{2,3},{3,2},{4,5},{5,4},{6,7},{7,6},{8,9},{9,8},{10,11... | collective-permute-start | bytes 368648 | tf_op jit(solution)/shard_map/ppermute | solution.py:365
  5.8 0.0 copy-done.3
  5.8 0.0 collective-permute-start.4
  5.8 1.5 %collective-permute-start.3 = (bf16[1,160,384]{2,1,0:T(8,128)(2,1)S(1)}, bf16[1,160,384]{2,1,0:T(8,128)(2,1)S(1)}, u32[]{:S(2)}, u32[]{:S(2)}) collective-permute-start(bf16[1,160,384]{2,1,0:T(8,128)(2,1)S(1)} %get-tuple-element.35), channel_id=1, source_target_pairs={{0,4},{2,6},{4,8},{6,10},{8,12},{10,14},{12,16},{14,18},{16,20},{1... | collective-permute-start | bytes 368648 | tf_op jit(solution)/shard_map/ppermute | solution.py:359
  7.3 0.0 copy-done
  7.3 0.0 copy-done.5
  7.3 0.0 copy-done.7
  7.3 1.5 %conv_own_frame.1.before = f32[2,160,384]{2,1,0:T(8,128)S(1)} custom-call(s32[5]{0:T(128)S(1)} %stack.35.place, bf16[2,160,384]{2,1,0:T(8,128)(2,1)S(1)} %bitcast.15, f32[384]{0:T(512)S(1)} %copy-done.5, f32[384]{0:T(512)S(1)} %copy-done.7, bf16[3,3,3,384,384]{4,3,2,1,0:T(8,128)(2,1)S(1)} %copy-done), custom_call_target="tpu_custom_call" | custom-call | flops 600000000 | bytes 1000 | tf_op jit(solution)/shard_map/conv_own_frame/pallas_call | solution.py:410
  8.8 1.8 %collective-permute-done.near2 = bf16[1,160,384]{2,1,0:T(8,128)(2,1)S(1)} collective-permute-done((bf16[1,160,384]{2,1,0:T(8,128)(2,1)S(1)}, bf16[1,160,384]{2,1,0:T(8,128)(2,1)S(1)}, u32[]{:S(2)}, u32[]{:S(2)}) %collective-permute-start) | collective-permute-done | bytes 122912 | tf_op jit(solution)/shard_map/ppermute | solution.py:359
  10.6 0.0 collective-permute-done.1.edges
  10.6 0.0 collective-permute-start.5
  10.6 1.5 %collective-permute-start.2 = (bf16[1,160,384]{2,1,0:T(8,128)(2,1)S(1)}, bf16[1,160,384]{2,1,0:T(8,128)(2,1)S(1)}, u32[]{:S(2)}, u32[]{:S(2)}) collective-permute-start(bf16[1,160,384]{2,1,0:T(8,128)(2,1)S(1)} %collective-permute-done.near2), channel_id=1, source_target_pairs={{0,1},{1,0},{2,3},{3,2},{4,5},{5,4},{6,7},{7,6},{8,9},{9,8},{10,11... | collective-permute-start | bytes 368648 | tf_op jit(solution)/shard_map/ppermute | solution.py:365
  12.1 0.2 collective-permute-start.7
  12.3 1.8 %collective-permute-done.3.rest2 = bf16[1,160,384]{2,1,0:T(8,128)(2,1)S(1)} collective-permute-done((bf16[1,160,384]{2,1,0:T(8,128)(2,1)S(1)}, bf16[1,160,384]{2,1,0:T(8,128)(2,1)S(1)}, u32[]{:S(2)}, u32[]{:S(2)}) %collective-permute-start.3) | collective-permute-done | bytes 122912 | tf_op jit(solution)/shard_map/ppermute | solution.py:359
  14.2 0.0 collective-permute-start.8
  14.2 0.0 collective-permute-done.5.odd_edges
  14.2 0.0 collective-permute-done.4.odd
  14.2 1.9 %conv_two_back.1.before = f32[2,160,384]{2,1,0:T(8,128)S(1)} custom-call(s32[5]{0:T(128)S(1)} %stack.35.place, bf16[1,160,384]{2,1,0:T(8,128)(2,1)S(1)} %collective-permute-done.near2, bf16[1,160,384]{2,1,0:T(8,128)(2,1)S(1)} %collective-permute-done.3.rest2, bf16[2,160,384]{2,1,0:T(8,128)(2,1)S(1)} %collective-permute-done.4.odd, ...), custom_call_target="tpu_custom_call" | custom-call | flops 600000000 | bytes 1000 | tf_op jit(solution)/shard_map/conv_two_back/pallas_call | solution.py:410
  16.1 0.2 collective-permute-done.2.edges2
  16.3 0.3 collective-permute-start.6
  16.7 0.0 collective-permute-done.7.even_near
  16.7 0.0 collective-permute-done.8.even_rest
  16.7 0.6 %conv_one_back.1.before = f32[2,160,384]{2,1,0:T(8,128)S(1)} custom-call(s32[5]{0:T(128)S(1)} %stack.35.place, bf16[1,160,384]{2,1,0:T(8,128)(2,1)S(1)} %collective-permute-done.7.even_near, bf16[1,160,384]{2,1,0:T(8,128)(2,1)S(1)} %collective-permute-done.8.even_rest, bf16[2,160,384]{2,1,0:T(8,128)(2,1)S(1)} %collective-permute-done.4.odd, ...), custom_call_target="tpu_custom_call" | custom-call | flops 3000000000 | bytes 1000 | tf_op jit(solution)/shard_map/conv_one_back/pallas_call | solution.py:410
  17.3 0.0 copy-start.2
  17.3 0.4 %collective-permute-done.6.even_edges = bf16[1,160,384]{2,1,0:T(8,128)(2,1)S(1)} collective-permute-done((bf16[1,160,384]{2,1,0:T(8,128)(2,1)S(1)}, bf16[1,160,384]{2,1,0:T(8,128)(2,1)S(1)}, u32[]{:S(2)}, u32[]{:S(2)}) %collective-permute-start.6) | collective-permute-done | bytes 122912 | tf_op jit(solution)/shard_map/ppermute | solution.py:354
  17.7 0.6 %conv_edge_rows.1 = (bf16[2,160,384]{2,1,0:T(8,128)(2,1)S(1)}, bf16[1,160,384]{2,1,0:T(8,128)(2,1)S(1)}, bf16[1,160,384]{2,1,0:T(8,128)(2,1)S(1)}) custom-call(s32[5]{0:T(128)S(1)} %stack.35.place, bf16[1,160,384]{2,1,0:T(8,128)(2,1)S(1)} %collective-permute-done.1.edges, bf16[1,160,384]{2,1,0:T(8,128)(2,1)S(1)} %collective-permute-done.2.edges2, ...), custom_call_target="tpu_custom_call" | custom-call | flops 3000000000 | bytes 1000 | tf_op jit(solution)/shard_map/conv_edge_rows/pallas_call | solution.py:445
  18.3 0.4 %collective-permute-start.11 = (bf16[2,160,384]{2,1,0:T(8,128)(2,1)S(1)}, bf16[2,160,384]{2,1,0:T(8,128)(2,1)S(1)}, u32[]{:S(2)}, u32[]{:S(2)}) collective-permute-start(bf16[2,160,384]{2,1,0:T(8,128)(2,1)S(1)} %get-tuple-element.40.own), channel_id=1, source_target_pairs={{0,2},{2,0},{4,6},{6,4},{8,10},{10,8},{12,14},{14,12},{16,18},{18,... | collective-permute-start | bytes 737288 | tf_op jit(solution)/shard_map/ppermute | solution.py:354
  18.7 1.3 %collective-permute-start.10 = (bf16[1,160,384]{2,1,0:T(8,128)(2,1)S(1)}, bf16[1,160,384]{2,1,0:T(8,128)(2,1)S(1)}, u32[]{:S(2)}, u32[]{:S(2)}) collective-permute-start(bf16[1,160,384]{2,1,0:T(8,128)(2,1)S(1)} %get-tuple-element.41), channel_id=1, source_target_pairs={{0,4},{2,6},{4,8},{6,10},{8,12},{10,14},{12,16},{14,18},{16,20},{1... | collective-permute-start | bytes 368648 | tf_op jit(solution)/shard_map/ppermute | solution.py:359
  20.0 1.5 %collective-permute-start.9 = (bf16[1,160,384]{2,1,0:T(8,128)(2,1)S(1)}, bf16[1,160,384]{2,1,0:T(8,128)(2,1)S(1)}, u32[]{:S(2)}, u32[]{:S(2)}) collective-permute-start(bf16[1,160,384]{2,1,0:T(8,128)(2,1)S(1)} %get-tuple-element.41), channel_id=1, source_target_pairs={{0,1},{1,0},{2,3},{3,2},{4,5},{5,4},{6,7},{7,6},{8,9},{9,8},{10,11... | collective-permute-start | bytes 368648 | tf_op jit(solution)/shard_map/ppermute | solution.py:365
  21.5 0.0 copy-done.2
  21.5 0.0 copy-start.1
  21.5 0.0 copy-start.4
  21.5 0.0 copy-start.6
  21.5 1.4 %merge_taps.1.uw = bf16[2,768,768]{2,1,0:T(8,128)(2,1)S(1)} custom-call(s32[5]{0:T(128)S(1)} %stack.35.place, bf16[3,3,192,384]{3,2,1,0:T(8,128)(2,1)S(1)} %bitcast.12), custom_call_target="tpu_custom_call" | custom-call | flops 600000000 | bytes 1000 | tf_op jit(solution)/shard_map/merge_taps/pallas_call | solution.py:456
  22.9 1.5 %collective-permute-start.12 = (bf16[1,160,384]{2,1,0:T(8,128)(2,1)S(1)}, bf16[1,160,384]{2,1,0:T(8,128)(2,1)S(1)}, u32[]{:S(2)}, u32[]{:S(2)}) collective-permute-start(bf16[1,160,384]{2,1,0:T(8,128)(2,1)S(1)} %get-tuple-element.48), channel_id=1, source_target_pairs={{0,4},{2,6},{4,8},{6,10},{8,12},{10,14},{12,16},{14,18},{16,20},{1... | collective-permute-start | bytes 368648 | tf_op jit(solution)/shard_map/ppermute | solution.py:359
  24.4 0.0 collective-permute-done.11.odd
  24.4 0.0 copy-done.1
  24.4 0.0 copy-done.4
  24.4 0.0 copy-done.6
  24.5 3.1 %first_chip_inner_rows.1 = (bf16[2,4,192,320]{3,2,1,0:T(8,128)(2,1)}, bf16[2,2,160,384]{3,2,1,0:T(8,128)(2,1)S(1)}) custom-call(s32[5]{0:T(128)S(1)} %stack.35.place, bf16[2,160,384]{2,1,0:T(8,128)(2,1)S(1)} %get-tuple-element.40.own, bf16[2,160,384]{2,1,0:T(8,128)(2,1)S(1)} %collective-permute-done.11.odd, f32[768]{0:T(1024)S(1)} %copy-done.4, ...), custom_call_target="tpu_custom_call" | custom-call | flops 30000000 | bytes 1000 | tf_op jit(solution)/shard_map/first_chip_inner_rows/pallas_call | solution.py:472
  27.6 0.0 collective-permute-done.10.near2
  27.6 0.0 collective-permute-done.9.edges
  27.6 0.1 collective-permute-start.16
  27.7 0.6 %collective-permute-start.15 = (bf16[1,160,384]{2,1,0:T(8,128)(2,1)S(1)}, bf16[1,160,384]{2,1,0:T(8,128)(2,1)S(1)}, u32[]{:S(2)}, u32[]{:S(2)}) collective-permute-start(bf16[1,160,384]{2,1,0:T(8,128)(2,1)S(1)} %collective-permute-done.10.near2), channel_id=1, source_target_pairs={{0,1},{1,0},{2,3},{3,2},{4,5},{5,4},{6,7},{7,6},{8,9},{9,8},{10,11... | collective-permute-start | bytes 368648 | tf_op jit(solution)/shard_map/ppermute | solution.py:365
  28.3 2.2 %collective-permute-done.12.rest2 = bf16[1,160,384]{2,1,0:T(8,128)(2,1)S(1)} collective-permute-done((bf16[1,160,384]{2,1,0:T(8,128)(2,1)S(1)}, bf16[1,160,384]{2,1,0:T(8,128)(2,1)S(1)}, u32[]{:S(2)}, u32[]{:S(2)}) %collective-permute-start.12) | collective-permute-done | bytes 122912 | tf_op jit(solution)/shard_map/ppermute | solution.py:359
  30.5 0.0 collective-permute-start.13
  30.5 0.5 %collective-permute-start.14 = (bf16[1,160,384]{2,1,0:T(8,128)(2,1)S(1)}, bf16[1,160,384]{2,1,0:T(8,128)(2,1)S(1)}, u32[]{:S(2)}, u32[]{:S(2)}) collective-permute-start(bf16[1,160,384]{2,1,0:T(8,128)(2,1)S(1)} %collective-permute-done.12.rest2), channel_id=1, source_target_pairs={{0,2},{2,0},{4,6},{6,4},{8,10},{10,8},{12,14},{14,12},{16,18},{18,... | collective-permute-start | bytes 368648 | tf_op jit(solution)/shard_map/ppermute | solution.py:354
  31.0 0.0 collective-permute-done.16.odd_edges
  31.1 2.8 %first_chip_edge_rows.1 = (bf16[2,4,192,320]{3,2,1,0:T(8,128)(2,1)}, f32[8,128]{1,0:T(8,128)S(1)}) custom-call(s32[5]{0:T(128)S(1)} %stack.35.place, bf16[1,160,384]{2,1,0:T(8,128)(2,1)S(1)} %collective-permute-done.9.edges, bf16[1,160,384]{2,1,0:T(8,128)(2,1)S(1)} %collective-permute-done.16.odd_edges, ...), custom_call_target="tpu_custom_call", output_to_operand_aliasing={{0}: (8, {})} | custom-call | flops 30000000 | bytes 1000 | tf_op jit(solution)/shard_map/first_chip_edge_rows/pallas_call | solution.py:485
  33.8 0.0 collective-permute-done.15.edges2
  33.8 0.1 collective-permute-start.17
  33.9 0.0 collective-permute-done.13.even_near
  33.9 0.0 collective-permute-done.14.even_rest
  33.9 1.3 %collective-permute-done.17.even_edges = bf16[1,160,384]{2,1,0:T(8,128)(2,1)S(1)} collective-permute-done((bf16[1,160,384]{2,1,0:T(8,128)(2,1)S(1)}, bf16[1,160,384]{2,1,0:T(8,128)(2,1)S(1)}, u32[]{:S(2)}, u32[]{:S(2)}) %collective-permute-start.17) | collective-permute-done | bytes 122912 | tf_op jit(solution)/shard_map/ppermute | solution.py:354
  35.2 0.8 %time_and_up.1 = bf16[2,4,192,320]{3,2,1,0:T(8,128)(2,1)} custom-call(s32[5]{0:T(128)S(1)} %stack.35.place, bf16[2,160,384]{2,1,0:T(8,128)(2,1)S(1)} %get-tuple-element.40.own, bf16[1,160,384]{2,1,0:T(8,128)(2,1)S(1)} %collective-permute-done.10.near2, bf16[1,160,384]{2,1,0:T(8,128)(2,1)S(1)} %collective-permute-done.12.rest2, ...), custom_call_target="tpu_custom_call", output_to_operand_aliasing={{}: (16, {})} | custom-call | flops 3000000000 | bytes 1000 | tf_op jit(solution)/shard_map/time_and_up/pallas_call | solution.py:494
Async XLA Ops:
  0.1 5.7 %copy-start.3 = (bf16[1,2,160,384]{3,2,1,0:T(8,128)(2,1)S(1)}, bf16[1,2,160,384]{3,2,1,0:T(8,128)(2,1)}, u32[]{:S(2)}) copy-start(bf16[1,2,160,384]{3,2,1,0:T(8,128)(2,1)} %param.8) | copy-start | bytes 737284
  0.1 7.2 %copy-start = (bf16[3,3,3,384,384]{4,3,2,1,0:T(8,128)(2,1)S(1)}, bf16[3,3,3,384,384]{4,3,2,1,0:T(8,128)(2,1)}, u32[]{:S(2)}) copy-start(bf16[3,3,3,384,384]{4,3,2,1,0:T(8,128)(2,1)} %weight.7) | copy-start | bytes 23887876
  0.1 7.2 %copy-start.5 = (f32[384]{0:T(512)S(1)}, f32[384]{0:T(512)}, u32[]{:S(2)}) copy-start(f32[384]{0:T(512)} %gain.7) | copy-start | bytes 4612
  0.1 7.2 %copy-start.7 = (f32[384]{0:T(512)S(1)}, f32[384]{0:T(512)}, u32[]{:S(2)}) copy-start(f32[384]{0:T(512)} %bias.1) | copy-start | bytes 4612
  1.2 9.4 %collective-permute-start = (bf16[1,160,384]{2,1,0:T(8,128)(2,1)S(1)}, bf16[1,160,384]{2,1,0:T(8,128)(2,1)S(1)}, u32[]{:S(2)}, u32[]{:S(2)}) collective-permute-start(bf16[1,160,384]{2,1,0:T(8,128)(2,1)S(1)} %get-tuple-element.32), channel_id=1, source_target_pairs={{0,4},{2,6},{4,8},{6,10},{8,12},{10,14},{12,16},{14,18},{16,20},{1... | collective-permute-start | bytes 368648 | tf_op jit(solution)/shard_map/ppermute | solution.py:359
  4.2 6.4 %collective-permute-start.1 = (bf16[1,160,384]{2,1,0:T(8,128)(2,1)S(1)}, bf16[1,160,384]{2,1,0:T(8,128)(2,1)S(1)}, u32[]{:S(2)}, u32[]{:S(2)}) collective-permute-start(bf16[1,160,384]{2,1,0:T(8,128)(2,1)S(1)} %get-tuple-element.32), channel_id=1, source_target_pairs={{0,1},{1,0},{2,3},{3,2},{4,5},{5,4},{6,7},{7,6},{8,9},{9,8},{10,11... | collective-permute-start | bytes 368648 | tf_op jit(solution)/shard_map/ppermute | solution.py:365
  5.8 8.4 %collective-permute-start.4 = (bf16[2,160,384]{2,1,0:T(8,128)(2,1)S(1)}, bf16[2,160,384]{2,1,0:T(8,128)(2,1)S(1)}, u32[]{:S(2)}, u32[]{:S(2)}) collective-permute-start(bf16[2,160,384]{2,1,0:T(8,128)(2,1)S(1)} %bitcast.14), channel_id=1, source_target_pairs={{0,2},{2,0},{4,6},{6,4},{8,10},{10,8},{12,14},{14,12},{16,18},{18,... | collective-permute-start | bytes 737288 | tf_op jit(solution)/shard_map/ppermute | solution.py:354
  5.8 8.4 %collective-permute-start.3 = (bf16[1,160,384]{2,1,0:T(8,128)(2,1)S(1)}, bf16[1,160,384]{2,1,0:T(8,128)(2,1)S(1)}, u32[]{:S(2)}, u32[]{:S(2)}) collective-permute-start(bf16[1,160,384]{2,1,0:T(8,128)(2,1)S(1)} %get-tuple-element.35), channel_id=1, source_target_pairs={{0,4},{2,6},{4,8},{6,10},{8,12},{10,14},{12,16},{14,18},{16,20},{1... | collective-permute-start | bytes 368648 | tf_op jit(solution)/shard_map/ppermute | solution.py:359
  10.6 3.6 %collective-permute-start.5 = (bf16[1,160,384]{2,1,0:T(8,128)(2,1)S(1)}, bf16[1,160,384]{2,1,0:T(8,128)(2,1)S(1)}, u32[]{:S(2)}, u32[]{:S(2)}) collective-permute-start(bf16[1,160,384]{2,1,0:T(8,128)(2,1)S(1)} %collective-permute-done.1.edges), channel_id=1, source_target_pairs={{0,2},{2,0},{4,6},{6,4},{8,10},{10,8},{12,14},{14,12},{16,18},{18,... | collective-permute-start | bytes 368648 | tf_op jit(solution)/shard_map/ppermute | solution.py:354
  10.6 5.7 %collective-permute-start.2 = (bf16[1,160,384]{2,1,0:T(8,128)(2,1)S(1)}, bf16[1,160,384]{2,1,0:T(8,128)(2,1)S(1)}, u32[]{:S(2)}, u32[]{:S(2)}) collective-permute-start(bf16[1,160,384]{2,1,0:T(8,128)(2,1)S(1)} %collective-permute-done.near2), channel_id=1, source_target_pairs={{0,1},{1,0},{2,3},{3,2},{4,5},{5,4},{6,7},{7,6},{8,9},{9,8},{10,11... | collective-permute-start | bytes 368648 | tf_op jit(solution)/shard_map/ppermute | solution.py:365
  12.1 4.6 %collective-permute-start.7 = (bf16[1,160,384]{2,1,0:T(8,128)(2,1)S(1)}, bf16[1,160,384]{2,1,0:T(8,128)(2,1)S(1)}, u32[]{:S(2)}, u32[]{:S(2)}) collective-permute-start(bf16[1,160,384]{2,1,0:T(8,128)(2,1)S(1)} %collective-permute-done.near2), channel_id=1, source_target_pairs={{0,2},{2,0},{4,6},{6,4},{8,10},{10,8},{12,14},{14,12},{16,18},{18,... | collective-permute-start | bytes 368648 | tf_op jit(solution)/shard_map/ppermute | solution.py:354
  14.2 2.5 %collective-permute-start.8 = (bf16[1,160,384]{2,1,0:T(8,128)(2,1)S(1)}, bf16[1,160,384]{2,1,0:T(8,128)(2,1)S(1)}, u32[]{:S(2)}, u32[]{:S(2)}) collective-permute-start(bf16[1,160,384]{2,1,0:T(8,128)(2,1)S(1)} %collective-permute-done.3.rest2), channel_id=1, source_target_pairs={{0,2},{2,0},{4,6},{6,4},{8,10},{10,8},{12,14},{14,12},{16,18},{18,... | collective-permute-start | bytes 368648 | tf_op jit(solution)/shard_map/ppermute | solution.py:354
  16.3 1.3 %collective-permute-start.6 = (bf16[1,160,384]{2,1,0:T(8,128)(2,1)S(1)}, bf16[1,160,384]{2,1,0:T(8,128)(2,1)S(1)}, u32[]{:S(2)}, u32[]{:S(2)}) collective-permute-start(bf16[1,160,384]{2,1,0:T(8,128)(2,1)S(1)} %collective-permute-done.2.edges2), channel_id=1, source_target_pairs={{0,2},{2,0},{4,6},{6,4},{8,10},{10,8},{12,14},{14,12},{16,18},{18,... | collective-permute-start | bytes 368648 | tf_op jit(solution)/shard_map/ppermute | solution.py:354
  17.3 4.3 %copy-start.2 = (bf16[3,3,384,192]{2,3,1,0:T(8,128)(2,1)S(1)}, bf16[3,3,384,192]{2,3,1,0:T(8,128)(2,1)}, u32[]{:S(2)}) copy-start(bf16[3,3,384,192]{2,3,1,0:T(8,128)(2,1)} %param.14) | copy-start | bytes 3981316
  18.3 6.2 %collective-permute-start.11 = (bf16[2,160,384]{2,1,0:T(8,128)(2,1)S(1)}, bf16[2,160,384]{2,1,0:T(8,128)(2,1)S(1)}, u32[]{:S(2)}, u32[]{:S(2)}) collective-permute-start(bf16[2,160,384]{2,1,0:T(8,128)(2,1)S(1)} %get-tuple-element.40.own), channel_id=1, source_target_pairs={{0,2},{2,0},{4,6},{6,4},{8,10},{10,8},{12,14},{14,12},{16,18},{18,... | collective-permute-start | bytes 737288 | tf_op jit(solution)/shard_map/ppermute | solution.py:354
  18.7 8.9 %collective-permute-start.10 = (bf16[1,160,384]{2,1,0:T(8,128)(2,1)S(1)}, bf16[1,160,384]{2,1,0:T(8,128)(2,1)S(1)}, u32[]{:S(2)}, u32[]{:S(2)}) collective-permute-start(bf16[1,160,384]{2,1,0:T(8,128)(2,1)S(1)} %get-tuple-element.41), channel_id=1, source_target_pairs={{0,4},{2,6},{4,8},{6,10},{8,12},{10,14},{12,16},{14,18},{16,20},{1... | collective-permute-start | bytes 368648 | tf_op jit(solution)/shard_map/ppermute | solution.py:359
  20.0 7.6 %collective-permute-start.9 = (bf16[1,160,384]{2,1,0:T(8,128)(2,1)S(1)}, bf16[1,160,384]{2,1,0:T(8,128)(2,1)S(1)}, u32[]{:S(2)}, u32[]{:S(2)}) collective-permute-start(bf16[1,160,384]{2,1,0:T(8,128)(2,1)S(1)} %get-tuple-element.41), channel_id=1, source_target_pairs={{0,1},{1,0},{2,3},{3,2},{4,5},{5,4},{6,7},{7,6},{8,9},{9,8},{10,11... | collective-permute-start | bytes 368648 | tf_op jit(solution)/shard_map/ppermute | solution.py:365
  21.5 2.9 %copy-start.1 = (bf16[3,384,768]{2,1,0:T(8,128)(2,1)S(1)}, bf16[3,384,768]{2,1,0:T(8,128)(2,1)}, u32[]{:S(2)}) copy-start(bf16[3,384,768]{2,1,0:T(8,128)(2,1)} %param.12) | copy-start | bytes 5308420
  21.5 2.9 %copy-start.4 = (f32[768]{0:T(1024)S(1)}, f32[768]{0:T(1024)}, u32[]{:S(2)}) copy-start(f32[768]{0:T(1024)} %tbias.5) | copy-start | bytes 9220
  21.5 2.9 %copy-start.6 = (f32[192]{0:T(256)S(1)}, f32[192]{0:T(256)}, u32[]{:S(2)}) copy-start(f32[192]{0:T(256)} %ubias.5) | copy-start | bytes 2308
  22.9 7.6 %collective-permute-start.12 = (bf16[1,160,384]{2,1,0:T(8,128)(2,1)S(1)}, bf16[1,160,384]{2,1,0:T(8,128)(2,1)S(1)}, u32[]{:S(2)}, u32[]{:S(2)}) collective-permute-start(bf16[1,160,384]{2,1,0:T(8,128)(2,1)S(1)} %get-tuple-element.48), channel_id=1, source_target_pairs={{0,4},{2,6},{4,8},{6,10},{8,12},{10,14},{12,16},{14,18},{16,20},{1... | collective-permute-start | bytes 368648 | tf_op jit(solution)/shard_map/ppermute | solution.py:359
  27.6 3.4 %collective-permute-start.16 = (bf16[1,160,384]{2,1,0:T(8,128)(2,1)S(1)}, bf16[1,160,384]{2,1,0:T(8,128)(2,1)S(1)}, u32[]{:S(2)}, u32[]{:S(2)}) collective-permute-start(bf16[1,160,384]{2,1,0:T(8,128)(2,1)S(1)} %collective-permute-done.9.edges), channel_id=1, source_target_pairs={{0,2},{2,0},{4,6},{6,4},{8,10},{10,8},{12,14},{14,12},{16,18},{18,... | collective-permute-start | bytes 368648 | tf_op jit(solution)/shard_map/ppermute | solution.py:354
  27.7 6.1 %collective-permute-start.15 = (bf16[1,160,384]{2,1,0:T(8,128)(2,1)S(1)}, bf16[1,160,384]{2,1,0:T(8,128)(2,1)S(1)}, u32[]{:S(2)}, u32[]{:S(2)}) collective-permute-start(bf16[1,160,384]{2,1,0:T(8,128)(2,1)S(1)} %collective-permute-done.10.near2), channel_id=1, source_target_pairs={{0,1},{1,0},{2,3},{3,2},{4,5},{5,4},{6,7},{7,6},{8,9},{9,8},{10,11... | collective-permute-start | bytes 368648 | tf_op jit(solution)/shard_map/ppermute | solution.py:365
  30.5 3.4 %collective-permute-start.13 = (bf16[1,160,384]{2,1,0:T(8,128)(2,1)S(1)}, bf16[1,160,384]{2,1,0:T(8,128)(2,1)S(1)}, u32[]{:S(2)}, u32[]{:S(2)}) collective-permute-start(bf16[1,160,384]{2,1,0:T(8,128)(2,1)S(1)} %collective-permute-done.10.near2), channel_id=1, source_target_pairs={{0,2},{2,0},{4,6},{6,4},{8,10},{10,8},{12,14},{14,12},{16,18},{18,... | collective-permute-start | bytes 368648 | tf_op jit(solution)/shard_map/ppermute | solution.py:354
  30.5 3.4 %collective-permute-start.14 = (bf16[1,160,384]{2,1,0:T(8,128)(2,1)S(1)}, bf16[1,160,384]{2,1,0:T(8,128)(2,1)S(1)}, u32[]{:S(2)}, u32[]{:S(2)}) collective-permute-start(bf16[1,160,384]{2,1,0:T(8,128)(2,1)S(1)} %collective-permute-done.12.rest2), channel_id=1, source_target_pairs={{0,2},{2,0},{4,6},{6,4},{8,10},{10,8},{12,14},{14,12},{16,18},{18,... | collective-permute-start | bytes 368648 | tf_op jit(solution)/shard_map/ppermute | solution.py:354
  33.8 1.4 %collective-permute-start.17 = (bf16[1,160,384]{2,1,0:T(8,128)(2,1)S(1)}, bf16[1,160,384]{2,1,0:T(8,128)(2,1)S(1)}, u32[]{:S(2)}, u32[]{:S(2)}) collective-permute-start(bf16[1,160,384]{2,1,0:T(8,128)(2,1)S(1)} %collective-permute-done.15.edges2), channel_id=1, source_target_pairs={{0,2},{2,0},{4,6},{6,4},{8,10},{10,8},{12,14},{14,12},{16,18},{18,... | collective-permute-start | bytes 368648 | tf_op jit(solution)/shard_map/ppermute | solution.py:354

commit v7 on v6

--- a/solution.py
+++ b/solution.py
@@ -245,7 +245,9 @@
     return inner[:half], inner[half:] + outer
 
 
-def first_inner(halos, place, own, odd, tbias, ubias, tw, uw, out_hbm, kept, wide, outs, osems):
+def merge_and_first(halos, place, taps, own, odd, tbias, ubias, tw, uw, out_hbm, kept, wide, outs, osems):
+    merge_taps(place, taps, uw)
+
     @pl.when(place[4] == 0)
     def _():
         rows = own.shape[0]
@@ -328,7 +330,7 @@
             copy.wait()
 
 
-def merge_kernel(place, taps, merged):
+def merge_taps(place, taps, merged):
     chans = taps.shape[3]
 
     def tap(dh, dw):
@@ -410,12 +412,6 @@
         return lambda *arrays: step(*arrays)[0]
 
     taps_t = up_weight.transpose(0, 1, 3, 2)
-    merge = call(
-        merge_kernel, "merge_taps", MERGE,
-        [VMEM],
-        [(pltpu.VMEM((2, 2 * chans, 4 * outs_n), BF16), VMEM)],
-        [],
-    )
     near_rest = [
         (jax.ShapeDtypeStruct(sides, BF16), VMEM),
         (jax.ShapeDtypeStruct((max(rows - halos, 1), cols, chans), BF16), VMEM),
@@ -453,7 +449,6 @@
     edges = beside(near)
     odd = in_chip(block)
     taps_t, main = together(taps_t, block)
-    (merged,) = merge(place, taps_t)
     tw = time_weight.reshape(3 * chans, 2 * chans)
     out_shape = (jax.ShapeDtypeStruct((2, 2 * rows, outs_n, 2 * cols), BF16), ANY)
 
@@ -465,16 +460,19 @@
             pltpu.SemaphoreType.DMA((2, count)),
         ]
 
-    rest, merged = together(rest, merged)
     rest2 = other(near2, rest, two_back)
+    one, two = (len(o) for o in first_rows(halos, rows))
+    merged, out, kept = call(
+        functools.partial(merge_and_first, halos), "merge_taps_and_first_chip_rows", MERGE,
+        [VMEM] * 6,
+        [
+            (pltpu.VMEM((2, 2 * chans, 4 * outs_n), BF16), VMEM),
+            out_shape,
+            (pltpu.VMEM((2,) + field, BF16), VMEM),
+        ],
+        scratch(one, rows)[1:],
+    )(place, taps_t, main, odd, time_bias, up_bias, tw)
     common = (time_bias, up_bias, tw, merged)
-    one, two = (len(o) for o in first_rows(halos, rows))
-    out, kept = call(
-        functools.partial(first_inner, halos), "first_chip_inner_rows", FIRST,
-        [VMEM] * 6,
-        [out_shape, (pltpu.VMEM((2,) + field, BF16), VMEM)],
-        scratch(one, rows)[1:],
-    )(place, main, odd, *common)
     near2, kept = together(near2, kept)
     edges2 = beside(near2)
     edges, near2 = together(edges, near2)
@@ -489,7 +487,6 @@
         scratch(two, halos),
         input_output_aliases={8: 0},
     )(place, edges, odd_edges, kept, *common, out)
-    edges2, token = together(edges2, token)
     even_edges = in_chip(edges2)
     (out,) = call(
         functools.partial(up_kernel, halos), "time_and_up", 1,

time: 36.4 us -> 36.1 us (level)
  starting transfers between devices: 14.2 us -> 15.1 us
  waiting for transfers between devices: 7.78 us -> 7 us
  Pallas kernels: 13.8 us -> 13.3 us
    ppermute x4, waiting for transfers between devices: 0.25 us -> 2.36 us  [beside(): return lax.ppermute(near, 'tile', [(0, 1), (1, 0)])]
    ppermute x4, waiting for transfers between devices: 5.82 us -> 4.26 us  [two_back(): lax.ppermute(array, 'tm', [(i, (i + 2) % frames) for i in range(frames)])]
    ppermute x10, waiting for transfers between devices: 1.71 us -> 0.37 us  [in_chip(): lax.ppermute(array, 'tm', [(i, i ^ 1) for i in range(lax.axis_size('tm'))])]
    ppermute x4, starting transfers between devices: 5.18 us -> 6.26 us  [beside(): return lax.ppermute(near, 'tile', [(0, 1), (1, 0)])]
    pallas_call x2 -> x1, Pallas kernels: 4.51 us -> 3.96 us  [local(): call(functools.partial(merge_and_first, halos), 'merge_taps_and_first_chi...]
  transfers between devices with their start and end apart: 18 -> 18, of which waited for: 6 -> 7; matrix products, arithmetic and copies ran while one was open for 0% -> 0% of each run, Pallas kernels for 31% -> 30%
where the time goes in v7:
time: 36.1 us; the launch traced here: 35.9 us
  starting transfers between devices  15.1 us (42%)
  Pallas kernels  13.3 us (37%)
  waiting for transfers between devices  7 us (19%)
    ppermute x4, starting transfers between devices, two_back(): lax.ppermute(array, 'tm', [(i, (i + 2) % frames) for i in range(frames)])  7.37 us
    ppermute x4, starting transfers between devices, beside(): return lax.ppermute(near, 'tile', [(0, 1), (1, 0)])  6.26 us
    ppermute x4, waiting for transfers between devices, two_back(): lax.ppermute(array, 'tm', [(i, (i + 2) % frames) for i in range(frames)])  4.26 us
    pallas_call x3, Pallas kernels, conv(): return lambda *arrays: step(*arrays)[0]  3.98 us
    pallas_call x1, Pallas kernels, local(): call(functools.partial(merge_and_first, halos), 'merge_taps_and_first_chi...  3.96 us
    pallas_call x1, Pallas kernels, local(): call(functools.partial(first_edges, halos), 'first_chip_edge_rows', FIRST...  2.81 us
    ppermute x4, waiting for transfers between devices, beside(): return lax.ppermute(near, 'tile', [(0, 1), (1, 0)])  2.36 us
    ppermute x10, starting transfers between devices, in_chip(): lax.ppermute(array, 'tm', [(i, i ^ 1) for i in range(lax.axis_size('tm'))])  1.49 us
  transfers between devices with their start and end apart: 18, of which 7 were waited for; matrix products, arithmetic and copies ran while one was open for 0% of the time, Pallas kernels for 30%

profile of v7, /device:TPU:0, one launch (start us, length us, event | category | flops | bytes accessed | tf_op | source)
XLA Modules:
  0.0 35.9 jit_solution(5969028686478379202)
XLA Ops:
  0.0 0.1 stack.35.place
  0.1 0.0 copy-start.3
  0.1 0.0 copy-start
  0.1 0.0 copy-start.5
  0.1 0.0 copy-start.7
  0.1 1.1 %split_rows.1 = (bf16[1,160,384]{2,1,0:T(8,128)(2,1)S(1)}, bf16[1,160,384]{2,1,0:T(8,128)(2,1)S(1)}) custom-call(s32[5]{0:T(128)S(1)} %stack.35.place, bf16[2,160,384]{2,1,0:T(8,128)(2,1)} %bitcast.13), custom_call_target="tpu_custom_call" | custom-call | flops 3000000000 | bytes 1000 | tf_op jit(solution)/shard_map/split_rows/pallas_call | solution.py:424
  1.2 3.0 %collective-permute-start = (bf16[1,160,384]{2,1,0:T(8,128)(2,1)S(1)}, bf16[1,160,384]{2,1,0:T(8,128)(2,1)S(1)}, u32[]{:S(2)}, u32[]{:S(2)}) collective-permute-start(bf16[1,160,384]{2,1,0:T(8,128)(2,1)S(1)} %get-tuple-element.29), channel_id=1, source_target_pairs={{0,4},{2,6},{4,8},{6,10},{8,12},{10,14},{12,16},{14,18},{16,20},{1... | collective-permute-start | bytes 368648 | tf_op jit(solution)/shard_map/ppermute | solution.py:361
  4.2 1.5 %collective-permute-start.1 = (bf16[1,160,384]{2,1,0:T(8,128)(2,1)S(1)}, bf16[1,160,384]{2,1,0:T(8,128)(2,1)S(1)}, u32[]{:S(2)}, u32[]{:S(2)}) collective-permute-start(bf16[1,160,384]{2,1,0:T(8,128)(2,1)S(1)} %get-tuple-element.29), channel_id=1, source_target_pairs={{0,1},{1,0},{2,3},{3,2},{4,5},{5,4},{6,7},{7,6},{8,9},{9,8},{10,11... | collective-permute-start | bytes 368648 | tf_op jit(solution)/shard_map/ppermute | solution.py:367
  5.8 0.0 copy-done.3
  5.8 0.0 collective-permute-start.4
  5.8 1.5 %collective-permute-start.3 = (bf16[1,160,384]{2,1,0:T(8,128)(2,1)S(1)}, bf16[1,160,384]{2,1,0:T(8,128)(2,1)S(1)}, u32[]{:S(2)}, u32[]{:S(2)}) collective-permute-start(bf16[1,160,384]{2,1,0:T(8,128)(2,1)S(1)} %get-tuple-element.32), channel_id=1, source_target_pairs={{0,4},{2,6},{4,8},{6,10},{8,12},{10,14},{12,16},{14,18},{16,20},{1... | collective-permute-start | bytes 368648 | tf_op jit(solution)/shard_map/ppermute | solution.py:361
  7.3 0.0 copy-done
  7.3 0.0 copy-done.5
  7.3 0.0 copy-done.7
  7.3 1.5 %conv_own_frame.1.before = f32[2,160,384]{2,1,0:T(8,128)S(1)} custom-call(s32[5]{0:T(128)S(1)} %stack.35.place, bf16[2,160,384]{2,1,0:T(8,128)(2,1)S(1)} %bitcast.15, f32[384]{0:T(512)S(1)} %copy-done.5, f32[384]{0:T(512)S(1)} %copy-done.7, bf16[3,3,3,384,384]{4,3,2,1,0:T(8,128)(2,1)S(1)} %copy-done), custom_call_target="tpu_custom_call" | custom-call | flops 600000000 | bytes 1000 | tf_op jit(solution)/shard_map/conv_own_frame/pallas_call | solution.py:412
  8.8 1.8 %collective-permute-done.near2 = bf16[1,160,384]{2,1,0:T(8,128)(2,1)S(1)} collective-permute-done((bf16[1,160,384]{2,1,0:T(8,128)(2,1)S(1)}, bf16[1,160,384]{2,1,0:T(8,128)(2,1)S(1)}, u32[]{:S(2)}, u32[]{:S(2)}) %collective-permute-start) | collective-permute-done | bytes 122912 | tf_op jit(solution)/shard_map/ppermute | solution.py:361
  10.6 0.0 collective-permute-done.1.edges
  10.6 0.0 collective-permute-start.5
  10.6 1.5 %collective-permute-start.2 = (bf16[1,160,384]{2,1,0:T(8,128)(2,1)S(1)}, bf16[1,160,384]{2,1,0:T(8,128)(2,1)S(1)}, u32[]{:S(2)}, u32[]{:S(2)}) collective-permute-start(bf16[1,160,384]{2,1,0:T(8,128)(2,1)S(1)} %collective-permute-done.near2), channel_id=1, source_target_pairs={{0,1},{1,0},{2,3},{3,2},{4,5},{5,4},{6,7},{7,6},{8,9},{9,8},{10,11... | collective-permute-start | bytes 368648 | tf_op jit(solution)/shard_map/ppermute | solution.py:367
  12.1 0.2 collective-permute-start.7
  12.3 1.8 %collective-permute-done.3.rest2 = bf16[1,160,384]{2,1,0:T(8,128)(2,1)S(1)} collective-permute-done((bf16[1,160,384]{2,1,0:T(8,128)(2,1)S(1)}, bf16[1,160,384]{2,1,0:T(8,128)(2,1)S(1)}, u32[]{:S(2)}, u32[]{:S(2)}) %collective-permute-start.3) | collective-permute-done | bytes 122912 | tf_op jit(solution)/shard_map/ppermute | solution.py:361
  14.2 0.0 collective-permute-start.8
  14.2 0.0 collective-permute-done.5.odd_edges
  14.2 0.0 collective-permute-done.4.odd
  14.2 1.9 %conv_two_back.1.before = f32[2,160,384]{2,1,0:T(8,128)S(1)} custom-call(s32[5]{0:T(128)S(1)} %stack.35.place, bf16[1,160,384]{2,1,0:T(8,128)(2,1)S(1)} %collective-permute-done.near2, bf16[1,160,384]{2,1,0:T(8,128)(2,1)S(1)} %collective-permute-done.3.rest2, bf16[2,160,384]{2,1,0:T(8,128)(2,1)S(1)} %collective-permute-done.4.odd, ...), custom_call_target="tpu_custom_call" | custom-call | flops 600000000 | bytes 1000 | tf_op jit(solution)/shard_map/conv_two_back/pallas_call | solution.py:412
  16.1 0.2 collective-permute-done.2.edges2
  16.3 0.3 collective-permute-start.6
  16.7 0.0 collective-permute-done.7.even_near
  16.7 0.0 collective-permute-done.8.even_rest
  16.7 0.6 %conv_one_back.1.before = f32[2,160,384]{2,1,0:T(8,128)S(1)} custom-call(s32[5]{0:T(128)S(1)} %stack.35.place, bf16[1,160,384]{2,1,0:T(8,128)(2,1)S(1)} %collective-permute-done.7.even_near, bf16[1,160,384]{2,1,0:T(8,128)(2,1)S(1)} %collective-permute-done.8.even_rest, bf16[2,160,384]{2,1,0:T(8,128)(2,1)S(1)} %collective-permute-done.4.odd, ...), custom_call_target="tpu_custom_call" | custom-call | flops 3000000000 | bytes 1000 | tf_op jit(solution)/shard_map/conv_one_back/pallas_call | solution.py:412
  17.3 0.0 copy-start.1
  17.3 0.0 copy-start.2
  17.3 0.0 copy-start.4
  17.3 0.0 copy-start.6
  17.3 0.3 collective-permute-done.6.even_edges
  17.7 0.6 %conv_edge_rows.1 = (bf16[2,160,384]{2,1,0:T(8,128)(2,1)S(1)}, bf16[1,160,384]{2,1,0:T(8,128)(2,1)S(1)}, bf16[1,160,384]{2,1,0:T(8,128)(2,1)S(1)}) custom-call(s32[5]{0:T(128)S(1)} %stack.35.place, bf16[1,160,384]{2,1,0:T(8,128)(2,1)S(1)} %collective-permute-done.1.edges, bf16[1,160,384]{2,1,0:T(8,128)(2,1)S(1)} %collective-permute-done.2.edges2, ...), custom_call_target="tpu_custom_call" | custom-call | flops 3000000000 | bytes 1000 | tf_op jit(solution)/shard_map/conv_edge_rows/pallas_call | solution.py:441
  18.3 0.4 %collective-permute-start.11 = (bf16[2,160,384]{2,1,0:T(8,128)(2,1)S(1)}, bf16[2,160,384]{2,1,0:T(8,128)(2,1)S(1)}, u32[]{:S(2)}, u32[]{:S(2)}) collective-permute-start(bf16[2,160,384]{2,1,0:T(8,128)(2,1)S(1)} %get-tuple-element.37.own), channel_id=1, source_target_pairs={{0,2},{2,0},{4,6},{6,4},{8,10},{10,8},{12,14},{14,12},{16,18},{18,... | collective-permute-start | bytes 737288 | tf_op jit(solution)/shard_map/ppermute | solution.py:356
  18.7 1.3 %collective-permute-start.10 = (bf16[1,160,384]{2,1,0:T(8,128)(2,1)S(1)}, bf16[1,160,384]{2,1,0:T(8,128)(2,1)S(1)}, u32[]{:S(2)}, u32[]{:S(2)}) collective-permute-start(bf16[1,160,384]{2,1,0:T(8,128)(2,1)S(1)} %get-tuple-element.38), channel_id=1, source_target_pairs={{0,4},{2,6},{4,8},{6,10},{8,12},{10,14},{12,16},{14,18},{16,20},{1... | collective-permute-start | bytes 368648 | tf_op jit(solution)/shard_map/ppermute | solution.py:361
  20.0 1.5 %collective-permute-start.9 = (bf16[1,160,384]{2,1,0:T(8,128)(2,1)S(1)}, bf16[1,160,384]{2,1,0:T(8,128)(2,1)S(1)}, u32[]{:S(2)}, u32[]{:S(2)}) collective-permute-start(bf16[1,160,384]{2,1,0:T(8,128)(2,1)S(1)} %get-tuple-element.38), channel_id=1, source_target_pairs={{0,1},{1,0},{2,3},{3,2},{4,5},{5,4},{6,7},{7,6},{8,9},{9,8},{10,11... | collective-permute-start | bytes 368648 | tf_op jit(solution)/shard_map/ppermute | solution.py:367
  21.5 1.5 %collective-permute-start.12 = (bf16[1,160,384]{2,1,0:T(8,128)(2,1)S(1)}, bf16[1,160,384]{2,1,0:T(8,128)(2,1)S(1)}, u32[]{:S(2)}, u32[]{:S(2)}) collective-permute-start(bf16[1,160,384]{2,1,0:T(8,128)(2,1)S(1)} %get-tuple-element.43), channel_id=1, source_target_pairs={{0,4},{2,6},{4,8},{6,10},{8,12},{10,14},{12,16},{14,18},{16,20},{1... | collective-permute-start | bytes 368648 | tf_op jit(solution)/shard_map/ppermute | solution.py:361
  23.0 0.0 collective-permute-done.11.odd
  23.0 0.0 copy-done.1
  23.0 0.0 copy-done.2
  23.1 0.0 copy-done.4
  23.1 0.0 copy-done.6
  23.1 4.0 %merge_taps_and_first_chip_rows.1 = (bf16[2,768,768]{2,1,0:T(8,128)(2,1)S(1)}, bf16[2,4,192,320]{3,2,1,0:T(8,128)(2,1)}, bf16[2,2,160,384]{3,2,1,0:T(8,128)(2,1)S(1)}) custom-call(s32[5]{0:T(128)S(1)} %stack.35.place, bf16[3,3,192,384]{3,2,1,0:T(8,128)(2,1)S(1)} %bitcast.12, bf16[2,160,384]{2,1,0:T(8,128)(2,1)S(1)} %get-tuple-element.37.own, ...), custom_call_target="tpu_custom_call" | custom-call | flops 600000000 | bytes 1000 | tf_op jit(solution)/shard_map/merge_taps_and_first_chip_rows/pallas_call | solution.py:465
  27.0 0.1 collective-permute-done.10.near2
  27.2 1.7 %collective-permute-start.15 = (bf16[1,160,384]{2,1,0:T(8,128)(2,1)S(1)}, bf16[1,160,384]{2,1,0:T(8,128)(2,1)S(1)}, u32[]{:S(2)}, u32[]{:S(2)}) collective-permute-start(bf16[1,160,384]{2,1,0:T(8,128)(2,1)S(1)} %collective-permute-done.10.near2), channel_id=1, source_target_pairs={{0,1},{1,0},{2,3},{3,2},{4,5},{5,4},{6,7},{7,6},{8,9},{9,8},{10,11... | collective-permute-start | bytes 368648 | tf_op jit(solution)/shard_map/ppermute | solution.py:367
  28.9 0.0 collective-permute-done.9.edges
  28.9 0.0 collective-permute-start.17
  28.9 0.5 %collective-permute-done.12.rest2 = bf16[1,160,384]{2,1,0:T(8,128)(2,1)S(1)} collective-permute-done((bf16[1,160,384]{2,1,0:T(8,128)(2,1)S(1)}, bf16[1,160,384]{2,1,0:T(8,128)(2,1)S(1)}, u32[]{:S(2)}, u32[]{:S(2)}) %collective-permute-start.12) | collective-permute-done | bytes 122912 | tf_op jit(solution)/shard_map/ppermute | solution.py:361
  29.4 0.0 collective-permute-start.13
  29.4 0.5 %collective-permute-start.14 = (bf16[1,160,384]{2,1,0:T(8,128)(2,1)S(1)}, bf16[1,160,384]{2,1,0:T(8,128)(2,1)S(1)}, u32[]{:S(2)}, u32[]{:S(2)}) collective-permute-start(bf16[1,160,384]{2,1,0:T(8,128)(2,1)S(1)} %collective-permute-done.12.rest2), channel_id=1, source_target_pairs={{0,2},{2,0},{4,6},{6,4},{8,10},{10,8},{12,14},{14,12},{16,18},{18,... | collective-permute-start | bytes 368648 | tf_op jit(solution)/shard_map/ppermute | solution.py:356
  29.9 2.1 %collective-permute-done.15.edges2 = bf16[1,160,384]{2,1,0:T(8,128)(2,1)S(1)} collective-permute-done((bf16[1,160,384]{2,1,0:T(8,128)(2,1)S(1)}, bf16[1,160,384]{2,1,0:T(8,128)(2,1)S(1)}, u32[]{:S(2)}, u32[]{:S(2)}) %collective-permute-start.15) | collective-permute-done | bytes 122912 | tf_op jit(solution)/shard_map/ppermute | solution.py:367
  32.0 0.0 collective-permute-start.16
  32.0 0.0 collective-permute-done.17.odd_edges
  32.0 2.8 %first_chip_edge_rows.1 = (bf16[2,4,192,320]{3,2,1,0:T(8,128)(2,1)}, f32[8,128]{1,0:T(8,128)S(1)}) custom-call(s32[5]{0:T(128)S(1)} %stack.35.place, bf16[1,160,384]{2,1,0:T(8,128)(2,1)S(1)} %collective-permute-done.9.edges, bf16[1,160,384]{2,1,0:T(8,128)(2,1)S(1)} %collective-permute-done.17.odd_edges, ...), custom_call_target="tpu_custom_call", output_to_operand_aliasing={{0}: (8, {})} | custom-call | flops 30000000 | bytes 1000 | tf_op jit(solution)/shard_map/first_chip_edge_rows/pallas_call | solution.py:483
  34.9 0.0 collective-permute-done.13.even_near
  34.9 0.0 collective-permute-done.14.even_rest
  34.9 0.0 collective-permute-done.16.even_edges
  34.9 0.8 %time_and_up.1 = bf16[2,4,192,320]{3,2,1,0:T(8,128)(2,1)} custom-call(s32[5]{0:T(128)S(1)} %stack.35.place, bf16[2,160,384]{2,1,0:T(8,128)(2,1)S(1)} %get-tuple-element.37.own, bf16[1,160,384]{2,1,0:T(8,128)(2,1)S(1)} %collective-permute-done.10.near2, bf16[1,160,384]{2,1,0:T(8,128)(2,1)S(1)} %collective-permute-done.12.rest2, ...), custom_call_target="tpu_custom_call", output_to_operand_aliasing={{}: (16, {})} | custom-call | flops 3000000000 | bytes 1000 | tf_op jit(solution)/shard_map/time_and_up/pallas_call | solution.py:491
Async XLA Ops:
  0.1 5.7 %copy-start.3 = (bf16[1,2,160,384]{3,2,1,0:T(8,128)(2,1)S(1)}, bf16[1,2,160,384]{3,2,1,0:T(8,128)(2,1)}, u32[]{:S(2)}) copy-start(bf16[1,2,160,384]{3,2,1,0:T(8,128)(2,1)} %param.8) | copy-start | bytes 737284
  0.1 7.2 %copy-start = (bf16[3,3,3,384,384]{4,3,2,1,0:T(8,128)(2,1)S(1)}, bf16[3,3,3,384,384]{4,3,2,1,0:T(8,128)(2,1)}, u32[]{:S(2)}) copy-start(bf16[3,3,3,384,384]{4,3,2,1,0:T(8,128)(2,1)} %weight.7) | copy-start | bytes 23887876
  0.1 7.2 %copy-start.5 = (f32[384]{0:T(512)S(1)}, f32[384]{0:T(512)}, u32[]{:S(2)}) copy-start(f32[384]{0:T(512)} %gain.7) | copy-start | bytes 4612
  0.1 7.2 %copy-start.7 = (f32[384]{0:T(512)S(1)}, f32[384]{0:T(512)}, u32[]{:S(2)}) copy-start(f32[384]{0:T(512)} %bias.1) | copy-start | bytes 4612
  1.2 9.4 %collective-permute-start = (bf16[1,160,384]{2,1,0:T(8,128)(2,1)S(1)}, bf16[1,160,384]{2,1,0:T(8,128)(2,1)S(1)}, u32[]{:S(2)}, u32[]{:S(2)}) collective-permute-start(bf16[1,160,384]{2,1,0:T(8,128)(2,1)S(1)} %get-tuple-element.29), channel_id=1, source_target_pairs={{0,4},{2,6},{4,8},{6,10},{8,12},{10,14},{12,16},{14,18},{16,20},{1... | collective-permute-start | bytes 368648 | tf_op jit(solution)/shard_map/ppermute | solution.py:361
  4.2 6.4 %collective-permute-start.1 = (bf16[1,160,384]{2,1,0:T(8,128)(2,1)S(1)}, bf16[1,160,384]{2,1,0:T(8,128)(2,1)S(1)}, u32[]{:S(2)}, u32[]{:S(2)}) collective-permute-start(bf16[1,160,384]{2,1,0:T(8,128)(2,1)S(1)} %get-tuple-element.29), channel_id=1, source_target_pairs={{0,1},{1,0},{2,3},{3,2},{4,5},{5,4},{6,7},{7,6},{8,9},{9,8},{10,11... | collective-permute-start | bytes 368648 | tf_op jit(solution)/shard_map/ppermute | solution.py:367
  5.8 8.4 %collective-permute-start.4 = (bf16[2,160,384]{2,1,0:T(8,128)(2,1)S(1)}, bf16[2,160,384]{2,1,0:T(8,128)(2,1)S(1)}, u32[]{:S(2)}, u32[]{:S(2)}) collective-permute-start(bf16[2,160,384]{2,1,0:T(8,128)(2,1)S(1)} %bitcast.14), channel_id=1, source_target_pairs={{0,2},{2,0},{4,6},{6,4},{8,10},{10,8},{12,14},{14,12},{16,18},{18,... | collective-permute-start | bytes 737288 | tf_op jit(solution)/shard_map/ppermute | solution.py:356
  5.8 8.4 %collective-permute-start.3 = (bf16[1,160,384]{2,1,0:T(8,128)(2,1)S(1)}, bf16[1,160,384]{2,1,0:T(8,128)(2,1)S(1)}, u32[]{:S(2)}, u32[]{:S(2)}) collective-permute-start(bf16[1,160,384]{2,1,0:T(8,128)(2,1)S(1)} %get-tuple-element.32), channel_id=1, source_target_pairs={{0,4},{2,6},{4,8},{6,10},{8,12},{10,14},{12,16},{14,18},{16,20},{1... | collective-permute-start | bytes 368648 | tf_op jit(solution)/shard_map/ppermute | solution.py:361
  10.6 3.6 %collective-permute-start.5 = (bf16[1,160,384]{2,1,0:T(8,128)(2,1)S(1)}, bf16[1,160,384]{2,1,0:T(8,128)(2,1)S(1)}, u32[]{:S(2)}, u32[]{:S(2)}) collective-permute-start(bf16[1,160,384]{2,1,0:T(8,128)(2,1)S(1)} %collective-permute-done.1.edges), channel_id=1, source_target_pairs={{0,2},{2,0},{4,6},{6,4},{8,10},{10,8},{12,14},{14,12},{16,18},{18,... | collective-permute-start | bytes 368648 | tf_op jit(solution)/shard_map/ppermute | solution.py:356
  10.6 5.7 %collective-permute-start.2 = (bf16[1,160,384]{2,1,0:T(8,128)(2,1)S(1)}, bf16[1,160,384]{2,1,0:T(8,128)(2,1)S(1)}, u32[]{:S(2)}, u32[]{:S(2)}) collective-permute-start(bf16[1,160,384]{2,1,0:T(8,128)(2,1)S(1)} %collective-permute-done.near2), channel_id=1, source_target_pairs={{0,1},{1,0},{2,3},{3,2},{4,5},{5,4},{6,7},{7,6},{8,9},{9,8},{10,11... | collective-permute-start | bytes 368648 | tf_op jit(solution)/shard_map/ppermute | solution.py:367
  12.1 4.6 %collective-permute-start.7 = (bf16[1,160,384]{2,1,0:T(8,128)(2,1)S(1)}, bf16[1,160,384]{2,1,0:T(8,128)(2,1)S(1)}, u32[]{:S(2)}, u32[]{:S(2)}) collective-permute-start(bf16[1,160,384]{2,1,0:T(8,128)(2,1)S(1)} %collective-permute-done.near2), channel_id=1, source_target_pairs={{0,2},{2,0},{4,6},{6,4},{8,10},{10,8},{12,14},{14,12},{16,18},{18,... | collective-permute-start | bytes 368648 | tf_op jit(solution)/shard_map/ppermute | solution.py:356
  14.2 2.5 %collective-permute-start.8 = (bf16[1,160,384]{2,1,0:T(8,128)(2,1)S(1)}, bf16[1,160,384]{2,1,0:T(8,128)(2,1)S(1)}, u32[]{:S(2)}, u32[]{:S(2)}) collective-permute-start(bf16[1,160,384]{2,1,0:T(8,128)(2,1)S(1)} %collective-permute-done.3.rest2), channel_id=1, source_target_pairs={{0,2},{2,0},{4,6},{6,4},{8,10},{10,8},{12,14},{14,12},{16,18},{18,... | collective-permute-start | bytes 368648 | tf_op jit(solution)/shard_map/ppermute | solution.py:356
  16.3 1.3 %collective-permute-start.6 = (bf16[1,160,384]{2,1,0:T(8,128)(2,1)S(1)}, bf16[1,160,384]{2,1,0:T(8,128)(2,1)S(1)}, u32[]{:S(2)}, u32[]{:S(2)}) collective-permute-start(bf16[1,160,384]{2,1,0:T(8,128)(2,1)S(1)} %collective-permute-done.2.edges2), channel_id=1, source_target_pairs={{0,2},{2,0},{4,6},{6,4},{8,10},{10,8},{12,14},{14,12},{16,18},{18,... | collective-permute-start | bytes 368648 | tf_op jit(solution)/shard_map/ppermute | solution.py:356
  17.3 5.8 %copy-start.1 = (bf16[3,384,768]{2,1,0:T(8,128)(2,1)S(1)}, bf16[3,384,768]{2,1,0:T(8,128)(2,1)}, u32[]{:S(2)}) copy-start(bf16[3,384,768]{2,1,0:T(8,128)(2,1)} %param.12) | copy-start | bytes 5308420
  17.3 5.8 %copy-start.2 = (bf16[3,3,384,192]{2,3,1,0:T(8,128)(2,1)S(1)}, bf16[3,3,384,192]{2,3,1,0:T(8,128)(2,1)}, u32[]{:S(2)}) copy-start(bf16[3,3,384,192]{2,3,1,0:T(8,128)(2,1)} %param.14) | copy-start | bytes 3981316
  17.3 5.8 %copy-start.4 = (f32[768]{0:T(1024)S(1)}, f32[768]{0:T(1024)}, u32[]{:S(2)}) copy-start(f32[768]{0:T(1024)} %tbias.5) | copy-start | bytes 9220
  17.3 5.8 %copy-start.6 = (f32[192]{0:T(256)S(1)}, f32[192]{0:T(256)}, u32[]{:S(2)}) copy-start(f32[192]{0:T(256)} %ubias.5) | copy-start | bytes 2308
  18.3 4.8 %collective-permute-start.11 = (bf16[2,160,384]{2,1,0:T(8,128)(2,1)S(1)}, bf16[2,160,384]{2,1,0:T(8,128)(2,1)S(1)}, u32[]{:S(2)}, u32[]{:S(2)}) collective-permute-start(bf16[2,160,384]{2,1,0:T(8,128)(2,1)S(1)} %get-tuple-element.37.own), channel_id=1, source_target_pairs={{0,2},{2,0},{4,6},{6,4},{8,10},{10,8},{12,14},{14,12},{16,18},{18,... | collective-permute-start | bytes 737288 | tf_op jit(solution)/shard_map/ppermute | solution.py:356
  18.7 8.5 %collective-permute-start.10 = (bf16[1,160,384]{2,1,0:T(8,128)(2,1)S(1)}, bf16[1,160,384]{2,1,0:T(8,128)(2,1)S(1)}, u32[]{:S(2)}, u32[]{:S(2)}) collective-permute-start(bf16[1,160,384]{2,1,0:T(8,128)(2,1)S(1)} %get-tuple-element.38), channel_id=1, source_target_pairs={{0,4},{2,6},{4,8},{6,10},{8,12},{10,14},{12,16},{14,18},{16,20},{1... | collective-permute-start | bytes 368648 | tf_op jit(solution)/shard_map/ppermute | solution.py:361
  20.0 8.8 %collective-permute-start.9 = (bf16[1,160,384]{2,1,0:T(8,128)(2,1)S(1)}, bf16[1,160,384]{2,1,0:T(8,128)(2,1)S(1)}, u32[]{:S(2)}, u32[]{:S(2)}) collective-permute-start(bf16[1,160,384]{2,1,0:T(8,128)(2,1)S(1)} %get-tuple-element.38), channel_id=1, source_target_pairs={{0,1},{1,0},{2,3},{3,2},{4,5},{5,4},{6,7},{7,6},{8,9},{9,8},{10,11... | collective-permute-start | bytes 368648 | tf_op jit(solution)/shard_map/ppermute | solution.py:367
  21.5 7.9 %collective-permute-start.12 = (bf16[1,160,384]{2,1,0:T(8,128)(2,1)S(1)}, bf16[1,160,384]{2,1,0:T(8,128)(2,1)S(1)}, u32[]{:S(2)}, u32[]{:S(2)}) collective-permute-start(bf16[1,160,384]{2,1,0:T(8,128)(2,1)S(1)} %get-tuple-element.43), channel_id=1, source_target_pairs={{0,4},{2,6},{4,8},{6,10},{8,12},{10,14},{12,16},{14,18},{16,20},{1... | collective-permute-start | bytes 368648 | tf_op jit(solution)/shard_map/ppermute | solution.py:361
  27.2 4.9 %collective-permute-start.15 = (bf16[1,160,384]{2,1,0:T(8,128)(2,1)S(1)}, bf16[1,160,384]{2,1,0:T(8,128)(2,1)S(1)}, u32[]{:S(2)}, u32[]{:S(2)}) collective-permute-start(bf16[1,160,384]{2,1,0:T(8,128)(2,1)S(1)} %collective-permute-done.10.near2), channel_id=1, source_target_pairs={{0,1},{1,0},{2,3},{3,2},{4,5},{5,4},{6,7},{7,6},{8,9},{9,8},{10,11... | collective-permute-start | bytes 368648 | tf_op jit(solution)/shard_map/ppermute | solution.py:367
  28.9 3.2 %collective-permute-start.17 = (bf16[1,160,384]{2,1,0:T(8,128)(2,1)S(1)}, bf16[1,160,384]{2,1,0:T(8,128)(2,1)S(1)}, u32[]{:S(2)}, u32[]{:S(2)}) collective-permute-start(bf16[1,160,384]{2,1,0:T(8,128)(2,1)S(1)} %collective-permute-done.9.edges), channel_id=1, source_target_pairs={{0,2},{2,0},{4,6},{6,4},{8,10},{10,8},{12,14},{14,12},{16,18},{18,... | collective-permute-start | bytes 368648 | tf_op jit(solution)/shard_map/ppermute | solution.py:356
  29.4 5.5 %collective-permute-start.13 = (bf16[1,160,384]{2,1,0:T(8,128)(2,1)S(1)}, bf16[1,160,384]{2,1,0:T(8,128)(2,1)S(1)}, u32[]{:S(2)}, u32[]{:S(2)}) collective-permute-start(bf16[1,160,384]{2,1,0:T(8,128)(2,1)S(1)} %collective-permute-done.10.near2), channel_id=1, source_target_pairs={{0,2},{2,0},{4,6},{6,4},{8,10},{10,8},{12,14},{14,12},{16,18},{18,... | collective-permute-start | bytes 368648 | tf_op jit(solution)/shard_map/ppermute | solution.py:356
  29.4 5.5 %collective-permute-start.14 = (bf16[1,160,384]{2,1,0:T(8,128)(2,1)S(1)}, bf16[1,160,384]{2,1,0:T(8,128)(2,1)S(1)}, u32[]{:S(2)}, u32[]{:S(2)}) collective-permute-start(bf16[1,160,384]{2,1,0:T(8,128)(2,1)S(1)} %collective-permute-done.12.rest2), channel_id=1, source_target_pairs={{0,2},{2,0},{4,6},{6,4},{8,10},{10,8},{12,14},{14,12},{16,18},{18,... | collective-permute-start | bytes 368648 | tf_op jit(solution)/shard_map/ppermute | solution.py:356
  32.0 2.8 %collective-permute-start.16 = (bf16[1,160,384]{2,1,0:T(8,128)(2,1)S(1)}, bf16[1,160,384]{2,1,0:T(8,128)(2,1)S(1)}, u32[]{:S(2)}, u32[]{:S(2)}) collective-permute-start(bf16[1,160,384]{2,1,0:T(8,128)(2,1)S(1)} %collective-permute-done.15.edges2), channel_id=1, source_target_pairs={{0,2},{2,0},{4,6},{6,4},{8,10},{10,8},{12,14},{14,12},{16,18},{18,... | collective-permute-start | bytes 368648 | tf_op jit(solution)/shard_map/ppermute | solution.py:356

commit v8 on v7

--- a/solution.py
+++ b/solution.py
@@ -242,7 +242,7 @@
 def first_rows(halos, rows):
     inner, outer = inner_rows(halos, rows)
     half = (len(inner) + 1) // 2
-    return inner[:half], inner[half:] + outer
+    return inner[:half], inner[half:], outer
 
 
 def merge_and_first(halos, place, taps, own, odd, tbias, ubias, tw, uw, out_hbm, kept, wide, outs, osems):
@@ -268,9 +268,22 @@
             copy.wait()
 
 
-def first_edges(halos, place, edges, odd_edges, kept, tbias, ubias, tw, uw, out_so_far,
+def first_middle(halos, place, kept, ubias, uw, out_so_far, out_hbm, token, wide, outs, osems):
+    del out_so_far
+    token[...] = jnp.zeros_like(token)
+
+    @pl.when(place[4] == 0)
+    def _():
+        rows = out_hbm.shape[1] // 2
+        out_rows = first_rows(halos, rows)[1]
+        pairs = row_pairs(halos, rows, lambda s, f: kept[f, s - (halos - 1)], out_rows)
+        for copy in up_rows(place, rows, out_rows, pairs, ubias, uw, wide, outs, out_hbm, osems):
+            copy.wait()
+
+
+def first_edges(halos, place, edges, odd_edges, kept, tbias, ubias, tw, uw, token_before, out_so_far,
                 out_hbm, token, doubled, wide, outs, osems):
-    del out_so_far
+    del token_before, out_so_far
     token[...] = jnp.zeros_like(token)
 
     @pl.when(place[4] == 0)
@@ -292,7 +305,7 @@
                 return kept[f, s - lead]
             return doubled[f, 0 if s < lead else halos - 1]
 
-        out_rows = first_rows(halos, rows)[1]
+        out_rows = first_rows(halos, rows)[2]
         pairs = row_pairs(halos, rows, at, out_rows)
         for copy in up_rows(place, rows, out_rows, pairs, ubias, uw, wide, outs, out_hbm, osems):
             copy.wait()
@@ -461,7 +474,7 @@
         ]
 
     rest2 = other(near2, rest, two_back)
-    one, two = (len(o) for o in first_rows(halos, rows))
+    one, two, three = (len(o) for o in first_rows(halos, rows))
     merged, out, kept = call(
         functools.partial(merge_and_first, halos), "merge_taps_and_first_chip_rows", MERGE,
         [VMEM] * 6,
@@ -480,13 +493,22 @@
     near2, rest2, kept = together(near2, rest2, kept)
     even_near = in_chip(near2)
     even_rest = other(even_near, rest2, in_chip)
+    token_spec = (jax.ShapeDtypeStruct((8, LANES), F32), VMEM)
+    out, token = call(
+        functools.partial(first_middle, halos), "first_chip_middle_rows", FIRST,
+        [VMEM] * 3 + [ANY],
+        [out_shape, token_spec],
+        scratch(two, halos)[1:],
+        input_output_aliases={4: 0},
+    )(place, kept, up_bias, merged, out)
+    edges2, token = together(edges2, token)
     out, token = call(
         functools.partial(first_edges, halos), "first_chip_edge_rows", FIRST,
-        [VMEM] * 7 + [ANY],
-        [out_shape, (jax.ShapeDtypeStruct((8, LANES), F32), VMEM)],
-        scratch(two, halos),
-        input_output_aliases={8: 0},
-    )(place, edges, odd_edges, kept, *common, out)
+        [VMEM] * 7 + [ANY] * 2,
+        [out_shape, token_spec],
+        scratch(three, halos),
+        input_output_aliases={9: 0},
+    )(place, edges, odd_edges, kept, *common, token, out)
     even_edges = in_chip(edges2)
     (out,) = call(
         functools.partial(up_kernel, halos), "time_and_up", 1,

time: 36.1 us -> 36.2 us (level)
  waiting for transfers between devices: 7 us -> 4.94 us
  Pallas kernels: 13.3 us -> 15 us
  starting transfers between devices: 15.1 us -> 15.6 us
    ppermute x4, waiting for transfers between devices: 2.36 us -> 0.31 us  [beside(): return lax.ppermute(near, 'tile', [(0, 1), (1, 0)])]
    pallas_call x0 -> x1, Pallas kernels: none -> 2.05 us  [local(): call(functools.partial(first_middle, halos), 'first_chip_middle_rows', FI...]
    ppermute x10, starting transfers between devices: 1.49 us -> 2.01 us  [in_chip(): lax.ppermute(array, 'tm', [(i, i ^ 1) for i in range(lax.axis_size('tm'))])]
  transfers between devices with their start and end apart: 18 -> 18, of which waited for: 7 -> 7; matrix products, arithmetic and copies ran while one was open for 0% -> 0% of each run, Pallas kernels for 30% -> 35%
where the time goes in v8:
time: 36.2 us; the launch traced here: 36.1 us
  starting transfers between devices  15.6 us (43%)
  Pallas kernels  15 us (41%)
  waiting for transfers between devices  4.94 us (14%)
    ppermute x4, starting transfers between devices, two_back(): lax.ppermute(array, 'tm', [(i, (i + 2) % frames) for i in range(frames)])  7.38 us
    ppermute x4, starting transfers between devices, beside(): return lax.ppermute(near, 'tile', [(0, 1), (1, 0)])  6.26 us
    ppermute x4, waiting for transfers between devices, two_back(): lax.ppermute(array, 'tm', [(i, (i + 2) % frames) for i in range(frames)])  4.26 us
    pallas_call x3, Pallas kernels, conv(): return lambda *arrays: step(*arrays)[0]  3.98 us
    pallas_call x1, Pallas kernels, local(): call(functools.partial(merge_and_first, halos), 'merge_taps_and_first_chi...  3.97 us
    pallas_call x1, Pallas kernels, local(): call(functools.partial(first_edges, halos), 'first_chip_edge_rows', FIRST...  2.47 us
    pallas_call x1, Pallas kernels, local(): call(functools.partial(first_middle, halos), 'first_chip_middle_rows', FI...  2.05 us
    ppermute x10, starting transfers between devices, in_chip(): lax.ppermute(array, 'tm', [(i, i ^ 1) for i in range(lax.axis_size('tm'))])  2.01 us
  transfers between devices with their start and end apart: 18, of which 7 were waited for; matrix products, arithmetic and copies ran while one was open for 0% of the time, Pallas kernels for 35%

profile of v8, /device:TPU:0, one launch (start us, length us, event | category | flops | bytes accessed | tf_op | source)
XLA Modules:
  0.0 36.1 jit_solution(1208203292436340438)
XLA Ops:
  0.0 0.1 stack.35.place
  0.1 0.0 copy-start.3
  0.1 0.0 copy-start
  0.1 0.0 copy-start.6
  0.1 0.0 copy-start.7
  0.1 1.1 %split_rows.1 = (bf16[1,160,384]{2,1,0:T(8,128)(2,1)S(1)}, bf16[1,160,384]{2,1,0:T(8,128)(2,1)S(1)}) custom-call(s32[5]{0:T(128)S(1)} %stack.35.place, bf16[2,160,384]{2,1,0:T(8,128)(2,1)} %bitcast.13), custom_call_target="tpu_custom_call" | custom-call | flops 3000000000 | bytes 1000 | tf_op jit(solution)/shard_map/split_rows/pallas_call | solution.py:437
  1.2 3.0 %collective-permute-start = (bf16[1,160,384]{2,1,0:T(8,128)(2,1)S(1)}, bf16[1,160,384]{2,1,0:T(8,128)(2,1)S(1)}, u32[]{:S(2)}, u32[]{:S(2)}) collective-permute-start(bf16[1,160,384]{2,1,0:T(8,128)(2,1)S(1)} %get-tuple-element.33), channel_id=1, source_target_pairs={{0,4},{2,6},{4,8},{6,10},{8,12},{10,14},{12,16},{14,18},{16,20},{1... | collective-permute-start | bytes 368648 | tf_op jit(solution)/shard_map/ppermute | solution.py:374
  4.2 1.5 %collective-permute-start.1 = (bf16[1,160,384]{2,1,0:T(8,128)(2,1)S(1)}, bf16[1,160,384]{2,1,0:T(8,128)(2,1)S(1)}, u32[]{:S(2)}, u32[]{:S(2)}) collective-permute-start(bf16[1,160,384]{2,1,0:T(8,128)(2,1)S(1)} %get-tuple-element.33), channel_id=1, source_target_pairs={{0,1},{1,0},{2,3},{3,2},{4,5},{5,4},{6,7},{7,6},{8,9},{9,8},{10,11... | collective-permute-start | bytes 368648 | tf_op jit(solution)/shard_map/ppermute | solution.py:380
  5.8 0.0 copy-done.3
  5.8 0.0 collective-permute-start.4
  5.8 1.5 %collective-permute-start.3 = (bf16[1,160,384]{2,1,0:T(8,128)(2,1)S(1)}, bf16[1,160,384]{2,1,0:T(8,128)(2,1)S(1)}, u32[]{:S(2)}, u32[]{:S(2)}) collective-permute-start(bf16[1,160,384]{2,1,0:T(8,128)(2,1)S(1)} %get-tuple-element.36), channel_id=1, source_target_pairs={{0,4},{2,6},{4,8},{6,10},{8,12},{10,14},{12,16},{14,18},{16,20},{1... | collective-permute-start | bytes 368648 | tf_op jit(solution)/shard_map/ppermute | solution.py:374
  7.3 0.0 copy-done
  7.3 0.0 copy-done.6
  7.3 0.0 copy-done.7
  7.3 1.5 %conv_own_frame.1.before = f32[2,160,384]{2,1,0:T(8,128)S(1)} custom-call(s32[5]{0:T(128)S(1)} %stack.35.place, bf16[2,160,384]{2,1,0:T(8,128)(2,1)S(1)} %bitcast.15, f32[384]{0:T(512)S(1)} %copy-done.6, f32[384]{0:T(512)S(1)} %copy-done.7, bf16[3,3,3,384,384]{4,3,2,1,0:T(8,128)(2,1)S(1)} %copy-done), custom_call_target="tpu_custom_call" | custom-call | flops 600000000 | bytes 1000 | tf_op jit(solution)/shard_map/conv_own_frame/pallas_call | solution.py:425
  8.8 1.8 %collective-permute-done.near2 = bf16[1,160,384]{2,1,0:T(8,128)(2,1)S(1)} collective-permute-done((bf16[1,160,384]{2,1,0:T(8,128)(2,1)S(1)}, bf16[1,160,384]{2,1,0:T(8,128)(2,1)S(1)}, u32[]{:S(2)}, u32[]{:S(2)}) %collective-permute-start) | collective-permute-done | bytes 122912 | tf_op jit(solution)/shard_map/ppermute | solution.py:374
  10.6 0.0 collective-permute-done.1.edges
  10.6 0.0 collective-permute-start.5
  10.6 1.5 %collective-permute-start.2 = (bf16[1,160,384]{2,1,0:T(8,128)(2,1)S(1)}, bf16[1,160,384]{2,1,0:T(8,128)(2,1)S(1)}, u32[]{:S(2)}, u32[]{:S(2)}) collective-permute-start(bf16[1,160,384]{2,1,0:T(8,128)(2,1)S(1)} %collective-permute-done.near2), channel_id=1, source_target_pairs={{0,1},{1,0},{2,3},{3,2},{4,5},{5,4},{6,7},{7,6},{8,9},{9,8},{10,11... | collective-permute-start | bytes 368648 | tf_op jit(solution)/shard_map/ppermute | solution.py:380
  12.1 0.2 collective-permute-start.7
  12.3 1.8 %collective-permute-done.3.rest2 = bf16[1,160,384]{2,1,0:T(8,128)(2,1)S(1)} collective-permute-done((bf16[1,160,384]{2,1,0:T(8,128)(2,1)S(1)}, bf16[1,160,384]{2,1,0:T(8,128)(2,1)S(1)}, u32[]{:S(2)}, u32[]{:S(2)}) %collective-permute-start.3) | collective-permute-done | bytes 122912 | tf_op jit(solution)/shard_map/ppermute | solution.py:374
  14.2 0.0 collective-permute-start.8
  14.2 0.0 collective-permute-done.5.odd_edges
  14.2 0.0 collective-permute-done.4.odd
  14.2 1.9 %conv_two_back.1.before = f32[2,160,384]{2,1,0:T(8,128)S(1)} custom-call(s32[5]{0:T(128)S(1)} %stack.35.place, bf16[1,160,384]{2,1,0:T(8,128)(2,1)S(1)} %collective-permute-done.near2, bf16[1,160,384]{2,1,0:T(8,128)(2,1)S(1)} %collective-permute-done.3.rest2, bf16[2,160,384]{2,1,0:T(8,128)(2,1)S(1)} %collective-permute-done.4.odd, ...), custom_call_target="tpu_custom_call" | custom-call | flops 600000000 | bytes 1000 | tf_op jit(solution)/shard_map/conv_two_back/pallas_call | solution.py:425
  16.1 0.2 collective-permute-done.2.edges2
  16.3 0.3 collective-permute-start.6
  16.7 0.0 collective-permute-done.7.even_near
  16.7 0.0 collective-permute-done.8.even_rest
  16.7 0.6 %conv_one_back.1.before = f32[2,160,384]{2,1,0:T(8,128)S(1)} custom-call(s32[5]{0:T(128)S(1)} %stack.35.place, bf16[1,160,384]{2,1,0:T(8,128)(2,1)S(1)} %collective-permute-done.7.even_near, bf16[1,160,384]{2,1,0:T(8,128)(2,1)S(1)} %collective-permute-done.8.even_rest, bf16[2,160,384]{2,1,0:T(8,128)(2,1)S(1)} %collective-permute-done.4.odd, ...), custom_call_target="tpu_custom_call" | custom-call | flops 3000000000 | bytes 1000 | tf_op jit(solution)/shard_map/conv_one_back/pallas_call | solution.py:425
  17.3 0.0 copy-start.1
  17.3 0.0 copy-start.2
  17.3 0.0 copy-start.4
  17.3 0.0 copy-start.5
  17.3 0.3 collective-permute-done.6.even_edges
  17.7 0.6 %conv_edge_rows.1 = (bf16[2,160,384]{2,1,0:T(8,128)(2,1)S(1)}, bf16[1,160,384]{2,1,0:T(8,128)(2,1)S(1)}, bf16[1,160,384]{2,1,0:T(8,128)(2,1)S(1)}) custom-call(s32[5]{0:T(128)S(1)} %stack.35.place, bf16[1,160,384]{2,1,0:T(8,128)(2,1)S(1)} %collective-permute-done.1.edges, bf16[1,160,384]{2,1,0:T(8,128)(2,1)S(1)} %collective-permute-done.2.edges2, ...), custom_call_target="tpu_custom_call" | custom-call | flops 3000000000 | bytes 1000 | tf_op jit(solution)/shard_map/conv_edge_rows/pallas_call | solution.py:454
  18.3 0.4 %collective-permute-start.11 = (bf16[2,160,384]{2,1,0:T(8,128)(2,1)S(1)}, bf16[2,160,384]{2,1,0:T(8,128)(2,1)S(1)}, u32[]{:S(2)}, u32[]{:S(2)}) collective-permute-start(bf16[2,160,384]{2,1,0:T(8,128)(2,1)S(1)} %get-tuple-element.41.own), channel_id=1, source_target_pairs={{0,2},{2,0},{4,6},{6,4},{8,10},{10,8},{12,14},{14,12},{16,18},{18,... | collective-permute-start | bytes 737288 | tf_op jit(solution)/shard_map/ppermute | solution.py:369
  18.7 1.3 %collective-permute-start.10 = (bf16[1,160,384]{2,1,0:T(8,128)(2,1)S(1)}, bf16[1,160,384]{2,1,0:T(8,128)(2,1)S(1)}, u32[]{:S(2)}, u32[]{:S(2)}) collective-permute-start(bf16[1,160,384]{2,1,0:T(8,128)(2,1)S(1)} %get-tuple-element.42), channel_id=1, source_target_pairs={{0,4},{2,6},{4,8},{6,10},{8,12},{10,14},{12,16},{14,18},{16,20},{1... | collective-permute-start | bytes 368648 | tf_op jit(solution)/shard_map/ppermute | solution.py:374
  20.0 1.5 %collective-permute-start.9 = (bf16[1,160,384]{2,1,0:T(8,128)(2,1)S(1)}, bf16[1,160,384]{2,1,0:T(8,128)(2,1)S(1)}, u32[]{:S(2)}, u32[]{:S(2)}) collective-permute-start(bf16[1,160,384]{2,1,0:T(8,128)(2,1)S(1)} %get-tuple-element.42), channel_id=1, source_target_pairs={{0,1},{1,0},{2,3},{3,2},{4,5},{5,4},{6,7},{7,6},{8,9},{9,8},{10,11... | collective-permute-start | bytes 368648 | tf_op jit(solution)/shard_map/ppermute | solution.py:380
  21.5 1.5 %collective-permute-start.12 = (bf16[1,160,384]{2,1,0:T(8,128)(2,1)S(1)}, bf16[1,160,384]{2,1,0:T(8,128)(2,1)S(1)}, u32[]{:S(2)}, u32[]{:S(2)}) collective-permute-start(bf16[1,160,384]{2,1,0:T(8,128)(2,1)S(1)} %get-tuple-element.47), channel_id=1, source_target_pairs={{0,4},{2,6},{4,8},{6,10},{8,12},{10,14},{12,16},{14,18},{16,20},{1... | collective-permute-start | bytes 368648 | tf_op jit(solution)/shard_map/ppermute | solution.py:374
  23.0 0.0 collective-permute-done.11.odd
  23.0 0.0 copy-done.1
  23.0 0.0 copy-done.2
  23.0 0.0 copy-done.4
  23.1 0.0 copy-done.5
  23.1 4.0 %merge_taps_and_first_chip_rows.1 = (bf16[2,768,768]{2,1,0:T(8,128)(2,1)S(1)}, bf16[2,4,192,320]{3,2,1,0:T(8,128)(2,1)}, bf16[2,2,160,384]{3,2,1,0:T(8,128)(2,1)S(1)}) custom-call(s32[5]{0:T(128)S(1)} %stack.35.place, bf16[3,3,192,384]{3,2,1,0:T(8,128)(2,1)S(1)} %bitcast.12, bf16[2,160,384]{2,1,0:T(8,128)(2,1)S(1)} %get-tuple-element.41.own, ...), custom_call_target="tpu_custom_call" | custom-call | flops 600000000 | bytes 1000 | tf_op jit(solution)/shard_map/merge_taps_and_first_chip_rows/pallas_call | solution.py:478
  27.0 0.1 collective-permute-done.10.near2
  27.2 1.7 %collective-permute-start.15 = (bf16[1,160,384]{2,1,0:T(8,128)(2,1)S(1)}, bf16[1,160,384]{2,1,0:T(8,128)(2,1)S(1)}, u32[]{:S(2)}, u32[]{:S(2)}) collective-permute-start(bf16[1,160,384]{2,1,0:T(8,128)(2,1)S(1)} %collective-permute-done.10.near2), channel_id=1, source_target_pairs={{0,1},{1,0},{2,3},{3,2},{4,5},{5,4},{6,7},{7,6},{8,9},{9,8},{10,11... | collective-permute-start | bytes 368648 | tf_op jit(solution)/shard_map/ppermute | solution.py:380
  28.9 0.0 collective-permute-done.9.edges
  28.9 0.5 %collective-permute-done.12.rest2 = bf16[1,160,384]{2,1,0:T(8,128)(2,1)S(1)} collective-permute-done((bf16[1,160,384]{2,1,0:T(8,128)(2,1)S(1)}, bf16[1,160,384]{2,1,0:T(8,128)(2,1)S(1)}, u32[]{:S(2)}, u32[]{:S(2)}) %collective-permute-start.12) | collective-permute-done | bytes 122912 | tf_op jit(solution)/shard_map/ppermute | solution.py:374
  29.4 0.0 collective-permute-start.17
  29.4 0.5 %collective-permute-start.13 = (bf16[1,160,384]{2,1,0:T(8,128)(2,1)S(1)}, bf16[1,160,384]{2,1,0:T(8,128)(2,1)S(1)}, u32[]{:S(2)}, u32[]{:S(2)}) collective-permute-start(bf16[1,160,384]{2,1,0:T(8,128)(2,1)S(1)} %collective-permute-done.10.near2), channel_id=1, source_target_pairs={{0,2},{2,0},{4,6},{6,4},{8,10},{10,8},{12,14},{14,12},{16,18},{18,... | collective-permute-start | bytes 368648 | tf_op jit(solution)/shard_map/ppermute | solution.py:369
  29.9 0.0 collective-permute-start.14
  29.9 2.0 %first_chip_middle_rows.1 = (bf16[2,4,192,320]{3,2,1,0:T(8,128)(2,1)}, f32[8,128]{1,0:T(8,128)S(1)}) custom-call(s32[5]{0:T(128)S(1)} %stack.35.place, bf16[2,2,160,384]{3,2,1,0:T(8,128)(2,1)S(1)} %get-tuple-element.52.kept, f32[192]{0:T(256)S(1)} %copy-done.5, bf16[2,768,768]{2,1,0:T(8,128)(2,1)S(1)} %get-tuple-element.53.uw, ...), custom_call_target="tpu_custom_call", output_to_operand_aliasing={{0}: (4, {})} | custom-call | flops 30000000 | bytes 1000 | tf_op jit(solution)/shard_map/first_chip_middle_rows/pallas_call | solution.py:497
  32.0 0.1 collective-permute-done.15.edges2
  32.0 0.5 %collective-permute-start.16 = (bf16[1,160,384]{2,1,0:T(8,128)(2,1)S(1)}, bf16[1,160,384]{2,1,0:T(8,128)(2,1)S(1)}, u32[]{:S(2)}, u32[]{:S(2)}) collective-permute-start(bf16[1,160,384]{2,1,0:T(8,128)(2,1)S(1)} %collective-permute-done.15.edges2), channel_id=1, source_target_pairs={{0,2},{2,0},{4,6},{6,4},{8,10},{10,8},{12,14},{14,12},{16,18},{18,... | collective-permute-start | bytes 368648 | tf_op jit(solution)/shard_map/ppermute | solution.py:369
  32.6 0.0 collective-permute-done.17.odd_edges
  32.6 2.5 %first_chip_edge_rows.1 = (bf16[2,4,192,320]{3,2,1,0:T(8,128)(2,1)}, f32[8,128]{1,0:T(8,128)S(1)}) custom-call(s32[5]{0:T(128)S(1)} %stack.35.place, bf16[1,160,384]{2,1,0:T(8,128)(2,1)S(1)} %collective-permute-done.9.edges, bf16[1,160,384]{2,1,0:T(8,128)(2,1)S(1)} %collective-permute-done.17.odd_edges, ...), custom_call_target="tpu_custom_call", output_to_operand_aliasing={{0}: (9, {})} | custom-call | flops 30000000 | bytes 1000 | tf_op jit(solution)/shard_map/first_chip_edge_rows/pallas_call | solution.py:505
  35.0 0.0 collective-permute-done.13.even_near
  35.1 0.0 collective-permute-done.14.even_rest
  35.1 0.0 collective-permute-done.16.even_edges
  35.1 0.8 %time_and_up.1 = bf16[2,4,192,320]{3,2,1,0:T(8,128)(2,1)} custom-call(s32[5]{0:T(128)S(1)} %stack.35.place, bf16[2,160,384]{2,1,0:T(8,128)(2,1)S(1)} %get-tuple-element.41.own, bf16[1,160,384]{2,1,0:T(8,128)(2,1)S(1)} %collective-permute-done.10.near2, bf16[1,160,384]{2,1,0:T(8,128)(2,1)S(1)} %collective-permute-done.12.rest2, ...), custom_call_target="tpu_custom_call", output_to_operand_aliasing={{}: (16, {})} | custom-call | flops 3000000000 | bytes 1000 | tf_op jit(solution)/shard_map/time_and_up/pallas_call | solution.py:513
Async XLA Ops:
  0.1 5.7 %copy-start.3 = (bf16[1,2,160,384]{3,2,1,0:T(8,128)(2,1)S(1)}, bf16[1,2,160,384]{3,2,1,0:T(8,128)(2,1)}, u32[]{:S(2)}) copy-start(bf16[1,2,160,384]{3,2,1,0:T(8,128)(2,1)} %param.8) | copy-start | bytes 737284
  0.1 7.2 %copy-start = (bf16[3,3,3,384,384]{4,3,2,1,0:T(8,128)(2,1)S(1)}, bf16[3,3,3,384,384]{4,3,2,1,0:T(8,128)(2,1)}, u32[]{:S(2)}) copy-start(bf16[3,3,3,384,384]{4,3,2,1,0:T(8,128)(2,1)} %weight.7) | copy-start | bytes 23887876
  0.1 7.2 %copy-start.6 = (f32[384]{0:T(512)S(1)}, f32[384]{0:T(512)}, u32[]{:S(2)}) copy-start(f32[384]{0:T(512)} %gain.7) | copy-start | bytes 4612
  0.1 7.2 %copy-start.7 = (f32[384]{0:T(512)S(1)}, f32[384]{0:T(512)}, u32[]{:S(2)}) copy-start(f32[384]{0:T(512)} %bias.1) | copy-start | bytes 4612
  1.2 9.4 %collective-permute-start = (bf16[1,160,384]{2,1,0:T(8,128)(2,1)S(1)}, bf16[1,160,384]{2,1,0:T(8,128)(2,1)S(1)}, u32[]{:S(2)}, u32[]{:S(2)}) collective-permute-start(bf16[1,160,384]{2,1,0:T(8,128)(2,1)S(1)} %get-tuple-element.33), channel_id=1, source_target_pairs={{0,4},{2,6},{4,8},{6,10},{8,12},{10,14},{12,16},{14,18},{16,20},{1... | collective-permute-start | bytes 368648 | tf_op jit(solution)/shard_map/ppermute | solution.py:374
  4.2 6.4 %collective-permute-start.1 = (bf16[1,160,384]{2,1,0:T(8,128)(2,1)S(1)}, bf16[1,160,384]{2,1,0:T(8,128)(2,1)S(1)}, u32[]{:S(2)}, u32[]{:S(2)}) collective-permute-start(bf16[1,160,384]{2,1,0:T(8,128)(2,1)S(1)} %get-tuple-element.33), channel_id=1, source_target_pairs={{0,1},{1,0},{2,3},{3,2},{4,5},{5,4},{6,7},{7,6},{8,9},{9,8},{10,11... | collective-permute-start | bytes 368648 | tf_op jit(solution)/shard_map/ppermute | solution.py:380
  5.8 8.4 %collective-permute-start.4 = (bf16[2,160,384]{2,1,0:T(8,128)(2,1)S(1)}, bf16[2,160,384]{2,1,0:T(8,128)(2,1)S(1)}, u32[]{:S(2)}, u32[]{:S(2)}) collective-permute-start(bf16[2,160,384]{2,1,0:T(8,128)(2,1)S(1)} %bitcast.14), channel_id=1, source_target_pairs={{0,2},{2,0},{4,6},{6,4},{8,10},{10,8},{12,14},{14,12},{16,18},{18,... | collective-permute-start | bytes 737288 | tf_op jit(solution)/shard_map/ppermute | solution.py:369
  5.8 8.4 %collective-permute-start.3 = (bf16[1,160,384]{2,1,0:T(8,128)(2,1)S(1)}, bf16[1,160,384]{2,1,0:T(8,128)(2,1)S(1)}, u32[]{:S(2)}, u32[]{:S(2)}) collective-permute-start(bf16[1,160,384]{2,1,0:T(8,128)(2,1)S(1)} %get-tuple-element.36), channel_id=1, source_target_pairs={{0,4},{2,6},{4,8},{6,10},{8,12},{10,14},{12,16},{14,18},{16,20},{1... | collective-permute-start | bytes 368648 | tf_op jit(solution)/shard_map/ppermute | solution.py:374
  10.6 3.6 %collective-permute-start.5 = (bf16[1,160,384]{2,1,0:T(8,128)(2,1)S(1)}, bf16[1,160,384]{2,1,0:T(8,128)(2,1)S(1)}, u32[]{:S(2)}, u32[]{:S(2)}) collective-permute-start(bf16[1,160,384]{2,1,0:T(8,128)(2,1)S(1)} %collective-permute-done.1.edges), channel_id=1, source_target_pairs={{0,2},{2,0},{4,6},{6,4},{8,10},{10,8},{12,14},{14,12},{16,18},{18,... | collective-permute-start | bytes 368648 | tf_op jit(solution)/shard_map/ppermute | solution.py:369
  10.6 5.7 %collective-permute-start.2 = (bf16[1,160,384]{2,1,0:T(8,128)(2,1)S(1)}, bf16[1,160,384]{2,1,0:T(8,128)(2,1)S(1)}, u32[]{:S(2)}, u32[]{:S(2)}) collective-permute-start(bf16[1,160,384]{2,1,0:T(8,128)(2,1)S(1)} %collective-permute-done.near2), channel_id=1, source_target_pairs={{0,1},{1,0},{2,3},{3,2},{4,5},{5,4},{6,7},{7,6},{8,9},{9,8},{10,11... | collective-permute-start | bytes 368648 | tf_op jit(solution)/shard_map/ppermute | solution.py:380
  12.1 4.6 %collective-permute-start.7 = (bf16[1,160,384]{2,1,0:T(8,128)(2,1)S(1)}, bf16[1,160,384]{2,1,0:T(8,128)(2,1)S(1)}, u32[]{:S(2)}, u32[]{:S(2)}) collective-permute-start(bf16[1,160,384]{2,1,0:T(8,128)(2,1)S(1)} %collective-permute-done.near2), channel_id=1, source_target_pairs={{0,2},{2,0},{4,6},{6,4},{8,10},{10,8},{12,14},{14,12},{16,18},{18,... | collective-permute-start | bytes 368648 | tf_op jit(solution)/shard_map/ppermute | solution.py:369
  14.2 2.5 %collective-permute-start.8 = (bf16[1,160,384]{2,1,0:T(8,128)(2,1)S(1)}, bf16[1,160,384]{2,1,0:T(8,128)(2,1)S(1)}, u32[]{:S(2)}, u32[]{:S(2)}) collective-permute-start(bf16[1,160,384]{2,1,0:T(8,128)(2,1)S(1)} %collective-permute-done.3.rest2), channel_id=1, source_target_pairs={{0,2},{2,0},{4,6},{6,4},{8,10},{10,8},{12,14},{14,12},{16,18},{18,... | collective-permute-start | bytes 368648 | tf_op jit(solution)/shard_map/ppermute | solution.py:369
  16.3 1.3 %collective-permute-start.6 = (bf16[1,160,384]{2,1,0:T(8,128)(2,1)S(1)}, bf16[1,160,384]{2,1,0:T(8,128)(2,1)S(1)}, u32[]{:S(2)}, u32[]{:S(2)}) collective-permute-start(bf16[1,160,384]{2,1,0:T(8,128)(2,1)S(1)} %collective-permute-done.2.edges2), channel_id=1, source_target_pairs={{0,2},{2,0},{4,6},{6,4},{8,10},{10,8},{12,14},{14,12},{16,18},{18,... | collective-permute-start | bytes 368648 | tf_op jit(solution)/shard_map/ppermute | solution.py:369
  17.3 5.8 %copy-start.1 = (bf16[3,384,768]{2,1,0:T(8,128)(2,1)S(1)}, bf16[3,384,768]{2,1,0:T(8,128)(2,1)}, u32[]{:S(2)}) copy-start(bf16[3,384,768]{2,1,0:T(8,128)(2,1)} %param.12) | copy-start | bytes 5308420
  17.3 5.8 %copy-start.2 = (bf16[3,3,384,192]{2,3,1,0:T(8,128)(2,1)S(1)}, bf16[3,3,384,192]{2,3,1,0:T(8,128)(2,1)}, u32[]{:S(2)}) copy-start(bf16[3,3,384,192]{2,3,1,0:T(8,128)(2,1)} %param.14) | copy-start | bytes 3981316
  17.3 5.8 %copy-start.4 = (f32[768]{0:T(1024)S(1)}, f32[768]{0:T(1024)}, u32[]{:S(2)}) copy-start(f32[768]{0:T(1024)} %tbias.5) | copy-start | bytes 9220
  17.3 5.8 %copy-start.5 = (f32[192]{0:T(256)S(1)}, f32[192]{0:T(256)}, u32[]{:S(2)}) copy-start(f32[192]{0:T(256)} %ubias.7) | copy-start | bytes 2308
  18.3 4.8 %collective-permute-start.11 = (bf16[2,160,384]{2,1,0:T(8,128)(2,1)S(1)}, bf16[2,160,384]{2,1,0:T(8,128)(2,1)S(1)}, u32[]{:S(2)}, u32[]{:S(2)}) collective-permute-start(bf16[2,160,384]{2,1,0:T(8,128)(2,1)S(1)} %get-tuple-element.41.own), channel_id=1, source_target_pairs={{0,2},{2,0},{4,6},{6,4},{8,10},{10,8},{12,14},{14,12},{16,18},{18,... | collective-permute-start | bytes 737288 | tf_op jit(solution)/shard_map/ppermute | solution.py:369
  18.7 8.5 %collective-permute-start.10 = (bf16[1,160,384]{2,1,0:T(8,128)(2,1)S(1)}, bf16[1,160,384]{2,1,0:T(8,128)(2,1)S(1)}, u32[]{:S(2)}, u32[]{:S(2)}) collective-permute-start(bf16[1,160,384]{2,1,0:T(8,128)(2,1)S(1)} %get-tuple-element.42), channel_id=1, source_target_pairs={{0,4},{2,6},{4,8},{6,10},{8,12},{10,14},{12,16},{14,18},{16,20},{1... | collective-permute-start | bytes 368648 | tf_op jit(solution)/shard_map/ppermute | solution.py:374
  20.0 8.8 %collective-permute-start.9 = (bf16[1,160,384]{2,1,0:T(8,128)(2,1)S(1)}, bf16[1,160,384]{2,1,0:T(8,128)(2,1)S(1)}, u32[]{:S(2)}, u32[]{:S(2)}) collective-permute-start(bf16[1,160,384]{2,1,0:T(8,128)(2,1)S(1)} %get-tuple-element.42), channel_id=1, source_target_pairs={{0,1},{1,0},{2,3},{3,2},{4,5},{5,4},{6,7},{7,6},{8,9},{9,8},{10,11... | collective-permute-start | bytes 368648 | tf_op jit(solution)/shard_map/ppermute | solution.py:380
  21.5 7.9 %collective-permute-start.12 = (bf16[1,160,384]{2,1,0:T(8,128)(2,1)S(1)}, bf16[1,160,384]{2,1,0:T(8,128)(2,1)S(1)}, u32[]{:S(2)}, u32[]{:S(2)}) collective-permute-start(bf16[1,160,384]{2,1,0:T(8,128)(2,1)S(1)} %get-tuple-element.47), channel_id=1, source_target_pairs={{0,4},{2,6},{4,8},{6,10},{8,12},{10,14},{12,16},{14,18},{16,20},{1... | collective-permute-start | bytes 368648 | tf_op jit(solution)/shard_map/ppermute | solution.py:374
  27.2 4.9 %collective-permute-start.15 = (bf16[1,160,384]{2,1,0:T(8,128)(2,1)S(1)}, bf16[1,160,384]{2,1,0:T(8,128)(2,1)S(1)}, u32[]{:S(2)}, u32[]{:S(2)}) collective-permute-start(bf16[1,160,384]{2,1,0:T(8,128)(2,1)S(1)} %collective-permute-done.10.near2), channel_id=1, source_target_pairs={{0,1},{1,0},{2,3},{3,2},{4,5},{5,4},{6,7},{7,6},{8,9},{9,8},{10,11... | collective-permute-start | bytes 368648 | tf_op jit(solution)/shard_map/ppermute | solution.py:380
  29.4 3.2 %collective-permute-start.17 = (bf16[1,160,384]{2,1,0:T(8,128)(2,1)S(1)}, bf16[1,160,384]{2,1,0:T(8,128)(2,1)S(1)}, u32[]{:S(2)}, u32[]{:S(2)}) collective-permute-start(bf16[1,160,384]{2,1,0:T(8,128)(2,1)S(1)} %collective-permute-done.9.edges), channel_id=1, source_target_pairs={{0,2},{2,0},{4,6},{6,4},{8,10},{10,8},{12,14},{14,12},{16,18},{18,... | collective-permute-start | bytes 368648 | tf_op jit(solution)/shard_map/ppermute | solution.py:369
  29.4 5.6 %collective-permute-start.13 = (bf16[1,160,384]{2,1,0:T(8,128)(2,1)S(1)}, bf16[1,160,384]{2,1,0:T(8,128)(2,1)S(1)}, u32[]{:S(2)}, u32[]{:S(2)}) collective-permute-start(bf16[1,160,384]{2,1,0:T(8,128)(2,1)S(1)} %collective-permute-done.10.near2), channel_id=1, source_target_pairs={{0,2},{2,0},{4,6},{6,4},{8,10},{10,8},{12,14},{14,12},{16,18},{18,... | collective-permute-start | bytes 368648 | tf_op jit(solution)/shard_map/ppermute | solution.py:369
  29.9 5.1 %collective-permute-start.14 = (bf16[1,160,384]{2,1,0:T(8,128)(2,1)S(1)}, bf16[1,160,384]{2,1,0:T(8,128)(2,1)S(1)}, u32[]{:S(2)}, u32[]{:S(2)}) collective-permute-start(bf16[1,160,384]{2,1,0:T(8,128)(2,1)S(1)} %collective-permute-done.12.rest2), channel_id=1, source_target_pairs={{0,2},{2,0},{4,6},{6,4},{8,10},{10,8},{12,14},{14,12},{16,18},{18,... | collective-permute-start | bytes 368648 | tf_op jit(solution)/shard_map/ppermute | solution.py:369
  32.0 3.0 %collective-permute-start.16 = (bf16[1,160,384]{2,1,0:T(8,128)(2,1)S(1)}, bf16[1,160,384]{2,1,0:T(8,128)(2,1)S(1)}, u32[]{:S(2)}, u32[]{:S(2)}) collective-permute-start(bf16[1,160,384]{2,1,0:T(8,128)(2,1)S(1)} %collective-permute-done.15.edges2), channel_id=1, source_target_pairs={{0,2},{2,0},{4,6},{6,4},{8,10},{10,8},{12,14},{14,12},{16,18},{18,... | collective-permute-start | bytes 368648 | tf_op jit(solution)/shard_map/ppermute | solution.py:369

commit v9 on v7

--- a/solution.py
+++ b/solution.py
@@ -391,7 +391,7 @@
             in_specs=[SMEM] + ins,
             out_specs=tuple(s for _, s in outs),
             scratch_shapes=scratch,
-            compiler_params=pltpu.CompilerParams(vmem_limit_bytes=20 << 20),
+            compiler_params=pltpu.CompilerParams(vmem_limit_bytes=32 << 20),
             cost_estimate=pl.CostEstimate(
                 flops=int(SHARE * share), bytes_accessed=1000, transcendentals=0
             ),

time: 36.1 us -> 36.1 us (level)
  no operation moved by 1% of the time
where the time goes in v9:
time: 36.1 us; the launch traced here: 35.9 us
  starting transfers between devices  15.1 us (42%)
  Pallas kernels  13.3 us (37%)
  waiting for transfers between devices  7 us (19%)
    ppermute x4, starting transfers between devices, two_back(): lax.ppermute(array, 'tm', [(i, (i + 2) % frames) for i in range(frames)])  7.37 us
    ppermute x4, starting transfers between devices, beside(): return lax.ppermute(near, 'tile', [(0, 1), (1, 0)])  6.26 us
    ppermute x4, waiting for transfers between devices, two_back(): lax.ppermute(array, 'tm', [(i, (i + 2) % frames) for i in range(frames)])  4.26 us
    pallas_call x3, Pallas kernels, conv(): return lambda *arrays: step(*arrays)[0]  3.98 us
    pallas_call x1, Pallas kernels, local(): call(functools.partial(merge_and_first, halos), 'merge_taps_and_first_chi...  3.96 us
    pallas_call x1, Pallas kernels, local(): call(functools.partial(first_edges, halos), 'first_chip_edge_rows', FIRST...  2.81 us
    ppermute x4, waiting for transfers between devices, beside(): return lax.ppermute(near, 'tile', [(0, 1), (1, 0)])  2.36 us
    ppermute x10, starting transfers between devices, in_chip(): lax.ppermute(array, 'tm', [(i, i ^ 1) for i in range(lax.axis_size('tm'))])  1.49 us
  transfers between devices with their start and end apart: 18, of which 7 were waited for; matrix products, arithmetic and copies ran while one was open for 0% of the time, Pallas kernels for 30%

profile of v9, /device:TPU:0, one launch (start us, length us, event | category | flops | bytes accessed | tf_op | source)
XLA Modules:
  0.0 35.9 jit_solution(13128017746944910078)
XLA Ops:
  0.0 0.1 stack.35.place
  0.1 0.0 copy-start.3
  0.1 0.0 copy-start
  0.1 0.0 copy-start.5
  0.1 0.0 copy-start.7
  0.1 1.1 %split_rows.1 = (bf16[1,160,384]{2,1,0:T(8,128)(2,1)S(1)}, bf16[1,160,384]{2,1,0:T(8,128)(2,1)S(1)}) custom-call(s32[5]{0:T(128)S(1)} %stack.35.place, bf16[2,160,384]{2,1,0:T(8,128)(2,1)} %bitcast.13), custom_call_target="tpu_custom_call" | custom-call | flops 3000000000 | bytes 1000 | tf_op jit(solution)/shard_map/split_rows/pallas_call | solution.py:424
  1.2 3.0 %collective-permute-start = (bf16[1,160,384]{2,1,0:T(8,128)(2,1)S(1)}, bf16[1,160,384]{2,1,0:T(8,128)(2,1)S(1)}, u32[]{:S(2)}, u32[]{:S(2)}) collective-permute-start(bf16[1,160,384]{2,1,0:T(8,128)(2,1)S(1)} %get-tuple-element.29), channel_id=1, source_target_pairs={{0,4},{2,6},{4,8},{6,10},{8,12},{10,14},{12,16},{14,18},{16,20},{1... | collective-permute-start | bytes 368648 | tf_op jit(solution)/shard_map/ppermute | solution.py:361
  4.2 1.5 %collective-permute-start.1 = (bf16[1,160,384]{2,1,0:T(8,128)(2,1)S(1)}, bf16[1,160,384]{2,1,0:T(8,128)(2,1)S(1)}, u32[]{:S(2)}, u32[]{:S(2)}) collective-permute-start(bf16[1,160,384]{2,1,0:T(8,128)(2,1)S(1)} %get-tuple-element.29), channel_id=1, source_target_pairs={{0,1},{1,0},{2,3},{3,2},{4,5},{5,4},{6,7},{7,6},{8,9},{9,8},{10,11... | collective-permute-start | bytes 368648 | tf_op jit(solution)/shard_map/ppermute | solution.py:367
  5.8 0.0 copy-done.3
  5.8 0.0 collective-permute-start.4
  5.8 1.5 %collective-permute-start.3 = (bf16[1,160,384]{2,1,0:T(8,128)(2,1)S(1)}, bf16[1,160,384]{2,1,0:T(8,128)(2,1)S(1)}, u32[]{:S(2)}, u32[]{:S(2)}) collective-permute-start(bf16[1,160,384]{2,1,0:T(8,128)(2,1)S(1)} %get-tuple-element.32), channel_id=1, source_target_pairs={{0,4},{2,6},{4,8},{6,10},{8,12},{10,14},{12,16},{14,18},{16,20},{1... | collective-permute-start | bytes 368648 | tf_op jit(solution)/shard_map/ppermute | solution.py:361
  7.3 0.0 copy-done
  7.3 0.0 copy-done.5
  7.3 0.0 copy-done.7
  7.3 1.5 %conv_own_frame.1.before = f32[2,160,384]{2,1,0:T(8,128)S(1)} custom-call(s32[5]{0:T(128)S(1)} %stack.35.place, bf16[2,160,384]{2,1,0:T(8,128)(2,1)S(1)} %bitcast.15, f32[384]{0:T(512)S(1)} %copy-done.5, f32[384]{0:T(512)S(1)} %copy-done.7, bf16[3,3,3,384,384]{4,3,2,1,0:T(8,128)(2,1)S(1)} %copy-done), custom_call_target="tpu_custom_call" | custom-call | flops 600000000 | bytes 1000 | tf_op jit(solution)/shard_map/conv_own_frame/pallas_call | solution.py:412
  8.8 1.8 %collective-permute-done.near2 = bf16[1,160,384]{2,1,0:T(8,128)(2,1)S(1)} collective-permute-done((bf16[1,160,384]{2,1,0:T(8,128)(2,1)S(1)}, bf16[1,160,384]{2,1,0:T(8,128)(2,1)S(1)}, u32[]{:S(2)}, u32[]{:S(2)}) %collective-permute-start) | collective-permute-done | bytes 122912 | tf_op jit(solution)/shard_map/ppermute | solution.py:361
  10.6 0.0 collective-permute-done.1.edges
  10.6 0.0 collective-permute-start.5
  10.6 1.5 %collective-permute-start.2 = (bf16[1,160,384]{2,1,0:T(8,128)(2,1)S(1)}, bf16[1,160,384]{2,1,0:T(8,128)(2,1)S(1)}, u32[]{:S(2)}, u32[]{:S(2)}) collective-permute-start(bf16[1,160,384]{2,1,0:T(8,128)(2,1)S(1)} %collective-permute-done.near2), channel_id=1, source_target_pairs={{0,1},{1,0},{2,3},{3,2},{4,5},{5,4},{6,7},{7,6},{8,9},{9,8},{10,11... | collective-permute-start | bytes 368648 | tf_op jit(solution)/shard_map/ppermute | solution.py:367
  12.1 0.2 collective-permute-start.7
  12.3 1.8 %collective-permute-done.3.rest2 = bf16[1,160,384]{2,1,0:T(8,128)(2,1)S(1)} collective-permute-done((bf16[1,160,384]{2,1,0:T(8,128)(2,1)S(1)}, bf16[1,160,384]{2,1,0:T(8,128)(2,1)S(1)}, u32[]{:S(2)}, u32[]{:S(2)}) %collective-permute-start.3) | collective-permute-done | bytes 122912 | tf_op jit(solution)/shard_map/ppermute | solution.py:361
  14.2 0.0 collective-permute-start.8
  14.2 0.0 collective-permute-done.5.odd_edges
  14.2 0.0 collective-permute-done.4.odd
  14.2 1.9 %conv_two_back.1.before = f32[2,160,384]{2,1,0:T(8,128)S(1)} custom-call(s32[5]{0:T(128)S(1)} %stack.35.place, bf16[1,160,384]{2,1,0:T(8,128)(2,1)S(1)} %collective-permute-done.near2, bf16[1,160,384]{2,1,0:T(8,128)(2,1)S(1)} %collective-permute-done.3.rest2, bf16[2,160,384]{2,1,0:T(8,128)(2,1)S(1)} %collective-permute-done.4.odd, ...), custom_call_target="tpu_custom_call" | custom-call | flops 600000000 | bytes 1000 | tf_op jit(solution)/shard_map/conv_two_back/pallas_call | solution.py:412
  16.1 0.2 collective-permute-done.2.edges2
  16.3 0.3 collective-permute-start.6
  16.7 0.0 collective-permute-done.7.even_near
  16.7 0.0 collective-permute-done.8.even_rest
  16.7 0.6 %conv_one_back.1.before = f32[2,160,384]{2,1,0:T(8,128)S(1)} custom-call(s32[5]{0:T(128)S(1)} %stack.35.place, bf16[1,160,384]{2,1,0:T(8,128)(2,1)S(1)} %collective-permute-done.7.even_near, bf16[1,160,384]{2,1,0:T(8,128)(2,1)S(1)} %collective-permute-done.8.even_rest, bf16[2,160,384]{2,1,0:T(8,128)(2,1)S(1)} %collective-permute-done.4.odd, ...), custom_call_target="tpu_custom_call" | custom-call | flops 3000000000 | bytes 1000 | tf_op jit(solution)/shard_map/conv_one_back/pallas_call | solution.py:412
  17.3 0.0 copy-start.1
  17.3 0.0 copy-start.2
  17.3 0.0 copy-start.4
  17.3 0.0 copy-start.6
  17.3 0.3 collective-permute-done.6.even_edges
  17.7 0.6 %conv_edge_rows.1 = (bf16[2,160,384]{2,1,0:T(8,128)(2,1)S(1)}, bf16[1,160,384]{2,1,0:T(8,128)(2,1)S(1)}, bf16[1,160,384]{2,1,0:T(8,128)(2,1)S(1)}) custom-call(s32[5]{0:T(128)S(1)} %stack.35.place, bf16[1,160,384]{2,1,0:T(8,128)(2,1)S(1)} %collective-permute-done.1.edges, bf16[1,160,384]{2,1,0:T(8,128)(2,1)S(1)} %collective-permute-done.2.edges2, ...), custom_call_target="tpu_custom_call" | custom-call | flops 3000000000 | bytes 1000 | tf_op jit(solution)/shard_map/conv_edge_rows/pallas_call | solution.py:441
  18.3 0.4 %collective-permute-start.11 = (bf16[2,160,384]{2,1,0:T(8,128)(2,1)S(1)}, bf16[2,160,384]{2,1,0:T(8,128)(2,1)S(1)}, u32[]{:S(2)}, u32[]{:S(2)}) collective-permute-start(bf16[2,160,384]{2,1,0:T(8,128)(2,1)S(1)} %get-tuple-element.37.own), channel_id=1, source_target_pairs={{0,2},{2,0},{4,6},{6,4},{8,10},{10,8},{12,14},{14,12},{16,18},{18,... | collective-permute-start | bytes 737288 | tf_op jit(solution)/shard_map/ppermute | solution.py:356
  18.7 1.3 %collective-permute-start.10 = (bf16[1,160,384]{2,1,0:T(8,128)(2,1)S(1)}, bf16[1,160,384]{2,1,0:T(8,128)(2,1)S(1)}, u32[]{:S(2)}, u32[]{:S(2)}) collective-permute-start(bf16[1,160,384]{2,1,0:T(8,128)(2,1)S(1)} %get-tuple-element.38), channel_id=1, source_target_pairs={{0,4},{2,6},{4,8},{6,10},{8,12},{10,14},{12,16},{14,18},{16,20},{1... | collective-permute-start | bytes 368648 | tf_op jit(solution)/shard_map/ppermute | solution.py:361
  20.0 1.5 %collective-permute-start.9 = (bf16[1,160,384]{2,1,0:T(8,128)(2,1)S(1)}, bf16[1,160,384]{2,1,0:T(8,128)(2,1)S(1)}, u32[]{:S(2)}, u32[]{:S(2)}) collective-permute-start(bf16[1,160,384]{2,1,0:T(8,128)(2,1)S(1)} %get-tuple-element.38), channel_id=1, source_target_pairs={{0,1},{1,0},{2,3},{3,2},{4,5},{5,4},{6,7},{7,6},{8,9},{9,8},{10,11... | collective-permute-start | bytes 368648 | tf_op jit(solution)/shard_map/ppermute | solution.py:367
  21.5 1.5 %collective-permute-start.12 = (bf16[1,160,384]{2,1,0:T(8,128)(2,1)S(1)}, bf16[1,160,384]{2,1,0:T(8,128)(2,1)S(1)}, u32[]{:S(2)}, u32[]{:S(2)}) collective-permute-start(bf16[1,160,384]{2,1,0:T(8,128)(2,1)S(1)} %get-tuple-element.43), channel_id=1, source_target_pairs={{0,4},{2,6},{4,8},{6,10},{8,12},{10,14},{12,16},{14,18},{16,20},{1... | collective-permute-start | bytes 368648 | tf_op jit(solution)/shard_map/ppermute | solution.py:361
  23.0 0.0 collective-permute-done.11.odd
  23.0 0.0 copy-done.1
  23.0 0.0 copy-done.2
  23.1 0.0 copy-done.4
  23.1 0.0 copy-done.6
  23.1 4.0 %merge_taps_and_first_chip_rows.1 = (bf16[2,768,768]{2,1,0:T(8,128)(2,1)S(1)}, bf16[2,4,192,320]{3,2,1,0:T(8,128)(2,1)}, bf16[2,2,160,384]{3,2,1,0:T(8,128)(2,1)S(1)}) custom-call(s32[5]{0:T(128)S(1)} %stack.35.place, bf16[3,3,192,384]{3,2,1,0:T(8,128)(2,1)S(1)} %bitcast.12, bf16[2,160,384]{2,1,0:T(8,128)(2,1)S(1)} %get-tuple-element.37.own, ...), custom_call_target="tpu_custom_call" | custom-call | flops 600000000 | bytes 1000 | tf_op jit(solution)/shard_map/merge_taps_and_first_chip_rows/pallas_call | solution.py:465
  27.0 0.1 collective-permute-done.10.near2
  27.2 1.7 %collective-permute-start.15 = (bf16[1,160,384]{2,1,0:T(8,128)(2,1)S(1)}, bf16[1,160,384]{2,1,0:T(8,128)(2,1)S(1)}, u32[]{:S(2)}, u32[]{:S(2)}) collective-permute-start(bf16[1,160,384]{2,1,0:T(8,128)(2,1)S(1)} %collective-permute-done.10.near2), channel_id=1, source_target_pairs={{0,1},{1,0},{2,3},{3,2},{4,5},{5,4},{6,7},{7,6},{8,9},{9,8},{10,11... | collective-permute-start | bytes 368648 | tf_op jit(solution)/shard_map/ppermute | solution.py:367
  28.9 0.0 collective-permute-done.9.edges
  28.9 0.0 collective-permute-start.17
  28.9 0.5 %collective-permute-done.12.rest2 = bf16[1,160,384]{2,1,0:T(8,128)(2,1)S(1)} collective-permute-done((bf16[1,160,384]{2,1,0:T(8,128)(2,1)S(1)}, bf16[1,160,384]{2,1,0:T(8,128)(2,1)S(1)}, u32[]{:S(2)}, u32[]{:S(2)}) %collective-permute-start.12) | collective-permute-done | bytes 122912 | tf_op jit(solution)/shard_map/ppermute | solution.py:361
  29.4 0.0 collective-permute-start.13
  29.4 0.5 %collective-permute-start.14 = (bf16[1,160,384]{2,1,0:T(8,128)(2,1)S(1)}, bf16[1,160,384]{2,1,0:T(8,128)(2,1)S(1)}, u32[]{:S(2)}, u32[]{:S(2)}) collective-permute-start(bf16[1,160,384]{2,1,0:T(8,128)(2,1)S(1)} %collective-permute-done.12.rest2), channel_id=1, source_target_pairs={{0,2},{2,0},{4,6},{6,4},{8,10},{10,8},{12,14},{14,12},{16,18},{18,... | collective-permute-start | bytes 368648 | tf_op jit(solution)/shard_map/ppermute | solution.py:356
  29.9 2.1 %collective-permute-done.15.edges2 = bf16[1,160,384]{2,1,0:T(8,128)(2,1)S(1)} collective-permute-done((bf16[1,160,384]{2,1,0:T(8,128)(2,1)S(1)}, bf16[1,160,384]{2,1,0:T(8,128)(2,1)S(1)}, u32[]{:S(2)}, u32[]{:S(2)}) %collective-permute-start.15) | collective-permute-done | bytes 122912 | tf_op jit(solution)/shard_map/ppermute | solution.py:367
  32.0 0.0 collective-permute-start.16
  32.0 0.0 collective-permute-done.17.odd_edges
  32.0 2.8 %first_chip_edge_rows.1 = (bf16[2,4,192,320]{3,2,1,0:T(8,128)(2,1)}, f32[8,128]{1,0:T(8,128)S(1)}) custom-call(s32[5]{0:T(128)S(1)} %stack.35.place, bf16[1,160,384]{2,1,0:T(8,128)(2,1)S(1)} %collective-permute-done.9.edges, bf16[1,160,384]{2,1,0:T(8,128)(2,1)S(1)} %collective-permute-done.17.odd_edges, ...), custom_call_target="tpu_custom_call", output_to_operand_aliasing={{0}: (8, {})} | custom-call | flops 30000000 | bytes 1000 | tf_op jit(solution)/shard_map/first_chip_edge_rows/pallas_call | solution.py:483
  34.9 0.0 collective-permute-done.13.even_near
  34.9 0.0 collective-permute-done.14.even_rest
  34.9 0.0 collective-permute-done.16.even_edges
  34.9 0.8 %time_and_up.1 = bf16[2,4,192,320]{3,2,1,0:T(8,128)(2,1)} custom-call(s32[5]{0:T(128)S(1)} %stack.35.place, bf16[2,160,384]{2,1,0:T(8,128)(2,1)S(1)} %get-tuple-element.37.own, bf16[1,160,384]{2,1,0:T(8,128)(2,1)S(1)} %collective-permute-done.10.near2, bf16[1,160,384]{2,1,0:T(8,128)(2,1)S(1)} %collective-permute-done.12.rest2, ...), custom_call_target="tpu_custom_call", output_to_operand_aliasing={{}: (16, {})} | custom-call | flops 3000000000 | bytes 1000 | tf_op jit(solution)/shard_map/time_and_up/pallas_call | solution.py:491
Async XLA Ops:
  0.1 5.7 %copy-start.3 = (bf16[1,2,160,384]{3,2,1,0:T(8,128)(2,1)S(1)}, bf16[1,2,160,384]{3,2,1,0:T(8,128)(2,1)}, u32[]{:S(2)}) copy-start(bf16[1,2,160,384]{3,2,1,0:T(8,128)(2,1)} %param.8) | copy-start | bytes 737284
  0.1 7.2 %copy-start = (bf16[3,3,3,384,384]{4,3,2,1,0:T(8,128)(2,1)S(1)}, bf16[3,3,3,384,384]{4,3,2,1,0:T(8,128)(2,1)}, u32[]{:S(2)}) copy-start(bf16[3,3,3,384,384]{4,3,2,1,0:T(8,128)(2,1)} %weight.7) | copy-start | bytes 23887876
  0.1 7.2 %copy-start.5 = (f32[384]{0:T(512)S(1)}, f32[384]{0:T(512)}, u32[]{:S(2)}) copy-start(f32[384]{0:T(512)} %gain.7) | copy-start | bytes 4612
  0.1 7.2 %copy-start.7 = (f32[384]{0:T(512)S(1)}, f32[384]{0:T(512)}, u32[]{:S(2)}) copy-start(f32[384]{0:T(512)} %bias.1) | copy-start | bytes 4612
  1.2 9.4 %collective-permute-start = (bf16[1,160,384]{2,1,0:T(8,128)(2,1)S(1)}, bf16[1,160,384]{2,1,0:T(8,128)(2,1)S(1)}, u32[]{:S(2)}, u32[]{:S(2)}) collective-permute-start(bf16[1,160,384]{2,1,0:T(8,128)(2,1)S(1)} %get-tuple-element.29), channel_id=1, source_target_pairs={{0,4},{2,6},{4,8},{6,10},{8,12},{10,14},{12,16},{14,18},{16,20},{1... | collective-permute-start | bytes 368648 | tf_op jit(solution)/shard_map/ppermute | solution.py:361
  4.2 6.4 %collective-permute-start.1 = (bf16[1,160,384]{2,1,0:T(8,128)(2,1)S(1)}, bf16[1,160,384]{2,1,0:T(8,128)(2,1)S(1)}, u32[]{:S(2)}, u32[]{:S(2)}) collective-permute-start(bf16[1,160,384]{2,1,0:T(8,128)(2,1)S(1)} %get-tuple-element.29), channel_id=1, source_target_pairs={{0,1},{1,0},{2,3},{3,2},{4,5},{5,4},{6,7},{7,6},{8,9},{9,8},{10,11... | collective-permute-start | bytes 368648 | tf_op jit(solution)/shard_map/ppermute | solution.py:367
  5.8 8.4 %collective-permute-start.4 = (bf16[2,160,384]{2,1,0:T(8,128)(2,1)S(1)}, bf16[2,160,384]{2,1,0:T(8,128)(2,1)S(1)}, u32[]{:S(2)}, u32[]{:S(2)}) collective-permute-start(bf16[2,160,384]{2,1,0:T(8,128)(2,1)S(1)} %bitcast.14), channel_id=1, source_target_pairs={{0,2},{2,0},{4,6},{6,4},{8,10},{10,8},{12,14},{14,12},{16,18},{18,... | collective-permute-start | bytes 737288 | tf_op jit(solution)/shard_map/ppermute | solution.py:356
  5.8 8.4 %collective-permute-start.3 = (bf16[1,160,384]{2,1,0:T(8,128)(2,1)S(1)}, bf16[1,160,384]{2,1,0:T(8,128)(2,1)S(1)}, u32[]{:S(2)}, u32[]{:S(2)}) collective-permute-start(bf16[1,160,384]{2,1,0:T(8,128)(2,1)S(1)} %get-tuple-element.32), channel_id=1, source_target_pairs={{0,4},{2,6},{4,8},{6,10},{8,12},{10,14},{12,16},{14,18},{16,20},{1... | collective-permute-start | bytes 368648 | tf_op jit(solution)/shard_map/ppermute | solution.py:361
  10.6 3.6 %collective-permute-start.5 = (bf16[1,160,384]{2,1,0:T(8,128)(2,1)S(1)}, bf16[1,160,384]{2,1,0:T(8,128)(2,1)S(1)}, u32[]{:S(2)}, u32[]{:S(2)}) collective-permute-start(bf16[1,160,384]{2,1,0:T(8,128)(2,1)S(1)} %collective-permute-done.1.edges), channel_id=1, source_target_pairs={{0,2},{2,0},{4,6},{6,4},{8,10},{10,8},{12,14},{14,12},{16,18},{18,... | collective-permute-start | bytes 368648 | tf_op jit(solution)/shard_map/ppermute | solution.py:356
  10.6 5.7 %collective-permute-start.2 = (bf16[1,160,384]{2,1,0:T(8,128)(2,1)S(1)}, bf16[1,160,384]{2,1,0:T(8,128)(2,1)S(1)}, u32[]{:S(2)}, u32[]{:S(2)}) collective-permute-start(bf16[1,160,384]{2,1,0:T(8,128)(2,1)S(1)} %collective-permute-done.near2), channel_id=1, source_target_pairs={{0,1},{1,0},{2,3},{3,2},{4,5},{5,4},{6,7},{7,6},{8,9},{9,8},{10,11... | collective-permute-start | bytes 368648 | tf_op jit(solution)/shard_map/ppermute | solution.py:367
  12.1 4.6 %collective-permute-start.7 = (bf16[1,160,384]{2,1,0:T(8,128)(2,1)S(1)}, bf16[1,160,384]{2,1,0:T(8,128)(2,1)S(1)}, u32[]{:S(2)}, u32[]{:S(2)}) collective-permute-start(bf16[1,160,384]{2,1,0:T(8,128)(2,1)S(1)} %collective-permute-done.near2), channel_id=1, source_target_pairs={{0,2},{2,0},{4,6},{6,4},{8,10},{10,8},{12,14},{14,12},{16,18},{18,... | collective-permute-start | bytes 368648 | tf_op jit(solution)/shard_map/ppermute | solution.py:356
  14.2 2.5 %collective-permute-start.8 = (bf16[1,160,384]{2,1,0:T(8,128)(2,1)S(1)}, bf16[1,160,384]{2,1,0:T(8,128)(2,1)S(1)}, u32[]{:S(2)}, u32[]{:S(2)}) collective-permute-start(bf16[1,160,384]{2,1,0:T(8,128)(2,1)S(1)} %collective-permute-done.3.rest2), channel_id=1, source_target_pairs={{0,2},{2,0},{4,6},{6,4},{8,10},{10,8},{12,14},{14,12},{16,18},{18,... | collective-permute-start | bytes 368648 | tf_op jit(solution)/shard_map/ppermute | solution.py:356
  16.3 1.3 %collective-permute-start.6 = (bf16[1,160,384]{2,1,0:T(8,128)(2,1)S(1)}, bf16[1,160,384]{2,1,0:T(8,128)(2,1)S(1)}, u32[]{:S(2)}, u32[]{:S(2)}) collective-permute-start(bf16[1,160,384]{2,1,0:T(8,128)(2,1)S(1)} %collective-permute-done.2.edges2), channel_id=1, source_target_pairs={{0,2},{2,0},{4,6},{6,4},{8,10},{10,8},{12,14},{14,12},{16,18},{18,... | collective-permute-start | bytes 368648 | tf_op jit(solution)/shard_map/ppermute | solution.py:356
  17.3 5.8 %copy-start.1 = (bf16[3,384,768]{2,1,0:T(8,128)(2,1)S(1)}, bf16[3,384,768]{2,1,0:T(8,128)(2,1)}, u32[]{:S(2)}) copy-start(bf16[3,384,768]{2,1,0:T(8,128)(2,1)} %param.12) | copy-start | bytes 5308420
  17.3 5.8 %copy-start.2 = (bf16[3,3,384,192]{2,3,1,0:T(8,128)(2,1)S(1)}, bf16[3,3,384,192]{2,3,1,0:T(8,128)(2,1)}, u32[]{:S(2)}) copy-start(bf16[3,3,384,192]{2,3,1,0:T(8,128)(2,1)} %param.14) | copy-start | bytes 3981316
  17.3 5.8 %copy-start.4 = (f32[768]{0:T(1024)S(1)}, f32[768]{0:T(1024)}, u32[]{:S(2)}) copy-start(f32[768]{0:T(1024)} %tbias.5) | copy-start | bytes 9220
  17.3 5.8 %copy-start.6 = (f32[192]{0:T(256)S(1)}, f32[192]{0:T(256)}, u32[]{:S(2)}) copy-start(f32[192]{0:T(256)} %ubias.5) | copy-start | bytes 2308
  18.3 4.8 %collective-permute-start.11 = (bf16[2,160,384]{2,1,0:T(8,128)(2,1)S(1)}, bf16[2,160,384]{2,1,0:T(8,128)(2,1)S(1)}, u32[]{:S(2)}, u32[]{:S(2)}) collective-permute-start(bf16[2,160,384]{2,1,0:T(8,128)(2,1)S(1)} %get-tuple-element.37.own), channel_id=1, source_target_pairs={{0,2},{2,0},{4,6},{6,4},{8,10},{10,8},{12,14},{14,12},{16,18},{18,... | collective-permute-start | bytes 737288 | tf_op jit(solution)/shard_map/ppermute | solution.py:356
  18.7 8.5 %collective-permute-start.10 = (bf16[1,160,384]{2,1,0:T(8,128)(2,1)S(1)}, bf16[1,160,384]{2,1,0:T(8,128)(2,1)S(1)}, u32[]{:S(2)}, u32[]{:S(2)}) collective-permute-start(bf16[1,160,384]{2,1,0:T(8,128)(2,1)S(1)} %get-tuple-element.38), channel_id=1, source_target_pairs={{0,4},{2,6},{4,8},{6,10},{8,12},{10,14},{12,16},{14,18},{16,20},{1... | collective-permute-start | bytes 368648 | tf_op jit(solution)/shard_map/ppermute | solution.py:361
  20.0 8.8 %collective-permute-start.9 = (bf16[1,160,384]{2,1,0:T(8,128)(2,1)S(1)}, bf16[1,160,384]{2,1,0:T(8,128)(2,1)S(1)}, u32[]{:S(2)}, u32[]{:S(2)}) collective-permute-start(bf16[1,160,384]{2,1,0:T(8,128)(2,1)S(1)} %get-tuple-element.38), channel_id=1, source_target_pairs={{0,1},{1,0},{2,3},{3,2},{4,5},{5,4},{6,7},{7,6},{8,9},{9,8},{10,11... | collective-permute-start | bytes 368648 | tf_op jit(solution)/shard_map/ppermute | solution.py:367
  21.5 7.9 %collective-permute-start.12 = (bf16[1,160,384]{2,1,0:T(8,128)(2,1)S(1)}, bf16[1,160,384]{2,1,0:T(8,128)(2,1)S(1)}, u32[]{:S(2)}, u32[]{:S(2)}) collective-permute-start(bf16[1,160,384]{2,1,0:T(8,128)(2,1)S(1)} %get-tuple-element.43), channel_id=1, source_target_pairs={{0,4},{2,6},{4,8},{6,10},{8,12},{10,14},{12,16},{14,18},{16,20},{1... | collective-permute-start | bytes 368648 | tf_op jit(solution)/shard_map/ppermute | solution.py:361
  27.2 4.9 %collective-permute-start.15 = (bf16[1,160,384]{2,1,0:T(8,128)(2,1)S(1)}, bf16[1,160,384]{2,1,0:T(8,128)(2,1)S(1)}, u32[]{:S(2)}, u32[]{:S(2)}) collective-permute-start(bf16[1,160,384]{2,1,0:T(8,128)(2,1)S(1)} %collective-permute-done.10.near2), channel_id=1, source_target_pairs={{0,1},{1,0},{2,3},{3,2},{4,5},{5,4},{6,7},{7,6},{8,9},{9,8},{10,11... | collective-permute-start | bytes 368648 | tf_op jit(solution)/shard_map/ppermute | solution.py:367
  28.9 3.2 %collective-permute-start.17 = (bf16[1,160,384]{2,1,0:T(8,128)(2,1)S(1)}, bf16[1,160,384]{2,1,0:T(8,128)(2,1)S(1)}, u32[]{:S(2)}, u32[]{:S(2)}) collective-permute-start(bf16[1,160,384]{2,1,0:T(8,128)(2,1)S(1)} %collective-permute-done.9.edges), channel_id=1, source_target_pairs={{0,2},{2,0},{4,6},{6,4},{8,10},{10,8},{12,14},{14,12},{16,18},{18,... | collective-permute-start | bytes 368648 | tf_op jit(solution)/shard_map/ppermute | solution.py:356
  29.4 5.5 %collective-permute-start.13 = (bf16[1,160,384]{2,1,0:T(8,128)(2,1)S(1)}, bf16[1,160,384]{2,1,0:T(8,128)(2,1)S(1)}, u32[]{:S(2)}, u32[]{:S(2)}) collective-permute-start(bf16[1,160,384]{2,1,0:T(8,128)(2,1)S(1)} %collective-permute-done.10.near2), channel_id=1, source_target_pairs={{0,2},{2,0},{4,6},{6,4},{8,10},{10,8},{12,14},{14,12},{16,18},{18,... | collective-permute-start | bytes 368648 | tf_op jit(solution)/shard_map/ppermute | solution.py:356
  29.4 5.5 %collective-permute-start.14 = (bf16[1,160,384]{2,1,0:T(8,128)(2,1)S(1)}, bf16[1,160,384]{2,1,0:T(8,128)(2,1)S(1)}, u32[]{:S(2)}, u32[]{:S(2)}) collective-permute-start(bf16[1,160,384]{2,1,0:T(8,128)(2,1)S(1)} %collective-permute-done.12.rest2), channel_id=1, source_target_pairs={{0,2},{2,0},{4,6},{6,4},{8,10},{10,8},{12,14},{14,12},{16,18},{18,... | collective-permute-start | bytes 368648 | tf_op jit(solution)/shard_map/ppermute | solution.py:356
  32.0 2.8 %collective-permute-start.16 = (bf16[1,160,384]{2,1,0:T(8,128)(2,1)S(1)}, bf16[1,160,384]{2,1,0:T(8,128)(2,1)S(1)}, u32[]{:S(2)}, u32[]{:S(2)}) collective-permute-start(bf16[1,160,384]{2,1,0:T(8,128)(2,1)S(1)} %collective-permute-done.15.edges2), channel_id=1, source_target_pairs={{0,2},{2,0},{4,6},{6,4},{8,10},{10,8},{12,14},{14,12},{16,18},{18,... | collective-permute-start | bytes 368648 | tf_op jit(solution)/shard_map/ppermute | solution.py:356
